TPU v7x, 256 devices: a whole 4x4x8 slice. The times are simulated.
256 devices in a mesh: dp: 4 (over y_hi, core), tm: 64 (over y_lo, x, z).
Axes of the slice: x: 4, y: 4 (y_hi: 2, y_lo: 2; y = y_hi * 2 + y_lo), z: 8, core: 2. Of those that a mesh axis runs over, the one named last changes fastest.
Arguments:
- frames: bfloat16 [4, 16384, 256], P('dp', 'tm'), may hold values from -6 to 6
- frames_grad: bfloat16 [4, 16384, 256], P('dp', 'tm'), may hold values from -6 to 6
- w_query: bfloat16 [2, 256, 256], replicated, may hold values from -32 to 32, as said below
- w_key: bfloat16 [2, 256, 256], replicated, may hold values from -0.375 to 0.375
- w_value: bfloat16 [2, 256, 256], replicated, may hold values from -0.375 to 0.375
- w_out: bfloat16 [2, 256, 256], replicated, may hold values from -0.375 to 0.375
- norm_gains: float32 [2, 256], replicated, may hold values from 0.1 to 1.9
Outputs:
- grad_frames: bfloat16 [4, 16384, 256], P('dp', 'tm')
- grad_query: float32 [2, 256, 256], replicated
- grad_key: float32 [2, 256, 256], replicated
- grad_value: float32 [2, 256, 256], replicated
- grad_out: float32 [2, 256, 256], replicated
- grad_gains: float32 [2, 256], replicated
Inputs may be any that keep to these rules, and one draw needn't show every extreme that they name: `w_query`: query projections of the two layers, full rank.
All inputs are finite; a program needn't handle non-finite values.
Results may differ from a plain program's by a relative error of at most 0.03.
The roundings to bfloat16 on the way count: a program that leaves them out, or rounds other values in their place, can miss the bound.
Values may be sent and summed in bfloat16 or wider, within the bound.
No kernel may reach another device: no remote copies, remote signals or barrier semaphores. Data moves between devices by JAX's collectives and lax.ppermute only.
A program may use at most 64 MiB of HBM per device.

v0:
```python
import jax
import jax.numpy as jnp
from jax import lax
from jax.sharding import PartitionSpec as P

HEADS = 8
K = 256
HOP = 128


EPSILON = 1e-05


def passed_along(shard, axis, by):
    length = lax.axis_size(axis)
    pairs = [(i, i + by) for i in range(length) if 0 <= i + by < length]
    return lax.ppermute(shard, axis, pairs)


def rounded(value):
    return lax.optimization_barrier(value.astype(jnp.bfloat16))


def normalize(activations, gain):
    average = jnp.mean(activations, axis=-1, keepdims=True)
    centered = activations - average
    variance = jnp.mean(centered * centered, axis=-1, keepdims=True)
    return centered * lax.rsqrt(variance + EPSILON) * gain


def project(left, weight):
    return jnp.dot(left, weight, preferred_element_type=jnp.float32)


def back_project(grad_rows, weight):
    return lax.dot_general(
        grad_rows,
        weight,
        (((grad_rows.ndim - 1,), (1,)), ((), ())),
        preferred_element_type=jnp.float32,
    )


def contract_tokens(left, right):
    left_rows = left.reshape(-1, left.shape[-1])
    right_rows = right.reshape(-1, right.shape[-1])
    return lax.dot_general(
        left_rows, right_rows, (((0,), (0,)), ((), ())), preferred_element_type=jnp.float32
    )


def product(form, left, right):
    return jnp.einsum(form, left, right, preferred_element_type=jnp.float32)


def attention_probs(queries, key_rows):
    scaling = queries.shape[-1] ** (-0.5)
    scores = product("gqmd,gkmd->gmqk", queries, key_rows) * scaling
    highest = jnp.max(scores, axis=-1, keepdims=True)
    exponentials = jnp.exp(scores - highest)
    return exponentials / jnp.sum(exponentials, axis=-1, keepdims=True)


def head_forward(queries, key_rows, value_rows):
    weights_low = rounded(attention_probs(queries, key_rows))
    return (rounded(product("gmqk,gkmd->gqmd", weights_low, value_rows)),)


def head_backward(queries, key_rows, value_rows, grad_context):
    scaling = queries.shape[-1] ** (-0.5)
    probabilities = attention_probs(queries, key_rows)
    weights_low = rounded(probabilities)
    context = rounded(product("gmqk,gkmd->gqmd", weights_low, value_rows))
    grad_probs = product("gqmd,gkmd->gmqk", grad_context, value_rows)
    grad_values = rounded(product("gmqk,gqmd->gkmd", weights_low, grad_context))
    inner = jnp.sum(grad_probs * probabilities, axis=-1, keepdims=True)
    grad_scores = rounded(probabilities * (grad_probs - inner) * scaling)
    grad_queries = rounded(product("gmqk,gkmd->gqmd", grad_scores, key_rows))
    grad_keys = rounded(product("gmqk,gqmd->gkmd", grad_scores, queries))
    return (context, grad_queries, grad_keys, grad_values)


def over_heads(function, operands):
    head_width = operands[0].shape[-1] // HEADS

    def single_head(head_index):
        offset = head_index * head_width
        return function(
            *[lax.dynamic_slice_in_dim(operand, offset, head_width, axis=3) for operand in operands]
        )

    stacked = lax.map(single_head, jnp.arange(HEADS))
    return tuple(
        (jnp.moveaxis(result_part, 0, 3).reshape(operands[0].shape) for result_part in stacked)
    )


def layer_front(inputs, gain, weight_query, weight_key, weight_value):
    normed = rounded(normalize(inputs.astype(jnp.float32), gain))
    return (
        normed,
        rounded(project(normed, weight_query)),
        rounded(project(normed, weight_key)),
        rounded(project(normed, weight_value)),
    )


def layer_output(inputs, context, weight_out):
    return rounded(inputs.astype(jnp.float32) + project(context, weight_out))


def layer_back(inputs, front, grad_rows, gain, weight_query, weight_key, weight_value, weight_out):
    normed, queries, key_rows, value_rows = front
    grad_context = rounded(back_project(grad_rows, weight_out))
    context, grad_queries, grad_keys, grad_values = over_heads(
        head_backward, (queries, key_rows, value_rows, grad_context)
    )
    grad_normed = (
        back_project(grad_queries, weight_query)
        + back_project(grad_keys, weight_key)
        + back_project(grad_values, weight_value)
    )
    unused_value, pullback = jax.vjp(normalize, inputs.astype(jnp.float32), gain)
    grad_inputs, grad_gain = pullback(grad_normed)
    parts = (
        contract_tokens(normed, grad_queries),
        contract_tokens(normed, grad_keys),
        contract_tokens(normed, grad_values),
        contract_tokens(context, grad_rows),
        grad_gain,
    )
    return (grad_rows.astype(jnp.float32) + grad_inputs, parts)


def shards(frames, frames_grad, w_query, w_key, w_value, w_out, norm_gains):
    mixtures, frame_count, width = frames.shape
    group_count = frame_count // HOP
    blocks = frames.reshape(mixtures, group_count, HOP, width)
    grad_blocks = frames_grad.reshape(mixtures, group_count, HOP, width)
    leading = jnp.concatenate([blocks[:, :1], grad_blocks[:, :1]], axis=1)
    arrived = passed_along(leading, "tm", -1)
    next_input = arrived[:, :1]
    next_grad = arrived[:, 1:]
    grouped = jnp.concatenate(
        [blocks, jnp.concatenate([blocks[:, 1:], next_input], axis=1)], axis=2
    )
    local_groups = grouped.reshape(mixtures * group_count, K, 1, width)
    front_intra = layer_front(local_groups, norm_gains[0], w_query[0], w_key[0], w_value[0])
    (context_intra,) = over_heads(head_forward, front_intra[1:])
    middle = layer_output(local_groups, context_intra, w_out[0]).reshape(
        mixtures, group_count, 2, HOP, width
    )
    grad_groups = jnp.concatenate(
        [grad_blocks, jnp.concatenate([grad_blocks[:, 1:], next_grad], axis=1)], axis=2
    )
    grad_groups = grad_groups.reshape(mixtures, group_count, 2, HOP, width)
    across, grad_across = (
        lax.all_to_all(middle, "tm", split_axis=3, concat_axis=1, tiled=True),
        lax.all_to_all(grad_groups, "tm", split_axis=3, concat_axis=1, tiled=True),
    )
    all_groups = across.shape[1]
    position_part = across.shape[3]
    across = across.reshape(mixtures, all_groups, 2 * position_part, width)
    grad_across = grad_across.reshape(mixtures, all_groups, 2 * position_part, width)
    front_inter = layer_front(across, norm_gains[1], w_query[1], w_key[1], w_value[1])
    grad_middle, parts_inter = layer_back(
        across, front_inter, grad_across, norm_gains[1], w_query[1], w_key[1], w_value[1], w_out[1]
    )
    grad_middle = rounded(grad_middle).reshape(mixtures, all_groups, 2, position_part, width)
    grad_local = lax.all_to_all(grad_middle, "tm", split_axis=1, concat_axis=3, tiled=True).reshape(
        mixtures * group_count, K, 1, width
    )
    grad_grouped, parts_intra = layer_back(
        local_groups,
        front_intra,
        grad_local,
        norm_gains[0],
        w_query[0],
        w_key[0],
        w_value[0],
        w_out[0],
    )
    halves = rounded(grad_grouped).reshape(mixtures, group_count, 2, HOP, width)
    carried = passed_along(halves[:, -1:, 1], "tm", 1)
    earlier = jnp.concatenate([carried, halves[:, :-1, 1]], axis=1)
    grad_input = rounded(halves[:, :, 0].astype(jnp.float32) + earlier.astype(jnp.float32)).reshape(
        mixtures, frame_count, width
    )
    stacked = tuple(
        (
            jnp.stack([intra_part, inter_part])
            for intra_part, inter_part in zip(parts_intra, parts_inter)
        )
    )
    totals = lax.psum((stacked[0], stacked[1], stacked[2], stacked[3], stacked[4]), ("dp", "tm"))
    return (grad_input, totals[0], totals[1], totals[2], totals[3], totals[4])


def solution(mesh):
    placed = (P("dp", "tm", None), P("dp", "tm", None), P(), P(), P(), P(), P())
    return jax.shard_map(
        shards,
        mesh=mesh,
        in_specs=placed,
        out_specs=(P("dp", "tm", None), P(), P(), P(), P(), P()),
        check_vma=False,
    )
```

profile of v0, /device:TPU:1, one launch (start us, length us, event | category | flops | bytes accessed | tf_op | source)
XLA Modules:
  0.0 507.9 jit_solution(2801803110200728133)
XLA Ops:
  8.2 1.3 collective-permute-start
  9.5 5.4 %collective-permute-done = bf16[1,2,128,256]{3,2,1,0:T(8,128)(2,1)S(1)} collective-permute-done((bf16[1,2,128,256]{3,2,1,0:T(8,128)(2,1)S(1)}, bf16[1,2,128,256]{3,2,1,0:T(8,128)(2,1)S(1)}, u32[]{:S(2)}, u32[]{:S(2)}) %collective-permute-start) | collective-permute-done | bytes 131104 | tf_op jit(solution)/shard_map/ppermute | solution.py:17
  19.8 21.1 %while.42 = (s32[]{:T(128)}, bf16[8,2,256,1,32]{2,4,0,1,3:T(8,128)(2,1)S(1)}, s32[8]{0:T(128)S(1)}, bf16[2,256,1,256]{1,3,0,2:T(8,128)(2,1)S(1)}, bf16[2,256,1,2...) while((s32[]{:T(128)}, ...), condition=%wide.region_5.6_spmd, body=%wide.region_2.5_spmd.sunk | while | flops 17319428 | bytes 722095 | solution.py:92
  21.0 1.2 fusion.377
  23.7 1.2 fusion.377
  26.3 1.2 fusion.377
  28.9 1.2 fusion.377
  31.6 1.2 fusion.377
  34.2 1.2 fusion.377
  36.9 1.2 fusion.377
  39.5 1.2 fusion.377
  42.1 14.8 %all-to-all-start.1 = ((bf16[1,2,2,128,256]{4,2,1,0,3:T(2,128)(2,1)}), bf16[1,2,2,128,256]{4,2,1,0,3:T(2,128)(2,1)S(1)}, u32[]{:S(2)}, u32[]{:S(2)}) async-start(bf16[1,2,2,128,256]{4,2,1,0,3:T(2,128)(2,1)} %copy.171), calls=%async_computation.1 | async-start | bytes 524288 | tf_op jit(solution)/shard_map/all_to_all | solution.py:158
  58.0 9.9 %all-to-all-done.1 = bf16[1,2,2,128,256]{4,2,1,0,3:T(2,128)(2,1)S(1)} async-done(((bf16[1,2,2,128,256]{4,2,1,0,3:T(2,128)(2,1)}), bf16[1,2,2,128,256]{4,2,1,0,3:T(2,128)(2,1)S(1)}, u32[]{:S(2)}, u32[]{:S(2)}) %all-to-all-start.1) | async-done | bytes 262176 | tf_op jit(solution)/shard_map/all_to_all | solution.py:158
  67.9 5.5 %all-to-all-start = ((bf16[1,2,2,128,256]{4,2,1,0,3:T(2,128)(2,1)}), bf16[1,2,2,128,256]{4,2,1,0,3:T(2,128)(2,1)S(1)}, u32[]{:S(2)}, u32[]{:S(2)}) async-start(bf16[1,2,2,128,256]{4,2,1,0,3:T(2,128)(2,1)} %copy.163), calls=%async_computation | async-start | bytes 524288 | tf_op jit(solution)/shard_map/all_to_all | solution.py:159
  78.8 5.7 %all-to-all-done = bf16[1,2,2,128,256]{4,2,1,0,3:T(2,128)(2,1)S(1)} async-done(((bf16[1,2,2,128,256]{4,2,1,0,3:T(2,128)(2,1)}), bf16[1,2,2,128,256]{4,2,1,0,3:T(2,128)(2,1)S(1)}, u32[]{:S(2)}, u32[]{:S(2)}) %all-to-all-start) | async-done | bytes 262176 | tf_op jit(solution)/shard_map/all_to_all | solution.py:159
  89.9 53.9 %while.43 = (s32[]{:T(128)}, bf16[8,1,128,4,32]{2,4,3,1,0:T(8,128)(2,1)}, bf16[8,1,128,4,32]{2,4,0,3,1:T(8,128)(2,1)}, bf16[8,1,128,4,32]{2,4,0,3,1:T(8,128)(2,1...) while((s32[]{:T(128)}, ...), condition=%wide.region_12.13_spmd, body=%wide.region_8.12_spmd.sunk | while | flops 30017412 | bytes 2559203 | solution.py:92
  91.2 1.1 fusion.395
  97.9 1.1 fusion.395
  104.7 1.1 fusion.395
  111.4 1.1 fusion.395
  118.2 1.1 fusion.395
  124.9 1.1 fusion.395
  131.6 1.1 fusion.395
  138.3 1.1 fusion.395
  143.8 1.3 fusion.262
  145.1 1.3 convolution_add_fusion.3
  148.6 5.8 %all-to-all-start.2 = ((bf16[1,128,2,2,256]{4,3,2,0,1:T(2,128)(2,1)}), bf16[1,128,2,2,256]{4,3,2,0,1:T(2,128)(2,1)}, u32[]{:S(2)}, u32[]{:S(2)}) async-start(bf16[1,128,2,2,256]{4,3,2,0,1:T(2,128)(2,1)} %copy.189), calls=%async_computation.2 | async-start | bytes 524288 | tf_op jit(solution)/shard_map/all_to_all | solution.py:170
  154.4 1.4 copy.206
  156.6 2.4 copy.208
  159.7 1.4 copy.210
  161.9 2.4 copy.213
  165.0 1.1 reshape_reshape.39
  168.0 1.0 convolution_bitcast_fusion.2
  169.9 1.1 copy.190
  172.6 45.9 %while.44 = (s32[]{:T(128)}, bf16[8,2,256,1,32]{2,4,1,3,0:T(8,128)(2,1)}, bf16[8,2,256,1,32]{2,4,0,1,3:T(8,128)(2,1)S(1)}, bf16[8,2,256,1,32]{2,4,0,1,3:T(8,128)...) while((s32[]{:T(128)}, ...), condition=%wide.region_19.20_spmd, body=%wide.region_15.0_spmd.sunk | while | flops 59967748 | bytes 4394211 | solution.py:92
  174.1 1.2 fusion.417
  179.8 1.2 fusion.417
  185.5 1.2 fusion.417
  191.2 1.2 fusion.417
  196.9 1.2 fusion.417
  202.6 1.2 fusion.417
  208.3 1.2 fusion.417
  214.0 1.2 fusion.417
  222.6 1.2 copy.211
  230.4 2.7 collective-permute-start.1
  233.2 81.6 %psum.39 = f32[2,256]{1,0:T(2,128)} all-reduce(f32[2,256]{1,0:T(2,128)S(1)} %pad_maximum_fusion.5), channel_id=1, replica_groups=mesh['dp'=4,'tm'=64] {'dp','tm'}, use_global_device_ids=true, to_apply=%region_28.29 | all-reduce | flops 512 | bytes 4096 | tf_op jit(solution)/shard_map/psum | solution.py:195
  315.5 180.3 %all-reduce.3.cloned.1.call-done = (f32[2,256,256]{2,1,0:T(8,128)}, f32[2,256,256]{2,1,0:T(8,128)}, f32[2,256,256]{2,1,0:T(8,128)}, f32[2,256,256]{2,1,0:T(8,128)}) async-done(((f32[2,256,256]{2,1,0:T(8,128)}, f32[2,256,256]{2,1,0:T(8,128)}, f32[2,256,256]{2,1,0:T(8,128)}, f32[2,256,256]{2,1,0:T(8,128)}), (f32[2,256,256]{2,1,0:T(8,128)}, f32[2,256,256]{2,1,0:T(8,128)}, f32[2,256,256]{2,1,0:T(8,128)}, ...) | async-done | bytes 2097168 | tf_op jit(solution)/shard_map/psum | solution.py:195
  495.8 1.9 copy.322
  (341 shorter events, 119.0 us)
Async XLA Ops:
  8.1 1.3 copy-start.24
  8.2 6.7 %collective-permute-start = (bf16[1,2,128,256]{3,2,1,0:T(8,128)(2,1)S(1)}, bf16[1,2,128,256]{3,2,1,0:T(8,128)(2,1)S(1)}, u32[]{:S(2)}, u32[]{:S(2)}) collective-permute-start(bf16[1,2,128,256]{3,2,1,0:T(8,128)(2,1)S(1)} %pad_maximum_fusion.4), channel_id=1, source_target_pairs={{1,0},{2,1},{3,2},{4,3},{5,4},{6,5},{7,6},{8,7},{9,8},{10,9},{11,1... | collective-permute-start | bytes 393224 | tf_op jit(solution)/shard_map/ppermute | solution.py:17
  9.5 5.4 %copy-start = (bf16[1,256,256]{2,1,0:T(8,128)(2,1)S(1)}, bf16[1,256,256]{2,1,0:T(8,128)(2,1)}, u32[]{:S(2)}) copy-start(bf16[1,256,256]{2,1,0:T(8,128)(2,1)} %param.13) | copy-start | bytes 393220
  15.3 1.0 copy-start.2
  16.5 1.0 copy-start.1
  17.7 1.0 copy-start.13
  19.8 21.1 %copy-start.21 = (bf16[2,256,256]{2,1,0:T(8,128)(2,1)S(1)}, bf16[2,256,256]{2,1,0:T(8,128)(2,1)}, u32[]{:S(2)}) copy-start(bf16[2,256,256]{2,1,0:T(8,128)(2,1)} %param.18) | copy-start | bytes 786436
  42.1 14.8 %copy-start.20 = (bf16[1,256,256]{2,1,0:T(8,128)(2,1)S(1)}, bf16[1,256,256]{2,1,0:T(8,128)(2,1)}, u32[]{:S(2)}) copy-start(bf16[1,256,256]{2,1,0:T(8,128)(2,1)} %param.14) | copy-start | bytes 393220
  42.1 25.8 %all-to-all-start.1 = ((bf16[1,2,2,128,256]{4,2,1,0,3:T(2,128)(2,1)}), bf16[1,2,2,128,256]{4,2,1,0,3:T(2,128)(2,1)S(1)}, u32[]{:S(2)}, u32[]{:S(2)}) async-start(bf16[1,2,2,128,256]{4,2,1,0,3:T(2,128)(2,1)} %copy.171), calls=%async_computation.1 | async-start | bytes 524288 | tf_op jit(solution)/shard_map/all_to_all | solution.py:158
  67.9 16.5 %all-to-all-start = ((bf16[1,2,2,128,256]{4,2,1,0,3:T(2,128)(2,1)}), bf16[1,2,2,128,256]{4,2,1,0,3:T(2,128)(2,1)S(1)}, u32[]{:S(2)}, u32[]{:S(2)}) async-start(bf16[1,2,2,128,256]{4,2,1,0,3:T(2,128)(2,1)} %copy.163), calls=%async_computation | async-start | bytes 524288 | tf_op jit(solution)/shard_map/all_to_all | solution.py:159
  77.6 0.9 copy-start.14
  85.8 0.9 copy-start.12
  86.7 0.9 copy-start.11
  88.5 0.9 copy-start.22
  143.8 1.3 copy-start.15
  145.1 1.3 copy-start.5
  148.6 5.9 %copy-start.4 = (bf16[8,1,128,4,32]{2,4,0,3,1:T(8,128)(2,1)S(1)}, bf16[8,1,128,4,32]{2,4,0,3,1:T(8,128)(2,1)}, u32[]{:S(2)}) copy-start(bf16[8,1,128,4,32]{2,4,0,3,1:T(8,128)(2,1)} %get-tuple-element.149) | copy-start | bytes 786436
  148.6 21.3 %all-to-all-start.2 = ((bf16[1,128,2,2,256]{4,3,2,0,1:T(2,128)(2,1)}), bf16[1,128,2,2,256]{4,3,2,0,1:T(2,128)(2,1)}, u32[]{:S(2)}, u32[]{:S(2)}) async-start(bf16[1,128,2,2,256]{4,3,2,0,1:T(2,128)(2,1)} %copy.189), calls=%async_computation.2 | async-start | bytes 524288 | tf_op jit(solution)/shard_map/all_to_all | solution.py:170
  154.4 341.4 %all-reduce.3.cloned.1.call-start = ((), (), s32[]{:S(2)}) async-start(), calls=%async_computation.3 | async-start | bytes 4194304 | tf_op jit(solution)/shard_map/psum | solution.py:195
  171.2 1.0 copy-start.23
  218.5 1.0 copy-start.16
  219.4 0.9 copy-start.3
  223.8 1.0 copy-start.10
  224.8 1.0 copy-start.9
  225.8 1.0 copy-start.8
  226.8 1.0 copy-start.6
  227.9 0.9 copy-start.7
  230.4 84.4 %collective-permute-start.1 = (bf16[1,1,128,256]{3,2,1,0:T(8,128)(2,1)S(1)}, bf16[1,1,128,256]{3,2,1,0:T(8,128)(2,1)S(1)}, u32[]{:S(2)}, u32[]{:S(2)}) collective-permute-start(bf16[1,1,128,256]{3,2,1,0:T(8,128)(2,1)S(1)} %get-tuple-element.325), channel_id=1, source_target_pairs={{0,1},{1,2},{2,3},{3,4},{4,5},{5,6},{6,7},{7,8},{8,9},{9,10},{10,1... | collective-permute-start | bytes 196616 | tf_op jit(solution)/shard_map/ppermute | solution.py:17
  495.8 1.9 copy-start.19
  497.8 1.2 copy-start.18
  499.0 1.2 copy-start.17
Sparse Core Ops, SparseCore 0:
  229.8 266.0 all-reduce.2
where the time goes:
time: 514 us; the launch traced here: 508 us
  waiting for transfers between devices  201 us (39%)
  blocking collectives  81.6 us (16%)
  matrix products  81.2 us (16%)
  local copies, waits for them, and re-layouts  73.9 us (14%)
  starting transfers between devices  30.1 us (6%)
  loops' own time  16.6 us (3%)
  between operations  14.8 us (3%)
  other arithmetic  8.22 us (2%)
    psum x1, waiting for transfers between devices, shards(): lax.psum((stacked[0], stacked[1], stacked[2], stacked[3], stacked[4]), ('...  180 us
    psum x1, blocking collectives, shards(): lax.psum((stacked[0], stacked[1], stacked[2], stacked[3], stacked[4]), ('...  81.6 us
    dot_general x72, matrix products, product(): return jnp.einsum(form, left, right, preferred_element_type=jnp.float32)  35.9 us
    div x24, matrix products, attention_probs(): return exponentials / jnp.sum(exponentials, axis=-1, keepdims=True)  28 us
    dynamic_update_slice x56, local copies, waits for them, and re-layouts, over_heads(): stacked = lax.map(single_head, jnp.arange(HEADS))  20.7 us
    another operation x3, loops' own time, over_heads(): stacked = lax.map(single_head, jnp.arange(HEADS))  16.6 us
    all_to_all x1, starting transfers between devices, shards(): lax.all_to_all(middle, 'tm', split_axis=3, concat_axis=1, tiled=True)  14.8 us
    dynamic_slice x24, local copies, waits for them, and re-layouts, over_heads(): stacked = lax.map(single_head, jnp.arange(HEADS))  14.3 us
  transfers between devices with their start and end apart: 6, of which 4 were waited for; matrix products, arithmetic and copies ran while one was open for 5% of the time, Pallas kernels for 0%

commit v1 on v0

v1 whole, which is shorter than its diff:
```python
import math

import jax
import jax.numpy as jnp
from jax import lax
from jax.experimental import pallas as pl
from jax.experimental.pallas import tpu as pltpu
from jax.sharding import Mesh, PartitionSpec as P

HEADS = 8
HEAD = 32
D = 256
K = 256
HOP = 128
SEGMENTS = 128
EPSILON = 1e-05
SCALE = HEAD ** (-0.5)
LOG2E = math.log2(math.e)
BF = jnp.bfloat16
F32 = jnp.float32
VMEM_LIMIT = 48 * 1024 * 1024

AXES = ("yh", "core", "yl", "x", "z")
DP = ("yh", "core")
TM = ("yl", "x", "z")
PLANE = ("yh", "yl", "x")


def dot(left, right, left_dim, right_dim):
    return lax.dot_general(
        left, right, (((left_dim,), (right_dim,)), ((), ())), preferred_element_type=F32
    )


def nn(left, right):
    return dot(left, right, 1, 0)


def nt(left, right):
    return dot(left, right, 1, 1)


def tn(left, right):
    return dot(left, right, 0, 0)


def standardize(rows):
    average = jnp.mean(rows, axis=-1, keepdims=True)
    centered = rows - average
    variance = jnp.mean(centered * centered, axis=-1, keepdims=True)
    inverse = lax.rsqrt(variance + EPSILON)
    return centered * inverse, inverse


def norm_pullback(grad_normed, unit, inverse, gain):
    grad_unit = grad_normed * gain
    first = jnp.mean(grad_unit, axis=-1, keepdims=True)
    second = jnp.mean(grad_unit * unit, axis=-1, keepdims=True)
    return inverse * (grad_unit - first - unit * second)


def head_masks():
    lane = lax.broadcasted_iota(jnp.int32, (1, 128), 1)
    return [jnp.where(lane // HEAD == i, 1.0, 0.0).astype(BF) for i in range(4)]


def row_masks():
    row = lax.broadcasted_iota(jnp.int32, (128, 1), 0)
    return [jnp.where(row // HEAD == i, 1.0, 0.0).astype(BF) for i in range(4)]


def select_rows(out_rows, in_rows, source):
    out = lax.broadcasted_iota(jnp.int32, (out_rows, in_rows), 0)
    col = lax.broadcasted_iota(jnp.int32, (out_rows, in_rows), 1)
    return jnp.where(source(out) == col, 1.0, 0.0).astype(BF)


def softmax_keys(scores):
    highest = jnp.max(scores, axis=0, keepdims=True)
    powers = jnp.exp2((scores - highest) * (SCALE * LOG2E))
    return powers * (1.0 / jnp.sum(powers, axis=0, keepdims=True))


def owner_source(out):
    return ((out // 2) % 4) * 64 + (out // 8) * 2 + out % 2


def owner_target(out):
    return ((out % 64) // 2) * 8 + (out // 64) * 2 + out % 2


def segment_source(out):
    return (out % 64) * 4 + out // 64


def segment_target(out):
    return (out % 4) * 64 + out // 4


def intra_forward_kernel(f_ref, n_ref, gain_ref, wq_ref, wk_ref, wv_ref, wo_ref, mid_ref, ctx_ref):
    rows = jnp.concatenate([f_ref[...], n_ref[...]], axis=0).astype(F32)
    unit, _ = standardize(rows)
    normed = (unit * gain_ref[0:1, :]).astype(BF)
    keys = nn(normed, wk_ref[0]).astype(BF)
    queries_t = nt(wq_ref[0].T, normed).astype(BF)
    values_t = nt(wv_ref[0].T, normed).astype(BF)
    masks = head_masks()
    mids = []
    for g in range(2):
        at = g * HOP
        for h in range(HEADS):
            block = slice((h // 4) * 128, (h // 4) * 128 + 128)
            feats = slice(h * HEAD, h * HEAD + HEAD)
            scores = nn(
                keys[at : at + K, block] * masks[h % 4], queries_t[block, at : at + K]
            )
            low = softmax_keys(scores).astype(BF)
            ctx_ref[g, feats, :] = nn(values_t[feats, at : at + K], low).astype(BF)
        mids.append((rows[at : at + K] + tn(ctx_ref[g], wo_ref[0])).astype(BF))
    pick = select_rows(256, 256, owner_source)
    for t in range(2):
        part = jnp.concatenate(
            [mids[g][h * HOP + 64 * t : h * HOP + 64 * t + 64] for g in range(2) for h in range(2)],
            axis=0,
        )
        mid_ref[256 * t : 256 * t + 256, :] = nn(pick, part).astype(BF)


def intra_forward(frames, following, gains, wq, wk, wv, wo):
    return pl.pallas_call(
        intra_forward_kernel,
        out_shape=(
            jax.ShapeDtypeStruct((2 * K, D), BF),
            jax.ShapeDtypeStruct((2, D, K), BF),
        ),
        compiler_params=pltpu.CompilerParams(vmem_limit_bytes=VMEM_LIMIT),
        name="intra_forward",
    )(frames, following, gains, wq, wk, wv, wo)


def inter_kernel(
    m_ref, g_ref, gain_ref, wq_ref, wk_ref, wv_ref, wo_ref, out_ref, dw_ref,
    ctx_t, gq_t, gk_ref, gv_ref,
):
    gain = gain_ref[1:2, :]
    pick = select_rows(256, 256, segment_source)
    tiles = [nn(pick, m_ref[256 * t : 256 * t + 256, :]) for t in range(2)]
    rows = jnp.concatenate(
        [tiles[t][64 * p : 64 * p + 64] for p in range(4) for t in range(2)], axis=0
    )

    def grad_source(out):
        segment = out % 128 + out // 256
        return jnp.where(segment < SEGMENTS, segment * 2 + (out // 128) % 2, -1)

    grads = nn(select_rows(512, 256, grad_source), g_ref[...]).astype(BF)
    unit, inverse = standardize(rows)
    normed = (unit * gain).astype(BF)
    normed_t = normed.T
    wq, wk, wv, wo = wq_ref[1], wk_ref[1], wv_ref[1], wo_ref[1]
    queries = nn(normed, wq).astype(BF)
    keys = nn(normed, wk).astype(BF)
    values = nn(normed, wv).astype(BF)
    grad_context = nt(grads, wo).astype(BF)
    queries_t = queries.T
    keys_t = keys.T
    values_t = values.T
    grad_context_t = grad_context.T
    masks = head_masks()
    downs = row_masks()
    for p in range(4):
        at = slice(128 * p, 128 * p + 128)
        for b in range(2):
            block = slice(128 * b, 128 * b + 128)
            gv = jnp.zeros((128, 128), F32)
            gk = jnp.zeros((128, 128), F32)
            for pair in range(2):
                first, second = 2 * pair, 2 * pair + 1
                feats = slice(128 * b + 64 * pair, 128 * b + 64 * pair + 64)
                top = slice(128 * b + 64 * pair, 128 * b + 64 * pair + 32)
                low_half = slice(128 * b + 64 * pair + 32, 128 * b + 64 * pair + 64)
                qt, gt = queries_t[block, at], grad_context_t[block, at]
                scores = nn(
                    keys[at, block],
                    jnp.concatenate([qt * downs[first], qt * downs[second]], axis=1),
                )
                probs = softmax_keys(scores)
                low = probs.astype(BF)
                both = nn(values_t[feats, at], low).astype(BF)
                ctx_t[top, at] = both[:32, :128]
                ctx_t[low_half, at] = both[32:, 128:]
                grad_probs = nn(
                    values[at, block],
                    jnp.concatenate([gt * downs[first], gt * downs[second]], axis=1),
                )
                inner = jnp.sum(grad_probs * probs, axis=0, keepdims=True)
                grad_scores = (probs * (grad_probs - inner) * SCALE).astype(BF)
                gc = grad_context[at, block]
                gv += nn(low, jnp.concatenate([gc * masks[first], gc * masks[second]], axis=0))
                qs = queries[at, block]
                gk += nn(
                    grad_scores, jnp.concatenate([qs * masks[first], qs * masks[second]], axis=0)
                )
                both = nn(keys_t[feats, at], grad_scores).astype(BF)
                gq_t[top, at] = both[:32, :128]
                gq_t[low_half, at] = both[32:, 128:]
            gk_ref[at, block] = gk.astype(BF)
            gv_ref[at, block] = gv.astype(BF)
    gqt, gk, gv = gq_t[...], gk_ref[...], gv_ref[...]
    dw_ref[0] = nt(normed_t, gqt)
    dw_ref[1] = nn(normed_t, gk)
    dw_ref[2] = nn(normed_t, gv)
    dw_ref[3] = nn(ctx_t[...], grads)
    grad_normed = nt(gqt.T, wq) + nt(gk, wk) + nt(gv, wv)
    result = (grads.astype(F32) + norm_pullback(grad_normed, unit, inverse, gain)).astype(BF)
    back = select_rows(256, 256, segment_target)
    for t in range(2):
        part = jnp.concatenate(
            [result[128 * p + 64 * t : 128 * p + 64 * t + 64] for p in range(4)], axis=0
        )
        out_ref[256 * t : 256 * t + 256, :] = nn(back, part).astype(BF)


def inter(middle, grads, gains, wq, wk, wv, wo):
    return pl.pallas_call(
        inter_kernel,
        out_shape=(
            jax.ShapeDtypeStruct((512, D), BF),
            jax.ShapeDtypeStruct((4, D, D), F32),
        ),
        scratch_shapes=[
            pltpu.VMEM((D, 512), BF),
            pltpu.VMEM((D, 512), BF),
            pltpu.VMEM((512, D), BF),
            pltpu.VMEM((512, D), BF),
        ],
        compiler_params=pltpu.CompilerParams(vmem_limit_bytes=VMEM_LIMIT),
        name="inter",
    )(middle, grads, gains, wq, wk, wv, wo)


def intra_backward_kernel(
    core_ref, m_ref, ctx_ref, dw1_ref, f_ref, n_ref, gain_ref, wq_ref, wk_ref, wv_ref, wo_ref,
    first_ref, second_ref, carry_ref, keep_ref, send_ref,
    gq_t, gk_ref, gv_ref,
):
    gain = gain_ref[0:1, :]
    rows = jnp.concatenate([f_ref[...], n_ref[...]], axis=0).astype(F32)
    unit, inverse = standardize(rows)
    normed = (unit * gain).astype(BF)
    normed_t = normed.T
    wq, wk, wv, wo = wq_ref[0], wk_ref[0], wv_ref[0], wo_ref[0]
    queries = nn(normed, wq).astype(BF)
    keys = nn(normed, wk).astype(BF)
    values = nn(normed, wv).astype(BF)
    queries_t = queries.T
    keys_t = keys.T
    masks = head_masks()
    pick = select_rows(256, 256, owner_target)
    tiles = [nn(pick, m_ref[256 * t : 256 * t + 256, :]).astype(BF) for t in range(2)]
    totals = [jnp.zeros((D, D), F32) for _ in range(4)]
    halves = []
    for g in range(2):
        at = slice(g * HOP, g * HOP + K)
        grads = jnp.concatenate(
            [tiles[t][128 * g + 64 * h : 128 * g + 64 * h + 64] for h in range(2) for t in range(2)],
            axis=0,
        )
        grad_context = nt(grads, wo).astype(BF)
        grad_context_t = grad_context.T
        for b in range(2):
            block = slice(128 * b, 128 * b + 128)
            gv = jnp.zeros((K, 128), F32)
            gk = jnp.zeros((K, 128), F32)
            for i in range(4):
                feats = slice(128 * b + HEAD * i, 128 * b + HEAD * i + HEAD)
                scores = nn(keys[at, block] * masks[i], queries_t[block, at])
                probs = softmax_keys(scores)
                low = probs.astype(BF)
                grad_probs = nn(values[at, block] * masks[i], grad_context_t[block, :])
                inner = jnp.sum(grad_probs * probs, axis=0, keepdims=True)
                grad_scores = (probs * (grad_probs - inner) * SCALE).astype(BF)
                gv += nn(low, grad_context[:, block] * masks[i])
                gk += nn(grad_scores, queries[at, block] * masks[i])
                gq_t[feats, :] = nn(keys_t[feats, at], grad_scores).astype(BF)
            gk_ref[:, block] = gk.astype(BF)
            gv_ref[:, block] = gv.astype(BF)
        gqt, gk, gv = gq_t[...], gk_ref[...], gv_ref[...]
        totals[0] += nt(normed_t[:, at], gqt)
        totals[1] += nn(normed_t[:, at], gk)
        totals[2] += nn(normed_t[:, at], gv)
        totals[3] += nn(ctx_ref[g], grads)
        grad_normed = nt(gqt.T, wq) + nt(gk, wk) + nt(gv, wv)
        result = grads.astype(F32) + norm_pullback(grad_normed, unit[at], inverse[at], gain)
        result = result.astype(BF)
        halves.append((result[:HOP], result[HOP:]))
    first_ref[...] = halves[0][0]
    second_ref[...] = (halves[1][0].astype(F32) + halves[0][1].astype(F32)).astype(BF)
    carry_ref[...] = halves[1][1]
    low_core = core_ref[0] == 0
    for i in range(2):
        for layer, pair in ((0, (totals[i], totals[2 + i])), (1, (dw1_ref[i], dw1_ref[2 + i]))):
            keep_ref[i, layer] = jnp.where(low_core, pair[0], pair[1])
            send_ref[i, layer] = jnp.where(low_core, pair[1], pair[0]).astype(BF)


def intra_backward(core, grads, ctx, dw1, frames, following, gains, wq, wk, wv, wo):
    vmem = pl.BlockSpec(memory_space=pltpu.VMEM)
    return pl.pallas_call(
        intra_backward_kernel,
        in_specs=[pl.BlockSpec(memory_space=pltpu.SMEM)] + [vmem] * 10,
        out_shape=(
            jax.ShapeDtypeStruct((HOP, D), BF),
            jax.ShapeDtypeStruct((HOP, D), BF),
            jax.ShapeDtypeStruct((HOP, D), BF),
            jax.ShapeDtypeStruct((2, 2, D, D), F32),
            jax.ShapeDtypeStruct((2, 2, D, D), BF),
        ),
        scratch_shapes=[
            pltpu.VMEM((D, K), BF),
            pltpu.VMEM((K, D), BF),
            pltpu.VMEM((K, D), BF),
        ],
        compiler_params=pltpu.CompilerParams(vmem_limit_bytes=VMEM_LIMIT),
        name="intra_backward",
    )(core, grads, ctx, dw1, frames, following, gains, wq, wk, wv, wo)


def finish_kernel(
    core_ref, mine_ref, other_ref, gain_ref, wq_ref, wk_ref, wv_ref,
    dq_ref, dk_ref, dv_ref, do_ref, dg_ref,
):
    low_core = core_ref[0] == 0
    for layer in range(2):
        lead = [mine_ref[i, layer].astype(F32) for i in range(2)]
        rest = [other_ref[i, layer].astype(F32) for i in range(2)]
        dq = jnp.where(low_core, lead[0], rest[0])
        dk = jnp.where(low_core, lead[1], rest[1])
        dv = jnp.where(low_core, rest[0], lead[0])
        dq_ref[layer] = dq
        dk_ref[layer] = dk
        dv_ref[layer] = dv
        do_ref[layer] = jnp.where(low_core, rest[1], lead[1])
        through = (
            dq * wq_ref[layer].astype(F32)
            + dk * wk_ref[layer].astype(F32)
            + dv * wv_ref[layer].astype(F32)
        )
        column = jnp.sum(through.T, axis=0, keepdims=True)
        dg_ref[layer : layer + 1, :] = column / gain_ref[layer : layer + 1, :]


def finish(core, mine, other, gains, wq, wk, wv):
    vmem = pl.BlockSpec(memory_space=pltpu.VMEM)
    full = jax.ShapeDtypeStruct((2, D, D), F32)
    return pl.pallas_call(
        finish_kernel,
        in_specs=[pl.BlockSpec(memory_space=pltpu.SMEM)] + [vmem] * 6,
        out_shape=(full, full, full, full, jax.ShapeDtypeStruct((2, D), F32)),
        compiler_params=pltpu.CompilerParams(vmem_limit_bytes=VMEM_LIMIT),
        name="finish",
    )(core, mine, other, gains, wq, wk, wv)


def shifted(shard, by):
    length = lax.axis_size(TM)
    pairs = [(i, i + by) for i in range(length) if 0 <= i + by < length]
    return lax.ppermute(shard, TM, pairs)


def exchanged(shard, axes):
    return lax.all_to_all(shard, axes, split_axis=0, concat_axis=0, tiled=True)


def swapped(shard):
    return lax.ppermute(shard, "core", [(0, 1), (1, 0)])


def shards(frames, frames_grad, wq, wk, wv, wo, gains):
    frames = frames[0]
    core = lax.axis_index("core").astype(jnp.int32).reshape(1)
    following = shifted(frames[:HOP], -1)
    by_owner = frames_grad.reshape(2, 64, 2, D).transpose(1, 0, 2, 3).reshape(64, 4, D)
    grads = exchanged(by_owner, TM).reshape(256, D)
    middle, ctx = intra_forward(frames, following, gains, wq, wk, wv, wo)
    across = exchanged(middle.reshape(64, 8, D), TM).reshape(512, D)
    grad_middle, dw1 = inter(across, grads, gains, wq, wk, wv, wo)
    grad_local = exchanged(grad_middle.reshape(64, 8, D), TM).reshape(512, D)
    first, second, carry, keep, send = intra_backward(
        core, grad_local, ctx, dw1, frames, following, gains, wq, wk, wv, wo
    )
    carried = shifted(carry, 1)
    arrived = swapped(send)
    half = (keep + arrived.astype(F32)).astype(BF).reshape(16, 64, D)
    pieces = exchanged(half, PLANE)
    piece = jnp.sum(pieces.astype(F32), axis=0).astype(BF)
    pieces = exchanged(jnp.broadcast_to(piece[None], (8, 64, D)), "z")
    piece = jnp.sum(pieces.astype(F32), axis=0).astype(BF)
    whole = exchanged(jnp.broadcast_to(piece[None], (16, 64, D)), PLANE).reshape(2, 2, D, D)
    other = swapped(whole)
    dq, dk, dv, do, dg = finish(core, whole, other, gains, wq, wk, wv)
    head = (first.astype(F32) + carried.astype(F32)).astype(BF)
    grad_frames = jnp.concatenate([head, second], axis=0)[None]
    return grad_frames, dq, dk, dv, do, dg


def solution(mesh):
    split = Mesh(mesh.devices.reshape(2, 2, 2, 4, 8), AXES)
    placed = (P(DP, TM, None), P(DP, TM, None), P(), P(), P(), P(), P())
    return jax.shard_map(
        shards,
        mesh=split,
        in_specs=placed,
        out_specs=(P(DP, TM, None), P(), P(), P(), P(), P()),
        check_vma=False,
    )
```

time: 514 us -> 145 us (0.28)
  the two profiles are of different devices: /device:TPU:1 before, /device:TPU:8 now
where the time goes in v1:
time: 145 us; the launch traced here: 144 us
  blocking collectives  42.8 us (30%)
  starting transfers between devices  36.8 us (25%)
  waiting for transfers between devices  35.6 us (25%)
  Pallas kernels  25.3 us (17%)
  local copies, waits for them, and re-layouts  1.96 us (1%)
    all_to_all x3, blocking collectives, exchanged(): return lax.all_to_all(shard, axes, split_axis=0, concat_axis=0, tiled=True)  42.8 us
    all_to_all x3, starting transfers between devices, exchanged(): return lax.all_to_all(shard, axes, split_axis=0, concat_axis=0, tiled=True)  27.5 us
    all_to_all x3, waiting for transfers between devices, exchanged(): return lax.all_to_all(shard, axes, split_axis=0, concat_axis=0, tiled=True)  23.7 us
    ppermute x2, waiting for transfers between devices, shifted(): return lax.ppermute(shard, TM, pairs)  9.97 us
    pallas_call x1, Pallas kernels, inter(): pl.pallas_call(inter_kernel, out_shape=(jax.ShapeDtypeStruct((512, D), BF...  9.55 us
    ppermute x2, starting transfers between devices, shifted(): return lax.ppermute(shard, TM, pairs)  9.2 us
    pallas_call x1, Pallas kernels, intra_backward(): pl.pallas_call(intra_backward_kernel, in_specs=[pl.BlockSpec(memory_space...  7.91 us
    pallas_call x1, Pallas kernels, intra_forward(): pl.pallas_call(intra_forward_kernel, out_shape=(jax.ShapeDtypeStruct((2 *...  6.2 us
  transfers between devices with their start and end apart: 7, of which 5 were waited for; matrix products, arithmetic and copies ran while one was open for 1% of the time, Pallas kernels for 4%

profile of v1, /device:TPU:8, one launch (start us, length us, event | category | flops | bytes accessed | tf_op | source)
XLA Modules:
  0.0 144.1 jit_solution(14646297536952214371)
XLA Ops:
  0.6 0.0 copy-start.3
  0.6 0.0 copy-start.5
  0.7 1.0 reshape.48
  1.7 0.0 copy-start.2
  1.7 0.1 copy.14
  1.8 0.0 copy-start.4
  1.8 0.0 copy-start.1
  1.8 0.7 reshape.49
  2.5 0.0 copy-start
  2.5 13.2 %all-to-all-start.1 = ((bf16[64,4,256]{2,1,0:T(4,128)(2,1)}), bf16[64,4,256]{2,1,0:T(4,128)(2,1)S(1)}, u32[]{:S(2)}, u32[]{:S(2)}) async-start(bf16[64,4,256]{2,1,0:T(4,128)(2,1)} %reshape.49), calls=%async_computation.1 | async-start | bytes 262144 | tf_op jit(solution)/shard_map/all_to_all | solution.py:372
  15.7 0.0 copy-done.4
  15.7 6.7 %collective-permute-start = (bf16[128,256]{1,0:T(8,128)(2,1)S(1)}, bf16[128,256]{1,0:T(8,128)(2,1)S(1)}, u32[]{:S(2)}, u32[]{:S(2)}) collective-permute-start(bf16[128,256]{1,0:T(8,128)(2,1)S(1)} %slice_bitcast_fusion), channel_id=1, source_target_pairs={{1,0},{2,1},{3,2},{4,3},{5,4},{6,5},{7,6},{8,7},{9,8},{10,9},{11,1... | collective-permute-start | bytes 196616 | tf_op jit(solution)/shard_map/ppermute | solution.py:368
  22.4 1.9 %collective-permute-done.n_ref = bf16[128,256]{1,0:T(8,128)(2,1)S(1)} collective-permute-done((bf16[128,256]{1,0:T(8,128)(2,1)S(1)}, bf16[128,256]{1,0:T(8,128)(2,1)S(1)}, u32[]{:S(2)}, u32[]{:S(2)}) %collective-permute-start) | collective-permute-done | bytes 65568 | tf_op jit(solution)/shard_map/ppermute | solution.py:368
  24.3 0.0 copy-done.3
  24.3 0.0 copy-done.5
  24.3 0.0 copy-done.2
  24.3 0.0 copy-done.1
  24.3 0.0 copy-done
  24.3 6.2 %intra_forward.1 = (bf16[512,256]{1,0:T(8,128)(2,1)}, bf16[2,256,256]{2,1,0:T(8,128)(2,1)S(1)}) custom-call(bf16[256,256]{1,0:T(8,128)(2,1)S(1)} %bitcast.17, bf16[128,256]{1,0:T(8,128)(2,1)S(1)} %collective-permute-done.n_ref, f32[2,256]{1,0:T(2,128)S(1)} %copy-done.5, bf16[2,256,256]{2,1,0:T(8,128)(2,1)S(1)} %copy-done, ...), custom_call_target="tpu_custom_call" | custom-call | tf_op jit(solution)/shard_map/intra_forward/pallas_call | solution.py:130
  30.5 0.0 all-to-all-done.1
  30.5 9.1 %all-to-all-start = ((bf16[64,8,256]{2,1,0:T(8,128)(2,1)}), bf16[64,8,256]{2,1,0:T(8,128)(2,1)S(1)}, u32[]{:S(2)}, u32[]{:S(2)}) async-start(bf16[64,8,256]{2,1,0:T(8,128)(2,1)} %bitcast.3), calls=%async_computation | async-start | bytes 524288 | tf_op jit(solution)/shard_map/all_to_all | solution.py:372
  39.7 11.8 %all-to-all-done = bf16[64,8,256]{2,1,0:T(8,128)(2,1)S(1)} async-done(((bf16[64,8,256]{2,1,0:T(8,128)(2,1)}), bf16[64,8,256]{2,1,0:T(8,128)(2,1)S(1)}, u32[]{:S(2)}, u32[]{:S(2)}) %all-to-all-start) | async-done | bytes 262176 | tf_op jit(solution)/shard_map/all_to_all | solution.py:372
  51.4 9.6 %inter.1 = (bf16[512,256]{1,0:T(8,128)(2,1)}, f32[4,256,256]{2,1,0:T(8,128)S(1)}) custom-call(bf16[512,256]{1,0:T(8,128)(2,1)S(1)} %bitcast.15, bf16[256,256]{1,0:T(8,128)(2,1)S(1)} %reshape.50.g_ref, f32[2,256]{1,0:T(2,128)S(1)} %copy-done.5, bf16[2,256,256]{2,1,0:T(8,128)(2,1)S(1)} %copy-done, bf16[2,256,256]{2,1,0:T(8,128)(2,1)S(1)} %copy-done.1, ...), custom_call_target="tpu_custom_call" | custom-call | tf_op jit(solution)/shard_map/inter/pallas_call | solution.py:225
  61.0 5.2 %all-to-all-start.2 = ((bf16[64,8,256]{2,1,0:T(8,128)(2,1)}), bf16[64,8,256]{2,1,0:T(8,128)(2,1)S(1)}, u32[]{:S(2)}, u32[]{:S(2)}) async-start(bf16[64,8,256]{2,1,0:T(8,128)(2,1)} %bitcast.6), calls=%async_computation.2 | async-start | bytes 524288 | tf_op jit(solution)/shard_map/all_to_all | solution.py:372
  66.2 11.9 %all-to-all-done.2 = bf16[64,8,256]{2,1,0:T(8,128)(2,1)S(1)} async-done(((bf16[64,8,256]{2,1,0:T(8,128)(2,1)}), bf16[64,8,256]{2,1,0:T(8,128)(2,1)S(1)}, u32[]{:S(2)}, u32[]{:S(2)}) %all-to-all-start.2) | async-done | bytes 262176 | tf_op jit(solution)/shard_map/all_to_all | solution.py:372
  78.2 7.9 %intra_backward.1 = (bf16[128,256]{1,0:T(8,128)(2,1)S(1)}, bf16[128,256]{1,0:T(8,128)(2,1)S(1)}, bf16[128,256]{1,0:T(8,128)(2,1)S(1)}, f32[2,2,256,256]{3,2,1,0:T(8,128)S(1)}, bf16[2,2,256,256]{3,2,1,0:T(8,128)(2,1)S(1)}) custom-call(s32[1]{0:T(128)} %bitcast.core_ref, bf16[512,256]{1,0:T(8,128)(2,1)S(1)} %bitcast.16, ...), custom_call_target="tpu_custom_call" | custom-call | tf_op jit(solution)/shard_map/intra_backward/pallas_call | solution.py:309
  86.1 0.1 collective-permute-start.2
  86.2 1.9 %collective-permute-done.2 = bf16[2,2,256,256]{3,2,1,0:T(8,128)(2,1)S(1)} collective-permute-done((bf16[2,2,256,256]{3,2,1,0:T(8,128)(2,1)S(1)}, bf16[2,2,256,256]{3,2,1,0:T(8,128)(2,1)S(1)}, u32[]{:S(2)}, u32[]{:S(2)}) %collective-permute-start.2) | collective-permute-done | bytes 524320 | tf_op jit(solution)/shard_map/ppermute | solution.py:376
  88.1 0.1 add_convert_fusion
  88.2 15.3 %all_to_all.30 = bf16[16,64,256]{2,1,0:T(8,128)(2,1)S(1)} all-to-all(bf16[16,64,256]{2,1,0:T(8,128)(2,1)S(1)} %bitcast.19), channel_id=1, replica_groups=mesh['yh'=2,'core'=2,'yl'=2,'x'=4,'z'=8] {'yh','yl','x'}, dimensions={0} | all-to-all | bytes 1048576 | tf_op jit(solution)/shard_map/all_to_all | solution.py:372
  103.5 0.1 reduce_sum.24
  103.6 13.8 %all_to_all.31 = bf16[8,64,256]{2,1,0:T(8,128)(2,1)S(1)} all-to-all(bf16[8,64,256]{2,1,0:T(8,128)(2,1)S(1)} %broadcast_in_dim.7), channel_id=1, replica_groups=mesh['yh'=2,'core'=2,'yl'=2,'x'=4,'z'=8] {'z'}, dimensions={0} | all-to-all | bytes 524288 | tf_op jit(solution)/shard_map/all_to_all | solution.py:372
  117.4 13.8 %all_to_all.32 = bf16[16,64,256]{2,1,0:T(8,128)(2,1)S(1)} all-to-all(bf16[16,64,256]{2,1,0:T(8,128)(2,1)S(1)} %broadcast_in_dim.8), channel_id=1, replica_groups=mesh['yh'=2,'core'=2,'yl'=2,'x'=4,'z'=8] {'yh','yl','x'}, dimensions={0} | all-to-all | bytes 1048576 | tf_op jit(solution)/shard_map/all_to_all | solution.py:372
  131.2 0.0 collective-permute-start.3
  131.2 2.5 %collective-permute-start.1 = (bf16[128,256]{1,0:T(8,128)(2,1)S(1)}, bf16[128,256]{1,0:T(8,128)(2,1)S(1)}, u32[]{:S(2)}, u32[]{:S(2)}) collective-permute-start(bf16[128,256]{1,0:T(8,128)(2,1)S(1)} %get-tuple-element.25), channel_id=1, source_target_pairs={{0,1},{1,2},{2,3},{3,4},{4,5},{5,6},{6,7},{7,8},{8,9},{9,10},{10,1... | collective-permute-start | bytes 196616 | tf_op jit(solution)/shard_map/ppermute | solution.py:368
  133.8 8.1 %collective-permute-done.1 = bf16[128,256]{1,0:T(8,128)(2,1)S(1)} collective-permute-done((bf16[128,256]{1,0:T(8,128)(2,1)S(1)}, bf16[128,256]{1,0:T(8,128)(2,1)S(1)}, u32[]{:S(2)}, u32[]{:S(2)}) %collective-permute-start.1) | collective-permute-done | bytes 65568 | tf_op jit(solution)/shard_map/ppermute | solution.py:368
  141.9 0.7 maximum_bitcast_fusion
  142.5 0.0 collective-permute-done.3.other_ref
  142.5 1.6 %finish.1 = (f32[2,256,256]{2,1,0:T(8,128)}, f32[2,256,256]{2,1,0:T(8,128)}, f32[2,256,256]{2,1,0:T(8,128)}, f32[2,256,256]{2,1,0:T(8,128)}, f32[2,256]{1,0:T(2,128)}) custom-call(s32[1]{0:T(128)} %bitcast.core_ref, bf16[2,2,256,256]{3,2,1,0:T(8,128)(2,1)S(1)} %bitcast.14, bf16[2,2,256,256]{3,2,1,0:T(8,128)(2,1)S(1)} %collective-permute-done.3.other_ref, ...), custom_call_target="tpu_custom_call" | custom-call | tf_op jit(solution)/shard_map/finish/pallas_call | solution.py:356
  (6 shorter events, 0.2 us)
Async XLA Ops:
  0.6 23.7 %copy-start.3 = (bf16[2,256,256]{2,1,0:T(8,128)(2,1)S(1)}, bf16[2,256,256]{2,1,0:T(8,128)(2,1)}, u32[]{:S(2)}) copy-start(bf16[2,256,256]{2,1,0:T(8,128)(2,1)} %wo_ref.5) | copy-start | bytes 786436
  0.6 23.7 %copy-start.5 = (f32[2,256]{1,0:T(2,128)S(1)}, f32[2,256]{1,0:T(2,128)}, u32[]{:S(2)}) copy-start(f32[2,256]{1,0:T(2,128)} %gain_ref.7) | copy-start | bytes 6148
  1.7 22.7 %copy-start.2 = (bf16[2,256,256]{2,1,0:T(8,128)(2,1)S(1)}, bf16[2,256,256]{2,1,0:T(8,128)(2,1)}, u32[]{:S(2)}) copy-start(bf16[2,256,256]{2,1,0:T(8,128)(2,1)} %wv_ref.7) | copy-start | bytes 786436
  1.8 13.9 %copy-start.4 = (bf16[1,256,256]{2,1,0:T(8,128)(2,1)S(1)}, bf16[1,256,256]{2,1,0:T(8,128)(2,1)}, u32[]{:S(2)}) copy-start(bf16[1,256,256]{2,1,0:T(8,128)(2,1)} %param.7) | copy-start | bytes 393220
  1.8 22.5 %copy-start.1 = (bf16[2,256,256]{2,1,0:T(8,128)(2,1)S(1)}, bf16[2,256,256]{2,1,0:T(8,128)(2,1)}, u32[]{:S(2)}) copy-start(bf16[2,256,256]{2,1,0:T(8,128)(2,1)} %wk_ref.7) | copy-start | bytes 786436
  2.5 21.8 %copy-start = (bf16[2,256,256]{2,1,0:T(8,128)(2,1)S(1)}, bf16[2,256,256]{2,1,0:T(8,128)(2,1)}, u32[]{:S(2)}) copy-start(bf16[2,256,256]{2,1,0:T(8,128)(2,1)} %wq_ref.7) | copy-start | bytes 786436
  2.5 28.0 %all-to-all-start.1 = ((bf16[64,4,256]{2,1,0:T(4,128)(2,1)}), bf16[64,4,256]{2,1,0:T(4,128)(2,1)S(1)}, u32[]{:S(2)}, u32[]{:S(2)}) async-start(bf16[64,4,256]{2,1,0:T(4,128)(2,1)} %reshape.49), calls=%async_computation.1 | async-start | bytes 262144 | tf_op jit(solution)/shard_map/all_to_all | solution.py:372
  15.7 8.6 %collective-permute-start = (bf16[128,256]{1,0:T(8,128)(2,1)S(1)}, bf16[128,256]{1,0:T(8,128)(2,1)S(1)}, u32[]{:S(2)}, u32[]{:S(2)}) collective-permute-start(bf16[128,256]{1,0:T(8,128)(2,1)S(1)} %slice_bitcast_fusion), channel_id=1, source_target_pairs={{1,0},{2,1},{3,2},{4,3},{5,4},{6,5},{7,6},{8,7},{9,8},{10,9},{11,1... | collective-permute-start | bytes 196616 | tf_op jit(solution)/shard_map/ppermute | solution.py:368
  30.5 20.9 %all-to-all-start = ((bf16[64,8,256]{2,1,0:T(8,128)(2,1)}), bf16[64,8,256]{2,1,0:T(8,128)(2,1)S(1)}, u32[]{:S(2)}, u32[]{:S(2)}) async-start(bf16[64,8,256]{2,1,0:T(8,128)(2,1)} %bitcast.3), calls=%async_computation | async-start | bytes 524288 | tf_op jit(solution)/shard_map/all_to_all | solution.py:372
  61.0 17.2 %all-to-all-start.2 = ((bf16[64,8,256]{2,1,0:T(8,128)(2,1)}), bf16[64,8,256]{2,1,0:T(8,128)(2,1)S(1)}, u32[]{:S(2)}, u32[]{:S(2)}) async-start(bf16[64,8,256]{2,1,0:T(8,128)(2,1)} %bitcast.6), calls=%async_computation.2 | async-start | bytes 524288 | tf_op jit(solution)/shard_map/all_to_all | solution.py:372
  86.1 2.0 %collective-permute-start.2 = (bf16[2,2,256,256]{3,2,1,0:T(8,128)(2,1)S(1)}, bf16[2,2,256,256]{3,2,1,0:T(8,128)(2,1)S(1)}, u32[]{:S(2)}, u32[]{:S(2)}) collective-permute-start(bf16[2,2,256,256]{3,2,1,0:T(8,128)(2,1)S(1)} %get-tuple-element.28), channel_id=1, source_target_pairs={{0,64},{64,0},{1,65},{65,1},{2,66},{66,2},{3,67},{67,3},{4,68},{68... | collective-permute-start | bytes 1572872 | tf_op jit(solution)/shard_map/ppermute | solution.py:376
  131.2 11.3 %collective-permute-start.3 = (bf16[2,2,256,256]{3,2,1,0:T(8,128)(2,1)S(1)}, bf16[2,2,256,256]{3,2,1,0:T(8,128)(2,1)S(1)}, u32[]{:S(2)}, u32[]{:S(2)}) collective-permute-start(bf16[2,2,256,256]{3,2,1,0:T(8,128)(2,1)S(1)} %bitcast.13), channel_id=1, source_target_pairs={{0,64},{64,0},{1,65},{65,1},{2,66},{66,2},{3,67},{67,3},{4,68},{68... | collective-permute-start | bytes 1572872 | tf_op jit(solution)/shard_map/ppermute | solution.py:376
  131.2 10.6 %collective-permute-start.1 = (bf16[128,256]{1,0:T(8,128)(2,1)S(1)}, bf16[128,256]{1,0:T(8,128)(2,1)S(1)}, u32[]{:S(2)}, u32[]{:S(2)}) collective-permute-start(bf16[128,256]{1,0:T(8,128)(2,1)S(1)} %get-tuple-element.25), channel_id=1, source_target_pairs={{0,1},{1,2},{2,3},{3,4},{4,5},{5,6},{6,7},{7,8},{8,9},{9,10},{10,1... | collective-permute-start | bytes 196616 | tf_op jit(solution)/shard_map/ppermute | solution.py:368

commit v2 on v1

v2 whole, which is shorter than its diff:
```python
import math

import jax
import jax.numpy as jnp
from jax import lax
from jax.experimental import pallas as pl
from jax.experimental.pallas import tpu as pltpu
from jax.sharding import Mesh, PartitionSpec as P

HEADS = 8
HEAD = 32
D = 256
K = 256
HOP = 128
SEGMENTS = 128
EPSILON = 1e-05
SCALE = HEAD ** (-0.5)
LOG2E = math.log2(math.e)
BF = jnp.bfloat16
F32 = jnp.float32
VMEM_LIMIT = 24 * 1024 * 1024

AXES = ("yh", "core", "yl", "x", "z")
DP = ("yh", "core")
TM = ("yl", "x", "z")
PLANE = ("yh", "yl", "x")


def dot(left, right, left_dim, right_dim):
    return lax.dot_general(
        left, right, (((left_dim,), (right_dim,)), ((), ())), preferred_element_type=F32
    )


def nn(left, right):
    return dot(left, right, 1, 0)


def nt(left, right):
    return dot(left, right, 1, 1)


def tn(left, right):
    return dot(left, right, 0, 0)


def standardize(rows):
    average = jnp.mean(rows, axis=-1, keepdims=True)
    centered = rows - average
    variance = jnp.mean(centered * centered, axis=-1, keepdims=True)
    inverse = lax.rsqrt(variance + EPSILON)
    return centered * inverse, inverse


def norm_pullback(grad_normed, unit, inverse, gain):
    grad_unit = grad_normed * gain
    first = jnp.mean(grad_unit, axis=-1, keepdims=True)
    second = jnp.mean(grad_unit * unit, axis=-1, keepdims=True)
    return inverse * (grad_unit - first - unit * second)


def head_masks():
    lane = lax.broadcasted_iota(jnp.int32, (1, 128), 1)
    return [jnp.where(lane // HEAD == i, 1.0, 0.0).astype(BF) for i in range(4)]


def row_masks():
    row = lax.broadcasted_iota(jnp.int32, (128, 1), 0)
    return [jnp.where(row // HEAD == i, 1.0, 0.0).astype(BF) for i in range(4)]


def select_rows(out_rows, in_rows, source):
    out = lax.broadcasted_iota(jnp.int32, (out_rows, in_rows), 0)
    col = lax.broadcasted_iota(jnp.int32, (out_rows, in_rows), 1)
    return jnp.where(source(out) == col, 1.0, 0.0).astype(BF)


def softmax_keys(scores):
    highest = jnp.max(scores, axis=0, keepdims=True)
    powers = jnp.exp2((scores - highest) * (SCALE * LOG2E))
    return powers * (1.0 / jnp.sum(powers, axis=0, keepdims=True))


def owner_target(out):
    return ((out % 64) // 2) * 8 + (out // 64) * 2 + out % 2


def segment_target(out):
    return (out % 4) * 64 + out // 4


def packed_source(out):
    device, row = out // 24, out % 24
    part = row % 8
    middle = (row // 8) * 128 + (part // 2) * 32 + device * 2 + part % 2
    rest = row - 16
    grads = 256 + (rest // 4) * 64 + ((rest % 4) // 2) * 32 + device * 2 + rest % 2
    return jnp.where(row < 16, middle, grads)


def unpacked_source(out):
    column, place = out // 128, out % 128
    segment = place % 32
    middle = (segment // 2) * 24 + column * 8 + (segment % 2) * 4 + place // 32
    rest = out - 256
    column, place = rest // 64, rest % 64
    segment = place % 32
    grads = (segment // 2) * 24 + 16 + column * 4 + (segment % 2) * 2 + place // 32
    return jnp.where(out < 256, middle, grads)


def staged(count, *stages):
    held = [{} for _ in stages]
    for t in range(count + len(stages) - 1):
        for i, stage in enumerate(stages):
            step = t - i
            if 0 <= step < count:
                held[i][step] = stage(step, *([held[i - 1].pop(step)] if i else []))


def attend(keys, queries_t, values_t, ctx_ref):
    masks = head_masks()

    def scores_of(h):
        block = slice((h // 4) * 128, (h // 4) * 128 + 128)
        return nn(keys[:, block] * masks[h % 4], queries_t[block, :])

    def weigh(h, scores):
        return softmax_keys(scores).astype(BF)

    def collect(h, low):
        feats = slice(h * HEAD, h * HEAD + HEAD)
        ctx_ref[feats, :] = nn(values_t[feats, :], low).astype(BF)

    staged(HEADS, scores_of, weigh, collect)


def intra_first_kernel(
    f_ref, gain_ref, wq_ref, wk_ref, wv_ref, wo_ref, mid_ref, ctx_ref, keys_ref, queries_ref, values_ref
):
    rows = f_ref[...].astype(F32)
    unit, _ = standardize(rows)
    normed = (unit * gain_ref[0:1, :]).astype(BF)
    keys = nn(normed, wk_ref[0]).astype(BF)
    queries_t = nt(wq_ref[0].T, normed).astype(BF)
    values_t = nt(wv_ref[0].T, normed).astype(BF)
    attend(keys, queries_t, values_t, ctx_ref)
    mid_ref[...] = (rows + tn(ctx_ref[...], wo_ref[0])).astype(BF)
    keys_ref[...] = keys[HOP:]
    queries_ref[...] = queries_t[:, HOP:]
    values_ref[...] = values_t[:, HOP:]


def intra_second_kernel(
    f_ref, n_ref, grad_ref, mid_in_ref, keys_ref, queries_ref, values_ref,
    gain_ref, wq_ref, wk_ref, wv_ref, wo_ref, packed_ref, ctx_ref,
):
    rows = n_ref[...].astype(F32)
    unit, _ = standardize(rows)
    normed = (unit * gain_ref[0:1, :]).astype(BF)
    keys = jnp.concatenate([keys_ref[...], nn(normed, wk_ref[0]).astype(BF)], axis=0)
    queries_t = jnp.concatenate(
        [queries_ref[...], nt(wq_ref[0].T, normed).astype(BF)], axis=1
    )
    values_t = jnp.concatenate([values_ref[...], nt(wv_ref[0].T, normed).astype(BF)], axis=1)
    attend(keys, queries_t, values_t, ctx_ref)
    rows = jnp.concatenate([f_ref[HOP:, :].astype(F32), rows], axis=0)
    mids = (mid_in_ref[...], (rows + tn(ctx_ref[...], wo_ref[0])).astype(BF))
    grads = grad_ref[...]
    pick = select_rows(384, 384, packed_source)
    for t in range(4):
        middle = jnp.concatenate(
            [mids[g][h * HOP + 32 * t : h * HOP + 32 * t + 32] for g in range(2) for h in range(2)],
            axis=0,
        )
        cotangent = jnp.concatenate(
            [grads[h * HOP + 32 * t : h * HOP + 32 * t + 32] for h in range(2)], axis=0
        )
        part = jnp.concatenate(
            [middle[:, :128], middle[:, 128:], cotangent[:, :128], cotangent[:, 128:]], axis=0
        )
        packed_ref[384 * t : 384 * t + 384, :] = nn(pick, part).astype(BF)


def params():
    return pltpu.CompilerParams(vmem_limit_bytes=VMEM_LIMIT)


def cost(micros):
    return pl.CostEstimate(flops=int(micros * 400e6), bytes_accessed=1 << 20, transcendentals=0)


def bf16(*shape):
    return jax.ShapeDtypeStruct(shape, BF)


def f32(*shape):
    return jax.ShapeDtypeStruct(shape, F32)


def intra_first(frames, gains, wq, wk, wv, wo):
    return pl.pallas_call(
        intra_first_kernel,
        out_shape=(bf16(K, D), bf16(D, K), bf16(HOP, D), bf16(D, HOP), bf16(D, HOP)),
        compiler_params=params(),
        cost_estimate=cost(4),
        name="intra_first",
    )(frames, gains, wq, wk, wv, wo)


def intra_second(frames, following, grads, mid, keys, queries, values, gains, wq, wk, wv, wo):
    return pl.pallas_call(
        intra_second_kernel,
        out_shape=(bf16(64 * 24, 128), bf16(D, K)),
        compiler_params=params(),
        cost_estimate=cost(4),
        name="intra_second",
    )(frames, following, grads, mid, keys, queries, values, gains, wq, wk, wv, wo)


def inter_kernel(
    packed_ref, gain_ref, wq_ref, wk_ref, wv_ref, wo_ref,
    out_ref, normed_t_ref, grads_ref, ctx_t, gq_t, gk_ref, gv_ref,
):
    gain = gain_ref[1:2, :]
    pick = select_rows(384, 384, unpacked_source)
    tiles = [nn(pick, packed_ref[384 * t : 384 * t + 384, :]) for t in range(4)]
    rows = jnp.concatenate(
        [
            jnp.concatenate(
                [tiles[t][c * 128 + 32 * p : c * 128 + 32 * p + 32] for c in range(2)], axis=1
            )
            for p in range(4)
            for t in range(4)
        ],
        axis=0,
    )
    hops = [
        jnp.concatenate(
            [
                jnp.concatenate(
                    [tiles[t][256 + c * 64 + 32 * r : 256 + c * 64 + 32 * r + 32] for c in range(2)],
                    axis=1,
                )
                for t in range(4)
            ],
            axis=0,
        )
        for r in range(2)
    ]
    last = jnp.zeros((1, D), F32)
    late = [jnp.concatenate([hop[1:], last], axis=0) for hop in hops]
    grads = jnp.concatenate(hops + late, axis=0).astype(BF)
    grads_ref[...] = grads
    unit, inverse = standardize(rows)
    normed = (unit * gain).astype(BF)
    normed_t_ref[...] = normed.T
    wq, wk, wv, wo = wq_ref[1], wk_ref[1], wv_ref[1], wo_ref[1]
    queries = nn(normed, wq).astype(BF)
    keys = nn(normed, wk).astype(BF)
    values = nn(normed, wv).astype(BF)
    grad_context = nt(grads, wo).astype(BF)
    queries_t = queries.T
    keys_t = keys.T
    values_t = values.T
    grad_context_t = grad_context.T
    masks = head_masks()
    downs = row_masks()

    def place(step):
        p, b = step // 2, step % 2
        return slice(128 * p, 128 * p + 128), slice(128 * b, 128 * b + 128)

    def columns(rows_t):
        return jnp.concatenate([rows_t * down for down in downs], axis=1)

    def stacked(rows):
        return jnp.concatenate([rows * mask for mask in masks], axis=0)

    def products(step):
        at, block = place(step)
        scores = nn(keys[at, block], columns(queries_t[block, at]))
        grad_probs = nn(values[at, block], columns(grad_context_t[block, at]))
        return scores, grad_probs

    def weigh(step, held):
        scores, grad_probs = held
        probs = softmax_keys(scores)
        inner = jnp.sum(grad_probs * probs, axis=0, keepdims=True)
        return probs.astype(BF), (probs * (grad_probs - inner) * SCALE).astype(BF)

    def collect(step, held):
        low, grad_scores = held
        at, block = place(step)
        gv_ref[at, block] = nn(low, stacked(grad_context[at, block])).astype(BF)
        gk_ref[at, block] = nn(grad_scores, stacked(queries[at, block])).astype(BF)
        for i in range(4):
            feats = slice(block.start + HEAD * i, block.start + HEAD * i + HEAD)
            cols = slice(128 * i, 128 * i + 128)
            ctx_t[feats, at] = nn(values_t[feats, at], low[:, cols]).astype(BF)
            gq_t[feats, at] = nn(keys_t[feats, at], grad_scores[:, cols]).astype(BF)

    staged(8, products, weigh, collect)
    gqt, gk, gv = gq_t[...], gk_ref[...], gv_ref[...]
    grad_normed = nt(gqt.T, wq) + nt(gk, wk) + nt(gv, wv)
    result = (grads.astype(F32) + norm_pullback(grad_normed, unit, inverse, gain)).astype(BF)
    back = select_rows(256, 256, segment_target)
    for t in range(2):
        part = jnp.concatenate(
            [result[128 * p + 64 * t : 128 * p + 64 * t + 64] for p in range(4)], axis=0
        )
        out_ref[256 * t : 256 * t + 256, :] = nn(back, part).astype(BF)


def inter(packed, gains, wq, wk, wv, wo):
    return pl.pallas_call(
        inter_kernel,
        out_shape=(
            bf16(512, D), bf16(D, 512), bf16(512, D), bf16(D, 512), bf16(D, 512), bf16(512, D),
            bf16(512, D),
        ),
        compiler_params=params(),
        cost_estimate=cost(9),
        name="inter",
    )(packed, gains, wq, wk, wv, wo)


def split_by_core(core_ref, weights, keep_ref, send_ref):
    low_core = core_ref[0] == 0
    for i in range(2):
        keep_ref[i] = jnp.where(low_core, weights[i], weights[2 + i])
        send_ref[i] = jnp.where(low_core, weights[2 + i], weights[i]).astype(BF)


def inter_weights_kernel(
    core_ref, normed_t_ref, grads_ref, ctx_t_ref, gq_t_ref, gk_ref, gv_ref, keep_ref, send_ref
):
    normed_t = normed_t_ref[...]
    weights = (
        nt(normed_t, gq_t_ref[...]),
        nn(normed_t, gk_ref[...]),
        nn(normed_t, gv_ref[...]),
        nn(ctx_t_ref[...], grads_ref[...]),
    )
    split_by_core(core_ref, weights, keep_ref, send_ref)


def specs(count):
    vmem = pl.BlockSpec(memory_space=pltpu.VMEM)
    return [pl.BlockSpec(memory_space=pltpu.SMEM)] + [vmem] * count


def inter_weights(core, *operands):
    return pl.pallas_call(
        inter_weights_kernel,
        in_specs=specs(6),
        out_shape=(f32(2, D, D), bf16(2, D, D)),
        compiler_params=params(),
        cost_estimate=cost(1),
        name="inter_weights",
    )(core, *operands)


def intra_prepare_kernel(
    f_ref, n_ref, gain_ref, wq_ref, wk_ref, wv_ref,
    normed_t_ref, queries_ref, keys_t_ref, values_ref, probs_ref,
):
    rows = jnp.concatenate([f_ref[...], n_ref[...]], axis=0).astype(F32)
    unit, _ = standardize(rows)
    normed = (unit * gain_ref[0:1, :]).astype(BF)
    normed_t_ref[...] = normed.T
    queries = nn(normed, wq_ref[0]).astype(BF)
    keys = nn(normed, wk_ref[0]).astype(BF)
    queries_ref[...] = queries
    values_ref[...] = nn(normed, wv_ref[0]).astype(BF)
    queries_t = queries.T
    keys_t_ref[...] = keys.T
    masks = head_masks()

    def scores_of(step):
        g, h = step // HEADS, step % HEADS
        at = slice(g * HOP, g * HOP + K)
        block = slice((h // 4) * 128, (h // 4) * 128 + 128)
        return nn(keys[at, block] * masks[h % 4], queries_t[block, at])

    def weigh(step, scores):
        probs_ref[step] = softmax_keys(scores)

    staged(2 * HEADS, scores_of, weigh)


def intra_prepare(frames, following, gains, wq, wk, wv):
    return pl.pallas_call(
        intra_prepare_kernel,
        out_shape=(
            bf16(D, 3 * HOP), bf16(3 * HOP, D), bf16(D, 3 * HOP), bf16(3 * HOP, D),
            f32(2 * HEADS, K, K),
        ),
        compiler_params=params(),
        cost_estimate=cost(4),
        name="intra_prepare",
    )(frames, following, gains, wq, wk, wv)


def intra_backward_kernel(
    core_ref, m_ref, ctx_a_ref, ctx_b_ref, normed_t_ref, queries_ref, keys_t_ref, values_ref,
    probs_ref, wo_ref,
    keep_ref, send_ref, grads_ref, gq_t, gk_ref, gv_ref,
):
    pick = select_rows(256, 256, owner_target)
    tiles = [nn(pick, m_ref[256 * t : 256 * t + 256, :]).astype(BF) for t in range(2)]
    masks = head_masks()
    context, context_t = [], []
    for g in range(2):
        grads_ref[g] = jnp.concatenate(
            [tiles[t][128 * g + 64 * h : 128 * g + 64 * h + 64] for h in range(2) for t in range(2)],
            axis=0,
        )
        context.append(nt(grads_ref[g], wo_ref[0]).astype(BF))
        context_t.append(context[g].T)

    def place(step):
        g, h = step // HEADS, step % HEADS
        return g, slice(g * HOP, g * HOP + K), h // 4, h % 4

    def products(step):
        g, at, b, i = place(step)
        block = slice(128 * b, 128 * b + 128)
        return nn(values_ref[at, block] * masks[i], context_t[g][block, :])

    def weigh(step, grad_probs):
        probs = probs_ref[step]
        inner = jnp.sum(grad_probs * probs, axis=0, keepdims=True)
        return probs.astype(BF), (probs * (grad_probs - inner) * SCALE).astype(BF)

    sums = {}

    def collect(step, held):
        low, grad_scores = held
        g, at, b, i = place(step)
        block = slice(128 * b, 128 * b + 128)
        feats = slice(128 * b + HEAD * i, 128 * b + HEAD * i + HEAD)
        gv = nn(low, context[g][:, block] * masks[i])
        gk = nn(grad_scores, queries_ref[at, block] * masks[i])
        gq_t[g, feats, :] = nn(keys_t_ref[feats, at], grad_scores).astype(BF)
        sums["v"] = gv if i == 0 else sums["v"] + gv
        sums["k"] = gk if i == 0 else sums["k"] + gk
        if i == 3:
            gv_ref[g, :, block] = sums["v"].astype(BF)
            gk_ref[g, :, block] = sums["k"].astype(BF)

    staged(2 * HEADS, products, weigh, collect)
    contexts = (ctx_a_ref, ctx_b_ref)
    parts = [
        (
            nt(normed_t_ref[:, g * HOP : g * HOP + K], gq_t[g]),
            nn(normed_t_ref[:, g * HOP : g * HOP + K], gk_ref[g]),
            nn(normed_t_ref[:, g * HOP : g * HOP + K], gv_ref[g]),
            nn(contexts[g][...], grads_ref[g]),
        )
        for g in range(2)
    ]
    totals = [first + second for first, second in zip(*parts)]
    split_by_core(core_ref, totals, keep_ref, send_ref)


def intra_backward(core, grads, ctx_a, ctx_b, *rest):
    return pl.pallas_call(
        intra_backward_kernel,
        in_specs=specs(9),
        out_shape=(
            f32(2, D, D), bf16(2, D, D), bf16(2, K, D), bf16(2, D, K), bf16(2, K, D), bf16(2, K, D),
        ),
        compiler_params=params(),
        cost_estimate=cost(6),
        name="intra_backward",
    )(core, grads, ctx_a, ctx_b, *rest)


def intra_tail_kernel(
    grads_ref, gq_t_ref, gk_ref, gv_ref, f_ref, n_ref, gain_ref, wq_ref, wk_ref, wv_ref,
    first_ref, second_ref, carry_ref,
):
    rows = jnp.concatenate([f_ref[...], n_ref[...]], axis=0).astype(F32)
    unit, inverse = standardize(rows)
    halves = []
    for g in range(2):
        at = slice(g * HOP, g * HOP + K)
        grad_normed = (
            nt(gq_t_ref[g].T, wq_ref[0]) + nt(gk_ref[g], wk_ref[0]) + nt(gv_ref[g], wv_ref[0])
        )
        pulled = norm_pullback(grad_normed, unit[at], inverse[at], gain_ref[0:1, :])
        result = (grads_ref[g].astype(F32) + pulled).astype(BF)
        halves.append((result[:HOP], result[HOP:]))
    first_ref[...] = halves[0][0]
    second_ref[...] = (halves[1][0].astype(F32) + halves[0][1].astype(F32)).astype(BF)
    carry_ref[...] = halves[1][1]


def intra_tail(*operands):
    return pl.pallas_call(
        intra_tail_kernel,
        out_shape=(bf16(HOP, D), bf16(HOP, D), bf16(HOP, D)),
        compiler_params=params(),
        cost_estimate=cost(2),
        name="intra_tail",
    )(*operands)


def finish_kernel(
    core_ref, mine_ref, other_ref, first_ref, second_ref, carried_ref, gain_ref, wq_ref, wk_ref, wv_ref,
    frames_ref, dq_ref, dk_ref, dv_ref, do_ref, dg_ref,
):
    frames_ref[:HOP] = (first_ref[...].astype(F32) + carried_ref[...].astype(F32)).astype(BF)
    frames_ref[HOP:] = second_ref[...]
    low_core = core_ref[0] == 0
    for layer in range(2):
        mine = mine_ref[:, layer].reshape(2, D, D).astype(F32)
        other = other_ref[:, layer].reshape(2, D, D).astype(F32)
        dq = jnp.where(low_core, mine[0], other[0])
        dk = jnp.where(low_core, mine[1], other[1])
        dv = jnp.where(low_core, other[0], mine[0])
        dq_ref[layer] = dq
        dk_ref[layer] = dk
        dv_ref[layer] = dv
        do_ref[layer] = jnp.where(low_core, other[1], mine[1])
        through = (
            dq * wq_ref[layer].astype(F32)
            + dk * wk_ref[layer].astype(F32)
            + dv * wv_ref[layer].astype(F32)
        )
        column = jnp.sum(through.T, axis=0, keepdims=True)
        dg_ref[layer : layer + 1, :] = column / gain_ref[layer : layer + 1, :]


def finish(core, mine, other, first, second, carried, gains, wq, wk, wv):
    full = f32(2, D, D)
    return pl.pallas_call(
        finish_kernel,
        in_specs=specs(9),
        out_shape=(bf16(K, D), full, full, full, full, f32(2, D)),
        compiler_params=params(),
        cost_estimate=cost(2),
        name="finish",
    )(core, mine, other, first, second, carried, gains, wq, wk, wv)


def shifted(shard, by):
    length = lax.axis_size(TM)
    pairs = [(i, i + by) for i in range(length) if 0 <= i + by < length]
    return lax.ppermute(shard, TM, pairs)


def exchanged(shard, axes):
    return lax.all_to_all(shard, axes, split_axis=0, concat_axis=0, tiled=True)


def swapped(shard):
    return lax.ppermute(shard, "core", [(0, 1), (1, 0)])


def copies(piece, count):
    return jnp.broadcast_to(piece[None], (count,) + piece.shape)


def summed(pieces):
    return jnp.sum(pieces.astype(F32), axis=0).astype(BF)


def core_sum(keep, send):
    return (keep + swapped(send).astype(F32)).astype(BF).reshape(16, 32, D)


def shards(frames, frames_grad, wq, wk, wv, wo, gains):
    frames = frames[0]
    core = lax.axis_index("core").astype(jnp.int32).reshape(1)
    following = shifted(frames[:HOP], -1)
    mid, ctx_a, *front = intra_first(frames, gains, wq, wk, wv, wo)
    packed, ctx_b = intra_second(
        frames, following, frames_grad[0], mid, *front, gains, wq, wk, wv, wo
    )
    across = exchanged(packed.reshape(64, 24, 128), TM).reshape(64 * 24, 128)
    grad_middle, *operands = inter(across, gains, wq, wk, wv, wo)
    grad_local = exchanged(grad_middle.reshape(64, 8, D), TM).reshape(512, D)
    inter_half = core_sum(*inter_weights(core, *operands))
    prepared = intra_prepare(frames, following, gains, wq, wk, wv)
    keep, send, *rest = intra_backward(core, grad_local, ctx_a, ctx_b, *prepared, wo)
    half = jnp.concatenate([core_sum(keep, send), inter_half], axis=1)
    first, second, carry = intra_tail(*rest, frames, following, gains, wq, wk, wv)
    carried = shifted(carry, 1)
    pieces = exchanged(half, PLANE)
    piece = summed(pieces)
    pieces = exchanged(copies(piece, 8), "z")
    pieces, carried = lax.optimization_barrier((pieces, carried))
    piece = summed(pieces)
    whole = exchanged(copies(piece, 16), PLANE).reshape(16, 2, 32, D)
    other = swapped(whole)
    grad_frames, *weights = finish(
        core, whole, other, first, second, carried, gains, wq, wk, wv
    )
    return (grad_frames[None], *weights)


def solution(mesh):
    split = Mesh(mesh.devices.reshape(2, 2, 2, 4, 8), AXES)
    placed = (P(DP, TM, None), P(DP, TM, None), P(), P(), P(), P(), P())
    return jax.shard_map(
        shards,
        mesh=split,
        in_specs=placed,
        out_specs=(P(DP, TM, None), P(), P(), P(), P(), P()),
        check_vma=False,
    )
```

time: 145 us -> 129 us (0.89)
  the two profiles are of different devices: /device:TPU:8 before, /device:TPU:1 now
where the time goes in v2:
time: 129 us; the launch traced here: 128 us
  blocking collectives  56.8 us (44%)
  starting transfers between devices  24.4 us (19%)
  Pallas kernels  18.5 us (14%)
  local copies, waits for them, and re-layouts  17.7 us (14%)
  waiting for transfers between devices  8.91 us (7%)
    all_to_all x3, blocking collectives, exchanged(): return lax.all_to_all(shard, axes, split_axis=0, concat_axis=0, tiled=True)  56.8 us
    unnamed x52, local copies, waits for them, and re-layouts  16.1 us
    ppermute x3, starting transfers between devices, swapped(): return lax.ppermute(shard, 'core', [(0, 1), (1, 0)])  10.4 us
    all_to_all x2, starting transfers between devices, exchanged(): return lax.all_to_all(shard, axes, split_axis=0, concat_axis=0, tiled=True)  9.43 us
    pallas_call x1, Pallas kernels, inter(): pl.pallas_call(inter_kernel, out_shape=(bf16(512, D), bf16(D, 512), bf16(...  4.95 us
    ppermute x2, starting transfers between devices, shifted(): return lax.ppermute(shard, TM, pairs)  4.54 us
    all_to_all x2, waiting for transfers between devices, exchanged(): return lax.all_to_all(shard, axes, split_axis=0, concat_axis=0, tiled=True)  4.38 us
    pallas_call x1, Pallas kernels, intra_backward(): pl.pallas_call(intra_backward_kernel, in_specs=specs(9), out_shape=(f32(2...  3.48 us
  transfers between devices with their start and end apart: 7, of which 5 were waited for; matrix products, arithmetic and copies ran while one was open for 1% of the time, Pallas kernels for 7%

profile of v2, /device:TPU:1, one launch (start us, length us, event | category | flops | bytes accessed | tf_op | source)
XLA Modules:
  0.0 128.5 jit_solution(5934664021324444994)
XLA Ops:
  0.6 0.9 slice_bitcast_fusion
  1.5 1.3 collective-permute-start
  2.8 0.0 copy-start
  2.8 0.9 copy-done
  3.7 0.9 copy-done.2
  4.7 0.9 copy-done.4
  5.6 0.9 copy-done.6
  6.6 0.9 copy-done.8
  7.5 0.7 copy-done.14
  8.2 1.8 %intra_first.1 = (bf16[256,256]{1,0:T(8,128)(2,1)S(1)}, bf16[256,256]{1,0:T(8,128)(2,1)S(1)}, bf16[128,256]{1,0:T(8,128)(2,1)S(1)}, bf16[256,128]{1,0:T(8,128)(2,1)S(1)}, bf16[256,128]{1,0:T(8,128)(2,1)S(1)}) custom-call(bf16[256,256]{1,0:T(8,128)(2,1)S(1)} %bitcast.18, f32[2,256]{1,0:T(2,128)S(1)} %copy-done.14, bf16[2,256,256]{2,1,0:T(8,128)(2,1)S(1)} %copy-done.4, ...), custom_call_target="tpu_custom_call" | custom-call | flops 1600000000 | bytes 1048576 | tf_op jit(solution)/shard_map/intra_first/pallas_call | solution.py:202
  10.0 0.0 copy-start.22
  10.1 0.6 copy-done.22
  10.7 2.9 %intra_second.1 = (bf16[1536,128]{1,0:T(8,128)(2,1)S(1)}, bf16[256,256]{1,0:T(8,128)(2,1)S(1)}) custom-call(bf16[256,256]{1,0:T(8,128)(2,1)S(1)} %bitcast.19, bf16[128,256]{1,0:T(8,128)(2,1)S(1)} %collective-permute-done.n_ref, bf16[256,256]{1,0:T(8,128)(2,1)S(1)} %bitcast.22, bf16[256,256]{1,0:T(8,128)(2,1)S(1)} %get-tuple-element.44.mid_in_ref, ...), custom_call_target="tpu_custom_call" | custom-call | flops 1600000000 | bytes 1048576 | tf_op jit(solution)/shard_map/intra_second/pallas_call | solution.py:212
  13.7 28.0 %all_to_all.25 = bf16[64,24,128]{2,1,0:T(8,128)(2,1)S(1)} all-to-all(bf16[64,24,128]{2,1,0:T(8,128)(2,1)S(1)} %bitcast.16), channel_id=1, replica_groups=mesh['yh'=2,'core'=2,'yl'=2,'x'=4,'z'=8] {'yl','x','z'}, dimensions={0} | all-to-all | bytes 786432 | tf_op jit(solution)/shard_map/all_to_all | solution.py:555
  41.7 0.0 copy-start.1
  41.7 0.0 copy-start.9
  41.7 5.0 %inter.1 = (bf16[512,256]{1,0:T(8,128)(2,1)}, bf16[256,512]{1,0:T(8,128)(2,1)S(1)}, bf16[512,256]{1,0:T(8,128)(2,1)S(1)}, bf16[256,512]{1,0:T(8,128)(2,1)S(1)}, ...) custom-call(bf16[1536,128]{1,0:T(8,128)(2,1)S(1)} %bitcast.15, ...), custom_call_target="tpu_custom_call" | custom-call | flops 3600000000 | bytes 1048576 | tf_op jit(solution)/shard_map/inter/pallas_call | solution.py:316
  46.6 6.0 %all-to-all-start.1 = ((bf16[64,8,256]{2,1,0:T(8,128)(2,1)}), bf16[64,8,256]{2,1,0:T(8,128)(2,1)S(1)}, u32[]{:S(2)}, u32[]{:S(2)}) async-start(bf16[64,8,256]{2,1,0:T(8,128)(2,1)} %bitcast.6), calls=%async_computation.1 | async-start | bytes 524288 | tf_op jit(solution)/shard_map/all_to_all | solution.py:555
  52.7 1.2 inter_weights.1
  53.8 2.1 %collective-permute-start.2 = (bf16[2,256,256]{2,1,0:T(8,128)(2,1)}, bf16[2,256,256]{2,1,0:T(8,128)(2,1)}, u32[]{:S(2)}, u32[]{:S(2)}) collective-permute-start(bf16[2,256,256]{2,1,0:T(8,128)(2,1)} %get-tuple-element.66), channel_id=1, source_target_pairs={{0,64},{64,0},{1,65},{65,1},{2,66},{66,2},{3,67},{67,3},{4,68},{68... | collective-permute-start | bytes 786440 | tf_op jit(solution)/shard_map/ppermute | solution.py:559
  55.9 0.8 copy-done.12
  56.8 1.9 %intra_prepare.1 = (bf16[256,384]{1,0:T(8,128)(2,1)S(1)}, bf16[384,256]{1,0:T(8,128)(2,1)S(1)}, bf16[256,384]{1,0:T(8,128)(2,1)S(1)}, bf16[384,256]{1,0:T(8,128)(2,1)S(1)}, f32[16,256,256]{2,1,0:T(8,128)S(1)}) custom-call(bf16[256,256]{1,0:T(8,128)(2,1)S(1)} %bitcast.20, bf16[128,256]{1,0:T(8,128)(2,1)S(1)} %copy-done.12, f32[2,256]{1,0:T(2,128)S(1)} %copy-done.15, ...), custom_call_target="tpu_custom_call" | custom-call | flops 1600000000 | bytes 1048576 | tf_op jit(solution)/shard_map/intra_prepare/pallas_call | solution.py:393
  58.7 2.0 %copy-done.16 = f32[16,256,256]{2,1,0:T(8,128)} copy-done((f32[16,256,256]{2,1,0:T(8,128)}, f32[16,256,256]{2,1,0:T(8,128)S(1)}, u32[]{:S(2)}) %copy-start.16) | copy-done | bytes 4194328
  60.7 0.7 copy-done.18
  61.3 0.7 copy-done.20
  62.0 1.6 %all-to-all-done.1 = bf16[64,8,256]{2,1,0:T(8,128)(2,1)S(1)} async-done(((bf16[64,8,256]{2,1,0:T(8,128)(2,1)}), bf16[64,8,256]{2,1,0:T(8,128)(2,1)S(1)}, u32[]{:S(2)}, u32[]{:S(2)}) %all-to-all-start.1) | async-done | bytes 262176 | tf_op jit(solution)/shard_map/all_to_all | solution.py:555
  63.7 2.2 %copy-done.17 = f32[16,256,256]{2,1,0:T(8,128)S(1)} copy-done((f32[16,256,256]{2,1,0:T(8,128)S(1)}, f32[16,256,256]{2,1,0:T(8,128)}, u32[]{:S(2)}) %copy-start.17) | copy-done | bytes 4194328
  65.9 0.9 copy-done.19
  66.8 0.9 copy-done.21
  67.7 0.9 copy-done.23
  68.6 0.9 copy-done.25
  69.5 3.5 %intra_backward.1 = (f32[2,256,256]{2,1,0:T(8,128)S(1)}, bf16[2,256,256]{2,1,0:T(8,128)(2,1)S(1)}, bf16[2,256,256]{2,1,0:T(8,128)(2,1)S(1)}, bf16[2,256,256]{2,1...) custom-call(s32[1]{0:T(128)} %bitcast.core_ref, bf16[512,256]{1,0:T(8,128)(2,1)S(1)} %bitcast.17, ...), custom_call_target="tpu_custom_call" | custom-call | flops 2400000000 | bytes 1048576 | tf_op jit(solution)/shard_map/intra_backward/pallas_call | solution.py:468
  73.0 3.7 %collective-permute-start.1 = (bf16[2,256,256]{2,1,0:T(8,128)(2,1)S(1)}, bf16[2,256,256]{2,1,0:T(8,128)(2,1)S(1)}, u32[]{:S(2)}, u32[]{:S(2)}) collective-permute-start(bf16[2,256,256]{2,1,0:T(8,128)(2,1)S(1)} %get-tuple-element.58), channel_id=1, source_target_pairs={{0,64},{64,0},{1,65},{65,1},{2,66},{66,2},{3,67},{67,3},{4,68},{68... | collective-permute-start | bytes 786440 | tf_op jit(solution)/shard_map/ppermute | solution.py:559
  76.8 1.0 add_convert_fusion
  77.8 0.1 collective-permute-done.1
  77.9 0.1 add_convert_fusion.1
  78.0 15.8 %all_to_all.26 = bf16[16,64,256]{2,1,0:T(8,128)(2,1)S(1)} all-to-all(bf16[16,64,256]{2,1,0:T(8,128)(2,1)S(1)} %pad_maximum_fusion), channel_id=1, replica_groups=mesh['yh'=2,'core'=2,'yl'=2,'x'=4,'z'=8] {'yh','yl','x'}, dimensions={0} | all-to-all | bytes 1048576 | tf_op jit(solution)/shard_map/all_to_all | solution.py:555
  93.8 0.1 reduce_sum.24
  93.9 0.7 broadcast_in_dim.6
  94.6 3.4 %all-to-all-start.3 = ((bf16[8,64,256]{2,1,0:T(8,128)(2,1)}), bf16[8,64,256]{2,1,0:T(8,128)(2,1)S(1)}, u32[]{:S(2)}, u32[]{:S(2)}) async-start(bf16[8,64,256]{2,1,0:T(8,128)(2,1)} %broadcast_in_dim.6), calls=%async_computation.3 | async-start | bytes 524288 | tf_op jit(solution)/shard_map/all_to_all | solution.py:555
  98.1 0.6 intra_tail.1
  98.7 3.3 %collective-permute-start.3 = (bf16[128,256]{1,0:T(8,128)(2,1)S(1)}, bf16[128,256]{1,0:T(8,128)(2,1)S(1)}, u32[]{:S(2)}, u32[]{:S(2)}) collective-permute-start(bf16[128,256]{1,0:T(8,128)(2,1)S(1)} %get-tuple-element.71), channel_id=1, source_target_pairs={{0,1},{1,2},{2,3},{3,4},{4,5},{5,6},{6,7},{7,8},{8,9},{9,10},{10,1... | collective-permute-start | bytes 196616 | tf_op jit(solution)/shard_map/ppermute | solution.py:551
  101.9 2.8 %collective-permute-done.3.carried_ref = bf16[128,256]{1,0:T(8,128)(2,1)S(1)} collective-permute-done((bf16[128,256]{1,0:T(8,128)(2,1)S(1)}, bf16[128,256]{1,0:T(8,128)(2,1)S(1)}, u32[]{:S(2)}, u32[]{:S(2)}) %collective-permute-start.3) | collective-permute-done | bytes 65568 | tf_op jit(solution)/shard_map/ppermute | solution.py:551
  104.8 2.7 %all-to-all-done.3 = bf16[8,64,256]{2,1,0:T(8,128)(2,1)S(1)} async-done(((bf16[8,64,256]{2,1,0:T(8,128)(2,1)}), bf16[8,64,256]{2,1,0:T(8,128)(2,1)S(1)}, u32[]{:S(2)}, u32[]{:S(2)}) %all-to-all-start.3) | async-done | bytes 262176 | tf_op jit(solution)/shard_map/all_to_all | solution.py:555
  107.6 13.1 %all_to_all.27 = bf16[16,64,256]{2,1,0:T(8,128)(2,1)S(1)} all-to-all(bf16[16,64,256]{2,1,0:T(8,128)(2,1)S(1)} %broadcast_in_dim.7), channel_id=1, replica_groups=mesh['yh'=2,'core'=2,'yl'=2,'x'=4,'z'=8] {'yh','yl','x'}, dimensions={0} | all-to-all | bytes 1048576 | tf_op jit(solution)/shard_map/all_to_all | solution.py:555
  120.7 4.6 %collective-permute-start.4 = (bf16[16,2,32,256]{3,2,1,0:T(8,128)(2,1)S(1)}, bf16[16,2,32,256]{3,2,1,0:T(8,128)(2,1)S(1)}, u32[]{:S(2)}, u32[]{:S(2)}) collective-permute-start(bf16[16,2,32,256]{3,2,1,0:T(8,128)(2,1)S(1)} %bitcast.13), channel_id=1, source_target_pairs={{0,64},{64,0},{1,65},{65,1},{2,66},{66,2},{3,67},{67,3},{4,68},{68... | collective-permute-start | bytes 1572872 | tf_op jit(solution)/shard_map/ppermute | solution.py:559
  125.3 1.5 %collective-permute-done.4.other_ref = bf16[16,2,32,256]{3,2,1,0:T(8,128)(2,1)S(1)} collective-permute-done((bf16[16,2,32,256]{3,2,1,0:T(8,128)(2,1)S(1)}, bf16[16,2,32,256]{3,2,1,0:T(8,128)(2,1)S(1)}, u32[]{:S(2)}, u32[]{:S(2)}) %collective-permute-start.4) | collective-permute-done | bytes 524320 | tf_op jit(solution)/shard_map/ppermute | solution.py:559
  126.8 1.6 %finish.1 = (bf16[256,256]{1,0:T(8,128)(2,1)}, f32[2,256,256]{2,1,0:T(8,128)}, f32[2,256,256]{2,1,0:T(8,128)}, f32[2,256,256]{2,1,0:T(8,128)}, f32[2,256,256]{2,1,0:T(8,128)}, /*index=5*/f32[2,256]{1,0:T(2,128)}) custom-call(s32[1]{0:T(128)} %bitcast.core_ref, bf16[16,2,32,256]{3,2,1,0:T(8,128)(2,1)S(1)} %bitcast.14, ...), custom_call_target="tpu_custom_call" | custom-call | flops 800000000 | bytes 1048576 | tf_op jit(solution)/shard_map/finish/pallas_call | solution.py:538
  (37 shorter events, 0.2 us)
Async XLA Ops:
  0.6 10.1 %copy-start.10 = (bf16[1,256,256]{2,1,0:T(8,128)(2,1)S(1)}, bf16[1,256,256]{2,1,0:T(8,128)(2,1)}, u32[]{:S(2)}) copy-start(bf16[1,256,256]{2,1,0:T(8,128)(2,1)} %param.8) | copy-start | bytes 393220
  1.5 9.2 %collective-permute-start = (bf16[128,256]{1,0:T(8,128)(2,1)S(1)}, bf16[128,256]{1,0:T(8,128)(2,1)S(1)}, u32[]{:S(2)}, u32[]{:S(2)}) collective-permute-start(bf16[128,256]{1,0:T(8,128)(2,1)S(1)} %slice_bitcast_fusion), channel_id=1, source_target_pairs={{1,0},{2,1},{3,2},{4,3},{5,4},{6,5},{7,6},{8,7},{9,8},{10,9},{11,1... | collective-permute-start | bytes 196616 | tf_op jit(solution)/shard_map/ppermute | solution.py:551
  2.8 0.9 copy-start
  3.7 0.9 copy-start.2
  4.7 0.9 copy-start.4
  5.6 0.9 copy-start.6
  6.6 0.9 copy-start.8
  7.5 0.7 copy-start.14
  10.0 0.7 copy-start.22
  10.7 30.9 %copy-start.3 = (bf16[2,256,256]{2,1,0:T(8,128)(2,1)S(1)}, bf16[2,256,256]{2,1,0:T(8,128)(2,1)}, u32[]{:S(2)}) copy-start(bf16[2,256,256]{2,1,0:T(8,128)(2,1)} %wo_ref.7) | copy-start | bytes 786436
  10.7 30.9 %copy-start.5 = (bf16[2,256,256]{2,1,0:T(8,128)(2,1)S(1)}, bf16[2,256,256]{2,1,0:T(8,128)(2,1)}, u32[]{:S(2)}) copy-start(bf16[2,256,256]{2,1,0:T(8,128)(2,1)} %wq_ref.11) | copy-start | bytes 786436
  10.7 30.9 %copy-start.7 = (bf16[2,256,256]{2,1,0:T(8,128)(2,1)S(1)}, bf16[2,256,256]{2,1,0:T(8,128)(2,1)}, u32[]{:S(2)}) copy-start(bf16[2,256,256]{2,1,0:T(8,128)(2,1)} %wk_ref.11) | copy-start | bytes 786436
  10.7 30.9 %copy-start.11 = (bf16[128,256]{1,0:T(8,128)(2,1)}, bf16[128,256]{1,0:T(8,128)(2,1)S(1)}, u32[]{:S(2)}) copy-start(bf16[128,256]{1,0:T(8,128)(2,1)S(1)} %collective-permute-done.n_ref) | copy-start | bytes 196612
  13.7 28.0 %copy-start.24 = (bf16[256,256]{1,0:T(8,128)(2,1)}, bf16[256,256]{1,0:T(8,128)(2,1)S(1)}, u32[]{:S(2)}) copy-start(bf16[256,256]{1,0:T(8,128)(2,1)S(1)} %get-tuple-element.51.ctx_b_ref) | copy-start | bytes 393220
  41.7 14.3 %copy-start.1 = (bf16[1,256,256]{2,1,0:T(8,128)(2,1)S(1)}, bf16[1,256,256]{2,1,0:T(8,128)(2,1)}, u32[]{:S(2)}) copy-start(bf16[1,256,256]{2,1,0:T(8,128)(2,1)} %param.7) | copy-start | bytes 393220
  41.7 14.3 %copy-start.9 = (bf16[2,256,256]{2,1,0:T(8,128)(2,1)S(1)}, bf16[2,256,256]{2,1,0:T(8,128)(2,1)}, u32[]{:S(2)}) copy-start(bf16[2,256,256]{2,1,0:T(8,128)(2,1)} %wv_ref.11) | copy-start | bytes 786436
  41.7 14.3 %copy-start.15 = (f32[2,256]{1,0:T(2,128)S(1)}, f32[2,256]{1,0:T(2,128)}, u32[]{:S(2)}) copy-start(f32[2,256]{1,0:T(2,128)} %gain_ref.11) | copy-start | bytes 6148
  46.6 17.0 %all-to-all-start.1 = ((bf16[64,8,256]{2,1,0:T(8,128)(2,1)}), bf16[64,8,256]{2,1,0:T(8,128)(2,1)S(1)}, u32[]{:S(2)}, u32[]{:S(2)}) async-start(bf16[64,8,256]{2,1,0:T(8,128)(2,1)} %bitcast.6), calls=%async_computation.1 | async-start | bytes 524288 | tf_op jit(solution)/shard_map/all_to_all | solution.py:555
  53.8 22.9 %collective-permute-start.2 = (bf16[2,256,256]{2,1,0:T(8,128)(2,1)}, bf16[2,256,256]{2,1,0:T(8,128)(2,1)}, u32[]{:S(2)}, u32[]{:S(2)}) collective-permute-start(bf16[2,256,256]{2,1,0:T(8,128)(2,1)} %get-tuple-element.66), channel_id=1, source_target_pairs={{0,64},{64,0},{1,65},{65,1},{2,66},{66,2},{3,67},{67,3},{4,68},{68... | collective-permute-start | bytes 786440 | tf_op jit(solution)/shard_map/ppermute | solution.py:559
  55.9 0.8 copy-start.12
  58.7 2.0 %copy-start.16 = (f32[16,256,256]{2,1,0:T(8,128)}, f32[16,256,256]{2,1,0:T(8,128)S(1)}, u32[]{:S(2)}) copy-start(f32[16,256,256]{2,1,0:T(8,128)S(1)} %get-tuple-element.56.probs_ref) | copy-start | bytes 12582916
  60.7 0.7 copy-start.18
  61.3 0.7 copy-start.20
  63.7 2.2 %copy-start.17 = (f32[16,256,256]{2,1,0:T(8,128)S(1)}, f32[16,256,256]{2,1,0:T(8,128)}, u32[]{:S(2)}) copy-start(f32[16,256,256]{2,1,0:T(8,128)} %copy-done.16) | copy-start | bytes 12582916
  65.8 0.9 copy-start.19
  66.8 0.9 copy-start.21
  67.7 0.9 copy-start.23
  68.6 0.9 copy-start.25
  73.0 25.1 %copy-start.13 = (bf16[128,256]{1,0:T(8,128)(2,1)S(1)}, bf16[128,256]{1,0:T(8,128)(2,1)}, u32[]{:S(2)}) copy-start(bf16[128,256]{1,0:T(8,128)(2,1)} %copy-done.11) | copy-start | bytes 196612
  73.0 4.9 %collective-permute-start.1 = (bf16[2,256,256]{2,1,0:T(8,128)(2,1)S(1)}, bf16[2,256,256]{2,1,0:T(8,128)(2,1)S(1)}, u32[]{:S(2)}, u32[]{:S(2)}) collective-permute-start(bf16[2,256,256]{2,1,0:T(8,128)(2,1)S(1)} %get-tuple-element.58), channel_id=1, source_target_pairs={{0,64},{64,0},{1,65},{65,1},{2,66},{66,2},{3,67},{67,3},{4,68},{68... | collective-permute-start | bytes 786440 | tf_op jit(solution)/shard_map/ppermute | solution.py:559
  94.6 12.9 %all-to-all-start.3 = ((bf16[8,64,256]{2,1,0:T(8,128)(2,1)}), bf16[8,64,256]{2,1,0:T(8,128)(2,1)S(1)}, u32[]{:S(2)}, u32[]{:S(2)}) async-start(bf16[8,64,256]{2,1,0:T(8,128)(2,1)} %broadcast_in_dim.6), calls=%async_computation.3 | async-start | bytes 524288 | tf_op jit(solution)/shard_map/all_to_all | solution.py:555
  98.7 6.1 %collective-permute-start.3 = (bf16[128,256]{1,0:T(8,128)(2,1)S(1)}, bf16[128,256]{1,0:T(8,128)(2,1)S(1)}, u32[]{:S(2)}, u32[]{:S(2)}) collective-permute-start(bf16[128,256]{1,0:T(8,128)(2,1)S(1)} %get-tuple-element.71), channel_id=1, source_target_pairs={{0,1},{1,2},{2,3},{3,4},{4,5},{5,6},{6,7},{7,8},{8,9},{9,10},{10,1... | collective-permute-start | bytes 196616 | tf_op jit(solution)/shard_map/ppermute | solution.py:551
  120.7 6.1 %collective-permute-start.4 = (bf16[16,2,32,256]{3,2,1,0:T(8,128)(2,1)S(1)}, bf16[16,2,32,256]{3,2,1,0:T(8,128)(2,1)S(1)}, u32[]{:S(2)}, u32[]{:S(2)}) collective-permute-start(bf16[16,2,32,256]{3,2,1,0:T(8,128)(2,1)S(1)} %bitcast.13), channel_id=1, source_target_pairs={{0,64},{64,0},{1,65},{65,1},{2,66},{66,2},{3,67},{67,3},{4,68},{68... | collective-permute-start | bytes 1572872 | tf_op jit(solution)/shard_map/ppermute | solution.py:559

commit v3 on v2

--- a/solution.py
+++ b/solution.py
@@ -18,7 +18,10 @@
 LOG2E = math.log2(math.e)
 BF = jnp.bfloat16
 F32 = jnp.float32
-VMEM_LIMIT = 24 * 1024 * 1024
+VMEM_LIMIT = 16 * 1024 * 1024
+WHOLE_LIMIT = 62 * 1024 * 1024
+PREPARE_LIMIT = 56 * 1024 * 1024
+BACKWARD_LIMIT = 16 * 1024 * 1024
 
 AXES = ("yh", "core", "yl", "x", "z")
 DP = ("yh", "core")
@@ -135,37 +138,119 @@
     staged(HEADS, scores_of, weigh, collect)
 
 
+VMEM = pl.BlockSpec(memory_space=pltpu.VMEM)
+SMEM = pl.BlockSpec(memory_space=pltpu.SMEM)
+HBM = pl.BlockSpec(memory_space=pltpu.HBM)
+
+
+def begin(sems, *pairs):
+    copies = [pltpu.make_async_copy(src, dst, sems.at[i]) for i, (src, dst) in enumerate(pairs)]
+    for copy in copies:
+        copy.start()
+    return copies
+
+
+def settle(copies):
+    for copy in copies:
+        copy.wait()
+
+
+def bf16(*shape):
+    return jax.ShapeDtypeStruct(shape, BF)
+
+
+def f32(*shape):
+    return jax.ShapeDtypeStruct(shape, F32)
+
+
+def kernel_call(kernel, name, micros, in_specs, out_specs, out_shape, scratch, limit=VMEM_LIMIT):
+    return pl.pallas_call(
+        kernel,
+        in_specs=in_specs,
+        out_specs=out_specs,
+        out_shape=out_shape,
+        scratch_shapes=scratch,
+        compiler_params=pltpu.CompilerParams(vmem_limit_bytes=limit),
+        cost_estimate=pl.CostEstimate(
+            flops=int(micros * 400e6), bytes_accessed=1 << 20, transcendentals=0
+        ),
+        name=name,
+    )
+
+
+def dma(count):
+    return pltpu.SemaphoreType.DMA((count,))
+
+
+def vbf(*shape):
+    return pltpu.VMEM(shape, BF)
+
+
 def intra_first_kernel(
-    f_ref, gain_ref, wq_ref, wk_ref, wv_ref, wo_ref, mid_ref, ctx_ref, keys_ref, queries_ref, values_ref
+    f_any, gain_any, wq_any, wk_any, wv_any, wo_any,
+    mid_ref, keys_ref, queries_ref, values_ref,
+    w_ref, gain_ref, f_ref, ctx_ref, sems,
 ):
+    copies = begin(
+        sems,
+        (f_any, f_ref),
+        (gain_any, gain_ref),
+        (wk_any.at[0], w_ref.at[1]),
+        (wq_any.at[0], w_ref.at[0]),
+        (wv_any.at[0], w_ref.at[2]),
+        (wo_any.at[0], w_ref.at[3]),
+    )
+    copies[0].wait()
     rows = f_ref[...].astype(F32)
     unit, _ = standardize(rows)
+    copies[1].wait()
     normed = (unit * gain_ref[0:1, :]).astype(BF)
-    keys = nn(normed, wk_ref[0]).astype(BF)
-    queries_t = nt(wq_ref[0].T, normed).astype(BF)
-    values_t = nt(wv_ref[0].T, normed).astype(BF)
+    settle(copies[2:5])
+    keys = nn(normed, w_ref[1]).astype(BF)
+    queries_t = nt(w_ref[0].T, normed).astype(BF)
+    values_t = nt(w_ref[2].T, normed).astype(BF)
     attend(keys, queries_t, values_t, ctx_ref)
-    mid_ref[...] = (rows + tn(ctx_ref[...], wo_ref[0])).astype(BF)
+    copies[5].wait()
+    mid_ref[...] = (rows + tn(ctx_ref[...], w_ref[3])).astype(BF)
     keys_ref[...] = keys[HOP:]
     queries_ref[...] = queries_t[:, HOP:]
     values_ref[...] = values_t[:, HOP:]
 
 
 def intra_second_kernel(
-    f_ref, n_ref, grad_ref, mid_in_ref, keys_ref, queries_ref, values_ref,
-    gain_ref, wq_ref, wk_ref, wv_ref, wo_ref, packed_ref, ctx_ref,
+    n_any, f_any, grad_any, mid_any, keys_any, queries_any, values_any,
+    gain_any, wq_any, wk_any, wv_any, wo_any, packed_ref,
+    n_ref, f_ref, grad_ref, mid_in_ref, keys_ref, queries_ref, values_ref, gain_ref, w_ref, ctx_ref, sems,
 ):
+    copies = begin(
+        sems,
+        (n_any.at[pl.ds(0, HOP)], n_ref),
+        (gain_any, gain_ref),
+        (wk_any.at[0], w_ref.at[1]),
+        (wq_any.at[0], w_ref.at[0]),
+        (wv_any.at[0], w_ref.at[2]),
+        (keys_any, keys_ref),
+        (queries_any, queries_ref),
+        (values_any, values_ref),
+        (wo_any.at[0], w_ref.at[3]),
+        (mid_any, mid_in_ref),
+        (f_any.at[pl.ds(HOP, HOP)], f_ref),
+        (grad_any, grad_ref),
+    )
+    copies[0].wait()
     rows = n_ref[...].astype(F32)
     unit, _ = standardize(rows)
+    settle(copies[1:8])
     normed = (unit * gain_ref[0:1, :]).astype(BF)
-    keys = jnp.concatenate([keys_ref[...], nn(normed, wk_ref[0]).astype(BF)], axis=0)
+    keys = jnp.concatenate([keys_ref[...], nn(normed, w_ref[1]).astype(BF)], axis=0)
     queries_t = jnp.concatenate(
-        [queries_ref[...], nt(wq_ref[0].T, normed).astype(BF)], axis=1
-    )
-    values_t = jnp.concatenate([values_ref[...], nt(wv_ref[0].T, normed).astype(BF)], axis=1)
+        [queries_ref[...], nt(w_ref[0].T, normed).astype(BF)], axis=1
+    )
+    values_t = jnp.concatenate([values_ref[...], nt(w_ref[2].T, normed).astype(BF)], axis=1)
     attend(keys, queries_t, values_t, ctx_ref)
-    rows = jnp.concatenate([f_ref[HOP:, :].astype(F32), rows], axis=0)
-    mids = (mid_in_ref[...], (rows + tn(ctx_ref[...], wo_ref[0])).astype(BF))
+    settle(copies[8:])
+    rows = jnp.concatenate([f_ref[...].astype(F32), rows], axis=0)
+    mids = (mid_in_ref[...], (rows + tn(ctx_ref[...], w_ref[3])).astype(BF))
     grads = grad_ref[...]
     pick = select_rows(384, 384, packed_source)
     for t in range(4):
@@ -182,40 +267,24 @@
         packed_ref[384 * t : 384 * t + 384, :] = nn(pick, part).astype(BF)
 
 
-def params():
-    return pltpu.CompilerParams(vmem_limit_bytes=VMEM_LIMIT)
-
-
-def cost(micros):
-    return pl.CostEstimate(flops=int(micros * 400e6), bytes_accessed=1 << 20, transcendentals=0)
-
-
-def bf16(*shape):
-    return jax.ShapeDtypeStruct(shape, BF)
-
-
-def f32(*shape):
-    return jax.ShapeDtypeStruct(shape, F32)
-
-
 def intra_first(frames, gains, wq, wk, wv, wo):
-    return pl.pallas_call(
-        intra_first_kernel,
-        out_shape=(bf16(K, D), bf16(D, K), bf16(HOP, D), bf16(D, HOP), bf16(D, HOP)),
-        compiler_params=params(),
-        cost_estimate=cost(4),
-        name="intra_first",
+    return kernel_call(
+        intra_first_kernel, "intra_first", 3, [HBM] * 6, [VMEM] * 4,
+        (bf16(K, D), bf16(HOP, D), bf16(D, HOP), bf16(D, HOP)),
+        [vbf(4, D, D), pltpu.VMEM((2, D), F32), vbf(K, D), vbf(D, K), dma(6)],
+        WHOLE_LIMIT,
     )(frames, gains, wq, wk, wv, wo)
 
 
-def intra_second(frames, following, grads, mid, keys, queries, values, gains, wq, wk, wv, wo):
-    return pl.pallas_call(
-        intra_second_kernel,
-        out_shape=(bf16(64 * 24, 128), bf16(D, K)),
-        compiler_params=params(),
-        cost_estimate=cost(4),
-        name="intra_second",
-    )(frames, following, grads, mid, keys, queries, values, gains, wq, wk, wv, wo)
+def intra_second(following, frames, grads, *rest):
+    return kernel_call(
+        intra_second_kernel, "intra_second", 3, [HBM] * 12, VMEM, bf16(64 * 24, 128),
+        [
+            vbf(HOP, D), vbf(HOP, D), vbf(K, D), vbf(K, D), vbf(HOP, D), vbf(D, HOP), vbf(D, HOP),
+            pltpu.VMEM((2, D), F32), vbf(4, D, D), vbf(D, K), dma(12),
+        ],
+        WHOLE_LIMIT,
+    )(following, frames, grads, *rest)
 
 
 def inter_kernel(
@@ -313,15 +382,13 @@
 
 
 def inter(packed, gains, wq, wk, wv, wo):
-    return pl.pallas_call(
-        inter_kernel,
-        out_shape=(
+    return kernel_call(
+        inter_kernel, "inter", 5, [VMEM] * 6, [VMEM] * 7,
+        (
             bf16(512, D), bf16(D, 512), bf16(512, D), bf16(D, 512), bf16(D, 512), bf16(512, D),
             bf16(512, D),
         ),
-        compiler_params=params(),
-        cost_estimate=cost(9),
-        name="inter",
+        [],
     )(packed, gains, wq, wk, wv, wo)
 
 
@@ -345,36 +412,71 @@
     split_by_core(core_ref, weights, keep_ref, send_ref)
 
 
-def specs(count):
-    vmem = pl.BlockSpec(memory_space=pltpu.VMEM)
-    return [pl.BlockSpec(memory_space=pltpu.SMEM)] + [vmem] * count
-
-
 def inter_weights(core, *operands):
-    return pl.pallas_call(
-        inter_weights_kernel,
-        in_specs=specs(6),
-        out_shape=(f32(2, D, D), bf16(2, D, D)),
-        compiler_params=params(),
-        cost_estimate=cost(1),
-        name="inter_weights",
+    return kernel_call(
+        inter_weights_kernel, "inter_weights", 1, [SMEM] + [VMEM] * 6, [VMEM] * 2,
+        (f32(2, D, D), bf16(2, D, D)), [],
     )(core, *operands)
 
 
+NORMED_T, QUERIES, QUERIES_T, KEYS, KEYS_T, VALUES, CONTEXT = (768 * i for i in range(7))
+HANDED_ROWS = 768 * 6 + 1024
+
+
+def put_blocks(handed_ref, start, array):
+    for i in range(array.shape[1] // 128):
+        at = start + i * array.shape[0]
+        handed_ref[at : at + array.shape[0], :] = array[:, 128 * i : 128 * i + 128]
+
+
+def features_of(handed_ref, start, rows, at):
+    return jnp.concatenate(
+        [
+            handed_ref[start + 256 * i + rows.start : start + 256 * i + rows.stop, :]
+            for i in range(at.start // 128, at.stop // 128)
+        ],
+        axis=1,
+    )
+
+
+def tokens_of(handed_ref, start, at, b):
+    return handed_ref[start + 384 * b + at.start : start + 384 * b + at.stop, :]
+
+
+def begin_layer(sems, f_any, n_any, gain_any, wq_any, wk_any, wv_any, rows_ref, gain_ref, w_ref):
+    return begin(
+        sems,
+        (f_any, rows_ref.at[pl.ds(0, K)]),
+        (n_any.at[pl.ds(0, HOP)], rows_ref.at[pl.ds(K, HOP)]),
+        (gain_any, gain_ref),
+        (wq_any.at[0], w_ref.at[0]),
+        (wk_any.at[0], w_ref.at[1]),
+        (wv_any.at[0], w_ref.at[2]),
+    )
+
+
+def layer_scratch():
+    return [vbf(3 * HOP, D), pltpu.VMEM((2, D), F32), vbf(3, D, D)]
+
+
 def intra_prepare_kernel(
-    f_ref, n_ref, gain_ref, wq_ref, wk_ref, wv_ref,
-    normed_t_ref, queries_ref, keys_t_ref, values_ref, probs_ref,
+    f_any, n_any, gain_any, wq_any, wk_any, wv_any, handed_ref, stats_ref,
+    ctx_ref, rows_ref, gain_ref, w_ref, sems,
 ):
-    rows = jnp.concatenate([f_ref[...], n_ref[...]], axis=0).astype(F32)
-    unit, _ = standardize(rows)
+    settle(begin_layer(sems, f_any, n_any, gain_any, wq_any, wk_any, wv_any, rows_ref, gain_ref, w_ref))
+    unit, _ = standardize(rows_ref[...].astype(F32))
     normed = (unit * gain_ref[0:1, :]).astype(BF)
-    normed_t_ref[...] = normed.T
-    queries = nn(normed, wq_ref[0]).astype(BF)
-    keys = nn(normed, wk_ref[0]).astype(BF)
-    queries_ref[...] = queries
-    values_ref[...] = nn(normed, wv_ref[0]).astype(BF)
+    queries = nn(normed, w_ref[0]).astype(BF)
+    keys = nn(normed, w_ref[1]).astype(BF)
+    values = nn(normed, w_ref[2]).astype(BF)
     queries_t = queries.T
-    keys_t_ref[...] = keys.T
+    values_t = values.T
+    put_blocks(handed_ref, NORMED_T, normed.T)
+    put_blocks(handed_ref, QUERIES, queries)
+    put_blocks(handed_ref, QUERIES_T, queries_t)
+    put_blocks(handed_ref, KEYS, keys)
+    put_blocks(handed_ref, KEYS_T, keys.T)
+    put_blocks(handed_ref, VALUES, values)
     masks = head_masks()
 
     def scores_of(step):
@@ -384,29 +486,40 @@
         return nn(keys[at, block] * masks[h % 4], queries_t[block, at])
 
     def weigh(step, scores):
-        probs_ref[step] = softmax_keys(scores)
-
-    staged(2 * HEADS, scores_of, weigh)
+        highest = jnp.max(scores, axis=0, keepdims=True)
+        powers = jnp.exp2((scores - highest) * (SCALE * LOG2E))
+        inverse = 1.0 / jnp.sum(powers, axis=0, keepdims=True)
+        stats_ref[2 * step : 2 * step + 1, :] = highest
+        stats_ref[2 * step + 1 : 2 * step + 2, :] = inverse
+        return (powers * inverse).astype(BF)
+
+    def collect(step, low):
+        g, h = step // HEADS, step % HEADS
+        feats = slice(h * HEAD, h * HEAD + HEAD)
+        ctx_ref[g, feats, :] = nn(values_t[feats, g * HOP : g * HOP + K], low).astype(BF)
+
+    staged(2 * HEADS, scores_of, weigh, collect)
+    for g in range(2):
+        put_blocks(handed_ref, CONTEXT + 512 * g, ctx_ref[g])
 
 
 def intra_prepare(frames, following, gains, wq, wk, wv):
-    return pl.pallas_call(
-        intra_prepare_kernel,
-        out_shape=(
-            bf16(D, 3 * HOP), bf16(3 * HOP, D), bf16(D, 3 * HOP), bf16(3 * HOP, D),
-            f32(2 * HEADS, K, K),
-        ),
-        compiler_params=params(),
-        cost_estimate=cost(4),
-        name="intra_prepare",
+    return kernel_call(
+        intra_prepare_kernel, "intra_prepare", 3, [HBM] * 6, [VMEM] * 2,
+        (bf16(HANDED_ROWS, 128), f32(4 * HEADS, K)),
+        [vbf(2, D, K)] + layer_scratch() + [dma(6)],
+        PREPARE_LIMIT,
     )(frames, following, gains, wq, wk, wv)
 
 
 def intra_backward_kernel(
-    core_ref, m_ref, ctx_a_ref, ctx_b_ref, normed_t_ref, queries_ref, keys_t_ref, values_ref,
-    probs_ref, wo_ref,
+    core_ref, m_ref, handed_any, stats_any, wo_any,
     keep_ref, send_ref, grads_ref, gq_t, gk_ref, gv_ref,
+    handed_ref, stats_ref, wo_ref, sems,
 ):
+    copies = begin(
+        sems, (wo_any.at[0], wo_ref), (stats_any, stats_ref), (handed_any, handed_ref)
+    )
     pick = select_rows(256, 256, owner_target)
     tiles = [nn(pick, m_ref[256 * t : 256 * t + 256, :]).astype(BF) for t in range(2)]
     masks = head_masks()
@@ -416,8 +529,12 @@
             [tiles[t][128 * g + 64 * h : 128 * g + 64 * h + 64] for h in range(2) for t in range(2)],
             axis=0,
         )
-        context.append(nt(grads_ref[g], wo_ref[0]).astype(BF))
+        if g == 0:
+            copies[0].wait()
+        context.append(nt(grads_ref[g], wo_ref[...]).astype(BF))
         context_t.append(context[g].T)
+
+    settle(copies[1:])
 
     def place(step):
         g, h = step // HEADS, step % HEADS
@@ -426,10 +543,15 @@
     def products(step):
         g, at, b, i = place(step)
         block = slice(128 * b, 128 * b + 128)
-        return nn(values_ref[at, block] * masks[i], context_t[g][block, :])
-
-    def weigh(step, grad_probs):
-        probs = probs_ref[step]
+        keys = tokens_of(handed_ref, KEYS, at, b) * masks[i]
+        scores = nn(keys, features_of(handed_ref, QUERIES_T, block, at))
+        values = tokens_of(handed_ref, VALUES, at, b) * masks[i]
+        return scores, nn(values, context_t[g][block, :])
+
+    def weigh(step, held):
+        scores, grad_probs = held
+        powers = jnp.exp2((scores - stats_ref[2 * step : 2 * step + 1, :]) * (SCALE * LOG2E))
+        probs = powers * stats_ref[2 * step + 1 : 2 * step + 2, :]
         inner = jnp.sum(grad_probs * probs, axis=0, keepdims=True)
         return probs.astype(BF), (probs * (grad_probs - inner) * SCALE).astype(BF)
 
@@ -441,8 +563,9 @@
         block = slice(128 * b, 128 * b + 128)
         feats = slice(128 * b + HEAD * i, 128 * b + HEAD * i + HEAD)
         gv = nn(low, context[g][:, block] * masks[i])
-        gk = nn(grad_scores, queries_ref[at, block] * masks[i])
-        gq_t[g, feats, :] = nn(keys_t_ref[feats, at], grad_scores).astype(BF)
+        gk = nn(grad_scores, tokens_of(handed_ref, QUERIES, at, b) * masks[i])
+        keys_t = features_of(handed_ref, KEYS_T, feats, at)
+        gq_t[g, feats, :] = nn(keys_t, grad_scores).astype(BF)
         sums["v"] = gv if i == 0 else sums["v"] + gv
         sums["k"] = gk if i == 0 else sums["k"] + gk
         if i == 3:
@@ -450,44 +573,54 @@
             gk_ref[g, :, block] = sums["k"].astype(BF)
 
     staged(2 * HEADS, products, weigh, collect)
-    contexts = (ctx_a_ref, ctx_b_ref)
-    parts = [
-        (
-            nt(normed_t_ref[:, g * HOP : g * HOP + K], gq_t[g]),
-            nn(normed_t_ref[:, g * HOP : g * HOP + K], gk_ref[g]),
-            nn(normed_t_ref[:, g * HOP : g * HOP + K], gv_ref[g]),
-            nn(contexts[g][...], grads_ref[g]),
-        )
-        for g in range(2)
-    ]
+    parts = []
+    for g in range(2):
+        normed_t = features_of(
+            handed_ref, NORMED_T, slice(0, D), slice(g * HOP, g * HOP + K)
+        )
+        context_0 = jnp.concatenate(
+            [handed_ref[pl.ds(CONTEXT + 512 * g + 256 * i, 256), :] for i in range(2)], axis=1
+        )
+        parts.append(
+            (
+                nt(normed_t, gq_t[g]),
+                nn(normed_t, gk_ref[g]),
+                nn(normed_t, gv_ref[g]),
+                nn(context_0, grads_ref[g]),
+            )
+        )
     totals = [first + second for first, second in zip(*parts)]
     split_by_core(core_ref, totals, keep_ref, send_ref)
 
 
-def intra_backward(core, grads, ctx_a, ctx_b, *rest):
-    return pl.pallas_call(
-        intra_backward_kernel,
-        in_specs=specs(9),
-        out_shape=(
+def intra_backward(core, grads, *rest):
+    return kernel_call(
+        intra_backward_kernel, "intra_backward", 4, [SMEM, VMEM] + [HBM] * 3, [VMEM] * 6,
+        (
             f32(2, D, D), bf16(2, D, D), bf16(2, K, D), bf16(2, D, K), bf16(2, K, D), bf16(2, K, D),
         ),
-        compiler_params=params(),
-        cost_estimate=cost(6),
-        name="intra_backward",
-    )(core, grads, ctx_a, ctx_b, *rest)
+        [vbf(HANDED_ROWS, 128), pltpu.VMEM((4 * HEADS, K), F32), vbf(D, D), dma(3)],
+        BACKWARD_LIMIT,
+    )(core, grads, *rest)
 
 
 def intra_tail_kernel(
-    grads_ref, gq_t_ref, gk_ref, gv_ref, f_ref, n_ref, gain_ref, wq_ref, wk_ref, wv_ref,
+    grads_any, gq_t_any, gk_any, gv_any, f_any, n_any, gain_any, wq_any, wk_any, wv_any,
     first_ref, second_ref, carry_ref,
+    grads_ref, gq_t_ref, gk_ref, gv_ref, rows_ref, gain_ref, w_ref, sems, own_sems,
 ):
-    rows = jnp.concatenate([f_ref[...], n_ref[...]], axis=0).astype(F32)
-    unit, inverse = standardize(rows)
+    copies = begin_layer(sems, f_any, n_any, gain_any, wq_any, wk_any, wv_any, rows_ref, gain_ref, w_ref)
+    copies += begin(
+        own_sems,
+        (grads_any, grads_ref), (gq_t_any, gq_t_ref), (gk_any, gk_ref), (gv_any, gv_ref),
+    )
+    settle(copies)
+    unit, inverse = standardize(rows_ref[...].astype(F32))
     halves = []
     for g in range(2):
         at = slice(g * HOP, g * HOP + K)
         grad_normed = (
-            nt(gq_t_ref[g].T, wq_ref[0]) + nt(gk_ref[g], wk_ref[0]) + nt(gv_ref[g], wv_ref[0])
+            nt(gq_t_ref[g].T, w_ref[0]) + nt(gk_ref[g], w_ref[1]) + nt(gv_ref[g], w_ref[2])
         )
         pulled = norm_pullback(grad_normed, unit[at], inverse[at], gain_ref[0:1, :])
         result = (grads_ref[g].astype(F32) + pulled).astype(BF)
@@ -498,12 +631,12 @@
 
 
 def intra_tail(*operands):
-    return pl.pallas_call(
-        intra_tail_kernel,
-        out_shape=(bf16(HOP, D), bf16(HOP, D), bf16(HOP, D)),
-        compiler_params=params(),
-        cost_estimate=cost(2),
-        name="intra_tail",
+    return kernel_call(
+        intra_tail_kernel, "intra_tail", 2, [HBM] * 10, [VMEM] * 3,
+        (bf16(HOP, D), bf16(HOP, D), bf16(HOP, D)),
+        [vbf(2, K, D), vbf(2, D, K), vbf(2, K, D), vbf(2, K, D)]
+        + layer_scratch()
+        + [dma(6), dma(4)],
     )(*operands)
 
 
@@ -533,16 +666,12 @@
         dg_ref[layer : layer + 1, :] = column / gain_ref[layer : layer + 1, :]
 
 
-def finish(core, mine, other, first, second, carried, gains, wq, wk, wv):
+def finish(core, *operands):
     full = f32(2, D, D)
-    return pl.pallas_call(
-        finish_kernel,
-        in_specs=specs(9),
-        out_shape=(bf16(K, D), full, full, full, full, f32(2, D)),
-        compiler_params=params(),
-        cost_estimate=cost(2),
-        name="finish",
-    )(core, mine, other, first, second, carried, gains, wq, wk, wv)
+    return kernel_call(
+        finish_kernel, "finish", 2, [SMEM] + [VMEM] * 9, [VMEM] * 6,
+        (bf16(K, D), full, full, full, full, f32(2, D)), [],
+    )(core, *operands)
 
 
 def shifted(shard, by):
@@ -574,21 +703,21 @@
 def shards(frames, frames_grad, wq, wk, wv, wo, gains):
     frames = frames[0]
     core = lax.axis_index("core").astype(jnp.int32).reshape(1)
-    following = shifted(frames[:HOP], -1)
-    mid, ctx_a, *front = intra_first(frames, gains, wq, wk, wv, wo)
-    packed, ctx_b = intra_second(
-        frames, following, frames_grad[0], mid, *front, gains, wq, wk, wv, wo
-    )
+    following = shifted(frames, -1)
+    front = intra_first(frames, gains, wq, wk, wv, wo)
+    packed = intra_second(following, frames, frames_grad[0], *front, gains, wq, wk, wv, wo)
     across = exchanged(packed.reshape(64, 24, 128), TM).reshape(64 * 24, 128)
     grad_middle, *operands = inter(across, gains, wq, wk, wv, wo)
     grad_local = exchanged(grad_middle.reshape(64, 8, D), TM).reshape(512, D)
     inter_half = core_sum(*inter_weights(core, *operands))
+    grad_local, inter_half = lax.optimization_barrier((grad_local, inter_half))
     prepared = intra_prepare(frames, following, gains, wq, wk, wv)
-    keep, send, *rest = intra_backward(core, grad_local, ctx_a, ctx_b, *prepared, wo)
+    keep, send, *rest = intra_backward(core, grad_local, *prepared, wo)
     half = jnp.concatenate([core_sum(keep, send), inter_half], axis=1)
     first, second, carry = intra_tail(*rest, frames, following, gains, wq, wk, wv)
+    pieces = exchanged(half, PLANE)
+    pieces, first, second, carry = lax.optimization_barrier((pieces, first, second, carry))
     carried = shifted(carry, 1)
-    pieces = exchanged(half, PLANE)
     piece = summed(pieces)
     pieces = exchanged(copies(piece, 8), "z")
     pieces, carried = lax.optimization_barrier((pieces, carried))

time: 129 us -> 127 us (0.984)
  blocking collectives: 56.8 us -> 13.1 us
  waiting for transfers between devices: 8.91 us -> 36.2 us
  starting transfers between devices: 24.4 us -> 45.3 us
  local copies, waits for them, and re-layouts: 17.7 us -> 3.58 us
  Pallas kernels: 18.5 us -> 26.3 us
    all_to_all x3 -> x1, blocking collectives: 56.8 us -> 13.1 us  [exchanged(): return lax.all_to_all(shard, axes, split_axis=0, concat_axis=0, tiled=True)]
    all_to_all x2 -> x4, waiting for transfers between devices: 4.38 us -> 29.1 us  [exchanged(): return lax.all_to_all(shard, axes, split_axis=0, concat_axis=0, tiled=True)]
    all_to_all x2 -> x4, starting transfers between devices: 9.43 us -> 29.7 us  [exchanged(): return lax.all_to_all(shard, axes, split_axis=0, concat_axis=0, tiled=True)]
    unnamed x52 -> x28, local copies, waits for them, and re-layouts: 16.1 us -> 2.82 us
    pallas_call x8, Pallas kernels: 18.5 us -> 26.3 us  [the longest x1 5.04 us: intra_prepare(): kernel_call(intra_prepare_kernel, 'intra_prepare', 3, [HBM] * 6, [VMEM] *...]
    ppermute x2, waiting for transfers between devices: 2.84 us -> 4.44 us  [shifted(): return lax.ppermute(shard, TM, pairs)]
  transfers between devices with their start and end apart: 7 -> 9, of which waited for: 5 -> 8; matrix products, arithmetic and copies ran while one was open for 1% -> 0% of each run, Pallas kernels for 7% -> 8%
where the time goes in v3:
time: 127 us
  starting transfers between devices  45.3 us (36%)
  waiting for transfers between devices  36.2 us (29%)
  Pallas kernels  26.3 us (21%)
  blocking collectives  13.1 us (10%)
  local copies, waits for them, and re-layouts  3.58 us (3%)
    all_to_all x4, starting transfers between devices, exchanged(): return lax.all_to_all(shard, axes, split_axis=0, concat_axis=0, tiled=True)  29.7 us
    all_to_all x4, waiting for transfers between devices, exchanged(): return lax.all_to_all(shard, axes, split_axis=0, concat_axis=0, tiled=True)  29.1 us
    all_to_all x1, blocking collectives, exchanged(): return lax.all_to_all(shard, axes, split_axis=0, concat_axis=0, tiled=True)  13.1 us
    ppermute x3, starting transfers between devices, swapped(): return lax.ppermute(shard, 'core', [(0, 1), (1, 0)])  11.1 us
    pallas_call x1, Pallas kernels, intra_prepare(): kernel_call(intra_prepare_kernel, 'intra_prepare', 3, [HBM] * 6, [VMEM] *...  5.04 us
    pallas_call x1, Pallas kernels, inter(): kernel_call(inter_kernel, 'inter', 5, [VMEM] * 6, [VMEM] * 7, (bf16(512,...  4.94 us
    pallas_call x1, Pallas kernels, intra_second(): kernel_call(intra_second_kernel, 'intra_second', 3, [HBM] * 12, VMEM, bf1...  4.85 us
    ppermute x2, starting transfers between devices, shifted(): return lax.ppermute(shard, TM, pairs)  4.55 us
  transfers between devices with their start and end apart: 9, of which 8 were waited for; matrix products, arithmetic and copies ran while one was open for 0% of the time, Pallas kernels for 8%

profile of v3, /device:TPU:1, one launch (start us, length us, event | category | flops | bytes accessed | tf_op | source)
XLA Modules:
  0.0 126.5 jit_solution(1080786668196578102)
XLA Ops:
  0.6 1.3 %collective-permute-start = (bf16[256,256]{1,0:T(8,128)(2,1)}, bf16[256,256]{1,0:T(8,128)(2,1)S(1)}, u32[]{:S(2)}, u32[]{:S(2)}) collective-permute-start(bf16[256,256]{1,0:T(8,128)(2,1)} %bitcast.15), channel_id=1, source_target_pairs={{1,0},{2,1},{3,2},{4,3},{5,4},{6,5},{7,6},{8,7},{9,8},{10,9},{11,1... | collective-permute-start | bytes 393224 | tf_op jit(solution)/shard_map/ppermute | solution.py:680
  1.9 3.5 %intra_first.1 = (bf16[256,256]{1,0:T(8,128)(2,1)}, bf16[128,256]{1,0:T(8,128)(2,1)}, bf16[256,128]{1,0:T(8,128)(2,1)}, bf16[256,128]{1,0:T(8,128)(2,1)}) custom-call(bf16[256,256]{1,0:T(8,128)(2,1)} %bitcast.16, f32[2,256]{1,0:T(2,128)} %gain_ref.3, bf16[2,256,256]{2,1,0:T(8,128)(2,1)} %wq_ref.3, bf16[2,256,256]{2,1,0:T(8,128)(2,1)} %wk_ref.3, ...), custom_call_target="tpu_custom_call" | custom-call | flops 1200000000 | bytes 1048576 | tf_op jit(solution)/shard_map/intra_first/pallas_call | solution.py:271
  5.4 2.1 %collective-permute-done.n_any = bf16[256,256]{1,0:T(8,128)(2,1)S(1)} collective-permute-done((bf16[256,256]{1,0:T(8,128)(2,1)}, bf16[256,256]{1,0:T(8,128)(2,1)S(1)}, u32[]{:S(2)}, u32[]{:S(2)}) %collective-permute-start) | collective-permute-done | bytes 131104 | tf_op jit(solution)/shard_map/ppermute | solution.py:680
  7.6 0.7 copy-done.8
  8.2 0.0 copy-start.10
  8.2 4.8 %intra_second.1 = bf16[1536,128]{1,0:T(8,128)(2,1)} custom-call(bf16[256,256]{1,0:T(8,128)(2,1)} %copy-done.8, bf16[256,256]{1,0:T(8,128)(2,1)} %bitcast.17, bf16[256,256]{1,0:T(8,128)(2,1)} %bitcast.23, bf16[256,256]{1,0:T(8,128)(2,1)} %get-tuple-element.44.mid_any, bf16[128,256]{1,0:T(8,128)(2,1)} %get-tuple-element.45.keys_any, ...), custom_call_target="tpu_custom_call" | custom-call | flops 1200000000 | bytes 1048576 | tf_op jit(solution)/shard_map/intra_second/pallas_call | solution.py:280
  13.1 14.6 %all-to-all-start = ((bf16[64,24,128]{2,1,0:T(8,128)(2,1)}), bf16[64,24,128]{2,1,0:T(8,128)(2,1)S(1)}, u32[]{:S(2)}, u32[]{:S(2)}) async-start(bf16[64,24,128]{2,1,0:T(8,128)(2,1)} %bitcast.22), calls=%async_computation | async-start | bytes 786432 | tf_op jit(solution)/shard_map/all_to_all | solution.py:684
  27.8 13.4 %all-to-all-done = bf16[64,24,128]{2,1,0:T(8,128)(2,1)S(1)} async-done(((bf16[64,24,128]{2,1,0:T(8,128)(2,1)}), bf16[64,24,128]{2,1,0:T(8,128)(2,1)S(1)}, u32[]{:S(2)}, u32[]{:S(2)}) %all-to-all-start) | async-done | bytes 393248 | tf_op jit(solution)/shard_map/all_to_all | solution.py:684
  41.2 0.0 copy-done
  41.2 0.0 copy-done.1
  41.2 0.0 copy-done.3
  41.2 0.0 copy-done.5
  41.2 0.0 copy-done.10
  41.2 4.9 %inter.1 = (bf16[512,256]{1,0:T(8,128)(2,1)}, bf16[256,512]{1,0:T(8,128)(2,1)S(1)}, bf16[512,256]{1,0:T(8,128)(2,1)S(1)}, bf16[256,512]{1,0:T(8,128)(2,1)S(1)}, ...) custom-call(bf16[1536,128]{1,0:T(8,128)(2,1)S(1)} %bitcast.13, ...), custom_call_target="tpu_custom_call" | custom-call | flops 2000000000 | bytes 1048576 | tf_op jit(solution)/shard_map/inter/pallas_call | solution.py:385
  46.1 6.1 %all-to-all-start.1 = ((bf16[64,8,256]{2,1,0:T(8,128)(2,1)}), bf16[64,8,256]{2,1,0:T(8,128)(2,1)S(1)}, u32[]{:S(2)}, u32[]{:S(2)}) async-start(bf16[64,8,256]{2,1,0:T(8,128)(2,1)} %bitcast.5), calls=%async_computation.1 | async-start | bytes 524288 | tf_op jit(solution)/shard_map/all_to_all | solution.py:684
  52.2 0.4 inter_weights.1
  52.7 2.7 %collective-permute-start.1 = (bf16[2,256,256]{2,1,0:T(8,128)(2,1)S(1)}, bf16[2,256,256]{2,1,0:T(8,128)(2,1)S(1)}, u32[]{:S(2)}, u32[]{:S(2)}) collective-permute-start(bf16[2,256,256]{2,1,0:T(8,128)(2,1)S(1)} %get-tuple-element.56), channel_id=1, source_target_pairs={{0,64},{64,0},{1,65},{65,1},{2,66},{66,2},{3,67},{67,3},{4,68},{68... | collective-permute-start | bytes 786440 | tf_op jit(solution)/shard_map/ppermute | solution.py:688
  55.3 5.0 %intra_prepare.1 = (bf16[5632,128]{1,0:T(8,128)(2,1)}, f32[32,256]{1,0:T(8,128)}) custom-call(bf16[256,256]{1,0:T(8,128)(2,1)} %bitcast.18, bf16[256,256]{1,0:T(8,128)(2,1)} %copy-done.8, f32[2,256]{1,0:T(2,128)} %gain_ref.3, bf16[2,256,256]{2,1,0:T(8,128)(2,1)} %wq_ref.3, bf16[2,256,256]{2,1,0:T(8,128)(2,1)} %wk_ref.3, bf16[2,256,256]{2,1,0:T(8,128)(2,1)} %wv_ref.3), custom_call_target="tpu_custom_call" | custom-call | flops 1200000000 | bytes 1048576 | tf_op jit(solution)/shard_map/intra_prepare/pallas_call | solution.py:507
  60.4 0.0 collective-permute-done.1
  60.4 0.1 add_convert_fusion.1
  60.5 2.7 %all-to-all-done.1 = bf16[64,8,256]{2,1,0:T(8,128)(2,1)S(1)} async-done(((bf16[64,8,256]{2,1,0:T(8,128)(2,1)}), bf16[64,8,256]{2,1,0:T(8,128)(2,1)S(1)}, u32[]{:S(2)}, u32[]{:S(2)}) %all-to-all-start.1) | async-done | bytes 262176 | tf_op jit(solution)/shard_map/all_to_all | solution.py:684
  63.2 1.4 %copy-done.12 = bf16[5632,128]{1,0:T(8,128)(2,1)S(1)} copy-done((bf16[5632,128]{1,0:T(8,128)(2,1)S(1)}, bf16[5632,128]{1,0:T(8,128)(2,1)}, u32[]{:S(2)}) %copy-start.12) | copy-done | bytes 1441816
  64.6 0.8 copy-done.13
  65.3 4.4 %intra_backward.1 = (f32[2,256,256]{2,1,0:T(8,128)S(1)}, bf16[2,256,256]{2,1,0:T(8,128)(2,1)S(1)}, bf16[2,256,256]{2,1,0:T(8,128)(2,1)S(1)}, bf16[2,256,256]{2,1...) custom-call(s32[1]{0:T(128)} %bitcast.core_ref, bf16[512,256]{1,0:T(8,128)(2,1)S(1)} %bitcast.14, ...), custom_call_target="tpu_custom_call" | custom-call | flops 1600000000 | bytes 1048576 | tf_op jit(solution)/shard_map/intra_backward/pallas_call | solution.py:597
  69.7 3.8 %collective-permute-start.2 = (bf16[2,256,256]{2,1,0:T(8,128)(2,1)S(1)}, bf16[2,256,256]{2,1,0:T(8,128)(2,1)S(1)}, u32[]{:S(2)}, u32[]{:S(2)}) collective-permute-start(bf16[2,256,256]{2,1,0:T(8,128)(2,1)S(1)} %get-tuple-element.61), channel_id=1, source_target_pairs={{0,64},{64,0},{1,65},{65,1},{2,66},{66,2},{3,67},{67,3},{4,68},{68... | collective-permute-start | bytes 786440 | tf_op jit(solution)/shard_map/ppermute | solution.py:688
  73.5 1.2 collective-permute-done.2
  74.7 0.0 copy-start.11
  74.7 0.1 add_convert_fusion
  74.8 0.8 pad_maximum_fusion
  75.6 5.6 %all-to-all-start.2 = ((bf16[16,64,256]{2,1,0:T(8,128)(2,1)}), bf16[16,64,256]{2,1,0:T(8,128)(2,1)S(1)}, u32[]{:S(2)}, u32[]{:S(2)}) async-start(bf16[16,64,256]{2,1,0:T(8,128)(2,1)} %pad_maximum_fusion), calls=%async_computation.2 | async-start | bytes 1048576 | tf_op jit(solution)/shard_map/all_to_all | solution.py:684
  81.2 0.0 copy-done.2
  81.2 0.0 copy-done.4
  81.2 0.0 copy-done.6
  81.2 0.0 copy-done.7
  81.2 0.0 copy-done.9
  81.2 0.0 copy-done.11
  81.2 1.5 %intra_tail.1 = (bf16[128,256]{1,0:T(8,128)(2,1)S(1)}, bf16[128,256]{1,0:T(8,128)(2,1)S(1)}, bf16[128,256]{1,0:T(8,128)(2,1)S(1)}) custom-call(bf16[2,256,256]{2,1,0:T(8,128)(2,1)S(1)} %get-tuple-element.63.grads_any, bf16[2,256,256]{2,1,0:T(8,128)(2,1)S(1)} %get-tuple-element.64.gq_t_any, bf16[2,256,256]{2,1,0:T(8,128)(2,1)S(1)} %get-tuple-element.65.gk_any, ...), custom_call_target="tpu_custom_call" | custom-call | flops 800000000 | bytes 1048576 | tf_op jit(solution)/shard_map/intra_tail/pallas_call | solution.py:634
  82.8 9.1 %all-to-all-done.2 = bf16[16,64,256]{2,1,0:T(8,128)(2,1)S(1)} async-done(((bf16[16,64,256]{2,1,0:T(8,128)(2,1)}), bf16[16,64,256]{2,1,0:T(8,128)(2,1)S(1)}, u32[]{:S(2)}, u32[]{:S(2)}) %all-to-all-start.2) | async-done | bytes 524320 | tf_op jit(solution)/shard_map/all_to_all | solution.py:684
  91.9 0.1 reduce_sum.24
  92.0 0.7 broadcast_in_dim.6
  92.7 3.4 %all-to-all-start.3 = ((bf16[8,64,256]{2,1,0:T(8,128)(2,1)}), bf16[8,64,256]{2,1,0:T(8,128)(2,1)S(1)}, u32[]{:S(2)}, u32[]{:S(2)}) async-start(bf16[8,64,256]{2,1,0:T(8,128)(2,1)} %broadcast_in_dim.6), calls=%async_computation.3 | async-start | bytes 524288 | tf_op jit(solution)/shard_map/all_to_all | solution.py:684
  96.1 3.3 %collective-permute-start.3 = (bf16[128,256]{1,0:T(8,128)(2,1)S(1)}, bf16[128,256]{1,0:T(8,128)(2,1)S(1)}, u32[]{:S(2)}, u32[]{:S(2)}) collective-permute-start(bf16[128,256]{1,0:T(8,128)(2,1)S(1)} %get-tuple-element.71), channel_id=1, source_target_pairs={{0,1},{1,2},{2,3},{3,4},{4,5},{5,6},{6,7},{7,8},{8,9},{9,10},{10,1... | collective-permute-start | bytes 196616 | tf_op jit(solution)/shard_map/ppermute | solution.py:680
  99.4 2.3 %collective-permute-done.3.carried_ref = bf16[128,256]{1,0:T(8,128)(2,1)S(1)} collective-permute-done((bf16[128,256]{1,0:T(8,128)(2,1)S(1)}, bf16[128,256]{1,0:T(8,128)(2,1)S(1)}, u32[]{:S(2)}, u32[]{:S(2)}) %collective-permute-start.3) | collective-permute-done | bytes 65568 | tf_op jit(solution)/shard_map/ppermute | solution.py:680
  101.7 3.9 %all-to-all-done.3 = bf16[8,64,256]{2,1,0:T(8,128)(2,1)S(1)} async-done(((bf16[8,64,256]{2,1,0:T(8,128)(2,1)}), bf16[8,64,256]{2,1,0:T(8,128)(2,1)S(1)}, u32[]{:S(2)}, u32[]{:S(2)}) %all-to-all-start.3) | async-done | bytes 262176 | tf_op jit(solution)/shard_map/all_to_all | solution.py:684
  105.6 13.1 %all_to_all.25 = bf16[16,64,256]{2,1,0:T(8,128)(2,1)S(1)} all-to-all(bf16[16,64,256]{2,1,0:T(8,128)(2,1)S(1)} %broadcast_in_dim.7), channel_id=1, replica_groups=mesh['yh'=2,'core'=2,'yl'=2,'x'=4,'z'=8] {'yh','yl','x'}, dimensions={0} | all-to-all | bytes 1048576 | tf_op jit(solution)/shard_map/all_to_all | solution.py:684
  118.7 4.6 %collective-permute-start.4 = (bf16[16,2,32,256]{3,2,1,0:T(8,128)(2,1)S(1)}, bf16[16,2,32,256]{3,2,1,0:T(8,128)(2,1)S(1)}, u32[]{:S(2)}, u32[]{:S(2)}) collective-permute-start(bf16[16,2,32,256]{3,2,1,0:T(8,128)(2,1)S(1)} %bitcast.11), channel_id=1, source_target_pairs={{0,64},{64,0},{1,65},{65,1},{2,66},{66,2},{3,67},{67,3},{4,68},{68... | collective-permute-start | bytes 1572872 | tf_op jit(solution)/shard_map/ppermute | solution.py:688
  123.3 1.5 %collective-permute-done.4.other_ref = bf16[16,2,32,256]{3,2,1,0:T(8,128)(2,1)S(1)} collective-permute-done((bf16[16,2,32,256]{3,2,1,0:T(8,128)(2,1)S(1)}, bf16[16,2,32,256]{3,2,1,0:T(8,128)(2,1)S(1)}, u32[]{:S(2)}, u32[]{:S(2)}) %collective-permute-start.4) | collective-permute-done | bytes 524320 | tf_op jit(solution)/shard_map/ppermute | solution.py:688
  124.9 1.6 %finish.1 = (bf16[256,256]{1,0:T(8,128)(2,1)}, f32[2,256,256]{2,1,0:T(8,128)}, f32[2,256,256]{2,1,0:T(8,128)}, f32[2,256,256]{2,1,0:T(8,128)}, f32[2,256,256]{2,1,0:T(8,128)}, /*index=5*/f32[2,256]{1,0:T(2,128)}) custom-call(s32[1]{0:T(128)} %bitcast.core_ref, bf16[16,2,32,256]{3,2,1,0:T(8,128)(2,1)S(1)} %bitcast.12, ...), custom_call_target="tpu_custom_call" | custom-call | flops 800000000 | bytes 1048576 | tf_op jit(solution)/shard_map/finish/pallas_call | solution.py:671
  (14 shorter events, 0.1 us)
Async XLA Ops:
  0.6 6.9 %collective-permute-start = (bf16[256,256]{1,0:T(8,128)(2,1)}, bf16[256,256]{1,0:T(8,128)(2,1)S(1)}, u32[]{:S(2)}, u32[]{:S(2)}) collective-permute-start(bf16[256,256]{1,0:T(8,128)(2,1)} %bitcast.15), channel_id=1, source_target_pairs={{1,0},{2,1},{3,2},{4,3},{5,4},{6,5},{7,6},{8,7},{9,8},{10,9},{11,1... | collective-permute-start | bytes 393224 | tf_op jit(solution)/shard_map/ppermute | solution.py:680
  7.6 0.7 copy-start.8
  8.2 32.9 %copy-start = (bf16[2,256,256]{2,1,0:T(8,128)(2,1)S(1)}, bf16[2,256,256]{2,1,0:T(8,128)(2,1)}, u32[]{:S(2)}) copy-start(bf16[2,256,256]{2,1,0:T(8,128)(2,1)} %wo_any.5) | copy-start | bytes 786436
  8.2 32.9 %copy-start.1 = (bf16[2,256,256]{2,1,0:T(8,128)(2,1)S(1)}, bf16[2,256,256]{2,1,0:T(8,128)(2,1)}, u32[]{:S(2)}) copy-start(bf16[2,256,256]{2,1,0:T(8,128)(2,1)} %wq_ref.3) | copy-start | bytes 786436
  8.2 32.9 %copy-start.3 = (bf16[2,256,256]{2,1,0:T(8,128)(2,1)S(1)}, bf16[2,256,256]{2,1,0:T(8,128)(2,1)}, u32[]{:S(2)}) copy-start(bf16[2,256,256]{2,1,0:T(8,128)(2,1)} %wk_ref.3) | copy-start | bytes 786436
  8.2 32.9 %copy-start.5 = (bf16[2,256,256]{2,1,0:T(8,128)(2,1)S(1)}, bf16[2,256,256]{2,1,0:T(8,128)(2,1)}, u32[]{:S(2)}) copy-start(bf16[2,256,256]{2,1,0:T(8,128)(2,1)} %wv_ref.3) | copy-start | bytes 786436
  8.2 32.9 %copy-start.10 = (f32[2,256]{1,0:T(2,128)S(1)}, f32[2,256]{1,0:T(2,128)}, u32[]{:S(2)}) copy-start(f32[2,256]{1,0:T(2,128)} %gain_ref.3) | copy-start | bytes 6148
  13.1 28.1 %all-to-all-start = ((bf16[64,24,128]{2,1,0:T(8,128)(2,1)}), bf16[64,24,128]{2,1,0:T(8,128)(2,1)S(1)}, u32[]{:S(2)}, u32[]{:S(2)}) async-start(bf16[64,24,128]{2,1,0:T(8,128)(2,1)} %bitcast.22), calls=%async_computation | async-start | bytes 786432 | tf_op jit(solution)/shard_map/all_to_all | solution.py:684
  46.1 17.1 %all-to-all-start.1 = ((bf16[64,8,256]{2,1,0:T(8,128)(2,1)}), bf16[64,8,256]{2,1,0:T(8,128)(2,1)S(1)}, u32[]{:S(2)}, u32[]{:S(2)}) async-start(bf16[64,8,256]{2,1,0:T(8,128)(2,1)} %bitcast.5), calls=%async_computation.1 | async-start | bytes 524288 | tf_op jit(solution)/shard_map/all_to_all | solution.py:684
  52.7 7.7 %collective-permute-start.1 = (bf16[2,256,256]{2,1,0:T(8,128)(2,1)S(1)}, bf16[2,256,256]{2,1,0:T(8,128)(2,1)S(1)}, u32[]{:S(2)}, u32[]{:S(2)}) collective-permute-start(bf16[2,256,256]{2,1,0:T(8,128)(2,1)S(1)} %get-tuple-element.56), channel_id=1, source_target_pairs={{0,64},{64,0},{1,65},{65,1},{2,66},{66,2},{3,67},{67,3},{4,68},{68... | collective-permute-start | bytes 786440 | tf_op jit(solution)/shard_map/ppermute | solution.py:688
  63.2 1.4 %copy-start.12 = (bf16[5632,128]{1,0:T(8,128)(2,1)S(1)}, bf16[5632,128]{1,0:T(8,128)(2,1)}, u32[]{:S(2)}) copy-start(bf16[5632,128]{1,0:T(8,128)(2,1)} %get-tuple-element.58.handed_any) | copy-start | bytes 4325380
  64.6 0.8 copy-start.13
  69.7 4.9 %collective-permute-start.2 = (bf16[2,256,256]{2,1,0:T(8,128)(2,1)S(1)}, bf16[2,256,256]{2,1,0:T(8,128)(2,1)S(1)}, u32[]{:S(2)}, u32[]{:S(2)}) collective-permute-start(bf16[2,256,256]{2,1,0:T(8,128)(2,1)S(1)} %get-tuple-element.61), channel_id=1, source_target_pairs={{0,64},{64,0},{1,65},{65,1},{2,66},{66,2},{3,67},{67,3},{4,68},{68... | collective-permute-start | bytes 786440 | tf_op jit(solution)/shard_map/ppermute | solution.py:688
  74.7 6.5 %copy-start.2 = (bf16[2,256,256]{2,1,0:T(8,128)(2,1)S(1)}, bf16[2,256,256]{2,1,0:T(8,128)(2,1)}, u32[]{:S(2)}) copy-start(bf16[2,256,256]{2,1,0:T(8,128)(2,1)} %wq_ref.3) | copy-start | bytes 786436
  74.7 6.5 %copy-start.4 = (bf16[2,256,256]{2,1,0:T(8,128)(2,1)S(1)}, bf16[2,256,256]{2,1,0:T(8,128)(2,1)}, u32[]{:S(2)}) copy-start(bf16[2,256,256]{2,1,0:T(8,128)(2,1)} %wk_ref.3) | copy-start | bytes 786436
  74.7 6.5 %copy-start.6 = (bf16[2,256,256]{2,1,0:T(8,128)(2,1)S(1)}, bf16[2,256,256]{2,1,0:T(8,128)(2,1)}, u32[]{:S(2)}) copy-start(bf16[2,256,256]{2,1,0:T(8,128)(2,1)} %wv_ref.3) | copy-start | bytes 786436
  74.7 6.5 %copy-start.7 = (bf16[1,256,256]{2,1,0:T(8,128)(2,1)S(1)}, bf16[1,256,256]{2,1,0:T(8,128)(2,1)}, u32[]{:S(2)}) copy-start(bf16[1,256,256]{2,1,0:T(8,128)(2,1)} %param.7) | copy-start | bytes 393220
  74.7 6.5 %copy-start.9 = (bf16[256,256]{1,0:T(8,128)(2,1)S(1)}, bf16[256,256]{1,0:T(8,128)(2,1)}, u32[]{:S(2)}) copy-start(bf16[256,256]{1,0:T(8,128)(2,1)} %copy-done.8) | copy-start | bytes 393220
  74.7 6.5 %copy-start.11 = (f32[2,256]{1,0:T(2,128)S(1)}, f32[2,256]{1,0:T(2,128)}, u32[]{:S(2)}) copy-start(f32[2,256]{1,0:T(2,128)} %gain_ref.3) | copy-start | bytes 6148
  75.6 16.3 %all-to-all-start.2 = ((bf16[16,64,256]{2,1,0:T(8,128)(2,1)}), bf16[16,64,256]{2,1,0:T(8,128)(2,1)S(1)}, u32[]{:S(2)}, u32[]{:S(2)}) async-start(bf16[16,64,256]{2,1,0:T(8,128)(2,1)} %pad_maximum_fusion), calls=%async_computation.2 | async-start | bytes 1048576 | tf_op jit(solution)/shard_map/all_to_all | solution.py:684
  92.7 12.8 %all-to-all-start.3 = ((bf16[8,64,256]{2,1,0:T(8,128)(2,1)}), bf16[8,64,256]{2,1,0:T(8,128)(2,1)S(1)}, u32[]{:S(2)}, u32[]{:S(2)}) async-start(bf16[8,64,256]{2,1,0:T(8,128)(2,1)} %broadcast_in_dim.6), calls=%async_computation.3 | async-start | bytes 524288 | tf_op jit(solution)/shard_map/all_to_all | solution.py:684
  96.1 5.6 %collective-permute-start.3 = (bf16[128,256]{1,0:T(8,128)(2,1)S(1)}, bf16[128,256]{1,0:T(8,128)(2,1)S(1)}, u32[]{:S(2)}, u32[]{:S(2)}) collective-permute-start(bf16[128,256]{1,0:T(8,128)(2,1)S(1)} %get-tuple-element.71), channel_id=1, source_target_pairs={{0,1},{1,2},{2,3},{3,4},{4,5},{5,6},{6,7},{7,8},{8,9},{9,10},{10,1... | collective-permute-start | bytes 196616 | tf_op jit(solution)/shard_map/ppermute | solution.py:680
  118.7 6.1 %collective-permute-start.4 = (bf16[16,2,32,256]{3,2,1,0:T(8,128)(2,1)S(1)}, bf16[16,2,32,256]{3,2,1,0:T(8,128)(2,1)S(1)}, u32[]{:S(2)}, u32[]{:S(2)}) collective-permute-start(bf16[16,2,32,256]{3,2,1,0:T(8,128)(2,1)S(1)} %bitcast.11), channel_id=1, source_target_pairs={{0,64},{64,0},{1,65},{65,1},{2,66},{66,2},{3,67},{67,3},{4,68},{68... | collective-permute-start | bytes 1572872 | tf_op jit(solution)/shard_map/ppermute | solution.py:688

commit v4 on v3

--- a/solution.py
+++ b/solution.py
@@ -19,9 +19,10 @@
 BF = jnp.bfloat16
 F32 = jnp.float32
 VMEM_LIMIT = 16 * 1024 * 1024
-WHOLE_LIMIT = 62 * 1024 * 1024
+FIRST_LIMIT = 54800 * 1024
+SECOND_LIMIT = 54300 * 1024
 PREPARE_LIMIT = 56 * 1024 * 1024
-BACKWARD_LIMIT = 16 * 1024 * 1024
+BACKWARD_LIMIT = 52850 * 1024
 
 AXES = ("yh", "core", "yl", "x", "z")
 DP = ("yh", "core")
@@ -218,29 +219,23 @@
 
 
 def intra_second_kernel(
-    n_any, f_any, grad_any, mid_any, keys_any, queries_any, values_any,
-    gain_any, wq_any, wk_any, wv_any, wo_any, packed_ref,
-    n_ref, f_ref, grad_ref, mid_in_ref, keys_ref, queries_ref, values_ref, gain_ref, w_ref, ctx_ref, sems,
+    n_ref, mid_in_ref, keys_ref, queries_ref, values_ref,
+    f_any, grad_any, gain_any, wq_any, wk_any, wv_any, wo_any, packed_ref,
+    f_ref, grad_ref, gain_ref, w_ref, ctx_ref, sems,
 ):
     copies = begin(
         sems,
-        (n_any.at[pl.ds(0, HOP)], n_ref),
         (gain_any, gain_ref),
         (wk_any.at[0], w_ref.at[1]),
         (wq_any.at[0], w_ref.at[0]),
         (wv_any.at[0], w_ref.at[2]),
-        (keys_any, keys_ref),
-        (queries_any, queries_ref),
-        (values_any, values_ref),
         (wo_any.at[0], w_ref.at[3]),
-        (mid_any, mid_in_ref),
         (f_any.at[pl.ds(HOP, HOP)], f_ref),
         (grad_any, grad_ref),
     )
-    copies[0].wait()
-    rows = n_ref[...].astype(F32)
+    rows = n_ref[:HOP].astype(F32)
     unit, _ = standardize(rows)
-    settle(copies[1:8])
+    settle(copies[:4])
     normed = (unit * gain_ref[0:1, :]).astype(BF)
     keys = jnp.concatenate([keys_ref[...], nn(normed, w_ref[1]).astype(BF)], axis=0)
     queries_t = jnp.concatenate(
@@ -248,7 +243,7 @@
     )
     values_t = jnp.concatenate([values_ref[...], nt(w_ref[2].T, normed).astype(BF)], axis=1)
     attend(keys, queries_t, values_t, ctx_ref)
-    settle(copies[8:])
+    settle(copies[4:])
     rows = jnp.concatenate([f_ref[...].astype(F32), rows], axis=0)
     mids = (mid_in_ref[...], (rows + tn(ctx_ref[...], w_ref[3])).astype(BF))
     grads = grad_ref[...]
@@ -272,19 +267,19 @@
         intra_first_kernel, "intra_first", 3, [HBM] * 6, [VMEM] * 4,
         (bf16(K, D), bf16(HOP, D), bf16(D, HOP), bf16(D, HOP)),
         [vbf(4, D, D), pltpu.VMEM((2, D), F32), vbf(K, D), vbf(D, K), dma(6)],
-        WHOLE_LIMIT,
+        FIRST_LIMIT,
     )(frames, gains, wq, wk, wv, wo)
 
 
-def intra_second(following, frames, grads, *rest):
+def intra_second(following, *rest):
     return kernel_call(
-        intra_second_kernel, "intra_second", 3, [HBM] * 12, VMEM, bf16(64 * 24, 128),
+        intra_second_kernel, "intra_second", 3, [VMEM] * 5 + [HBM] * 7, VMEM,
+        bf16(64 * 24, 128),
         [
-            vbf(HOP, D), vbf(HOP, D), vbf(K, D), vbf(K, D), vbf(HOP, D), vbf(D, HOP), vbf(D, HOP),
-            pltpu.VMEM((2, D), F32), vbf(4, D, D), vbf(D, K), dma(12),
+            vbf(HOP, D), vbf(K, D), pltpu.VMEM((2, D), F32), vbf(4, D, D), vbf(D, K), dma(7),
         ],
-        WHOLE_LIMIT,
-    )(following, frames, grads, *rest)
+        SECOND_LIMIT,
+    )(following, *rest)
 
 
 def inter_kernel(
@@ -419,8 +414,30 @@
     )(core, *operands)
 
 
-NORMED_T, QUERIES, QUERIES_T, KEYS, KEYS_T, VALUES, CONTEXT = (768 * i for i in range(7))
-HANDED_ROWS = 768 * 6 + 1024
+KEYS, QUERIES_T, VALUES, STATS = 0, 768, 1536, 2304
+QUERIES, KEYS_T, NORMED_T, CONTEXT = 2496, 3264, 4032, 4800
+HANDED_ROWS = 5824
+
+
+def put_stats(handed_ref, stats):
+    for i in range(3):
+        part = stats.astype(BF)
+        stats = stats - part.astype(F32)
+        put_blocks(handed_ref, STATS + 64 * i, part)
+
+
+def stats_of(handed_ref):
+    parts = [
+        jnp.concatenate(
+            [
+                handed_ref[STATS + 64 * i + 32 * j : STATS + 64 * i + 32 * j + 32, :].astype(F32)
+                for j in range(2)
+            ],
+            axis=1,
+        )
+        for i in range(3)
+    ]
+    return parts[0] + parts[1] + parts[2]
 
 
 def put_blocks(handed_ref, start, array):
@@ -460,8 +477,8 @@
 
 
 def intra_prepare_kernel(
-    f_any, n_any, gain_any, wq_any, wk_any, wv_any, handed_ref, stats_ref,
-    ctx_ref, rows_ref, gain_ref, w_ref, sems,
+    f_any, n_any, gain_any, wq_any, wk_any, wv_any, handed_ref,
+    stats_ref, ctx_ref, rows_ref, gain_ref, w_ref, sems,
 ):
     settle(begin_layer(sems, f_any, n_any, gain_any, wq_any, wk_any, wv_any, rows_ref, gain_ref, w_ref))
     unit, _ = standardize(rows_ref[...].astype(F32))
@@ -501,24 +518,28 @@
     staged(2 * HEADS, scores_of, weigh, collect)
     for g in range(2):
         put_blocks(handed_ref, CONTEXT + 512 * g, ctx_ref[g])
+    put_stats(handed_ref, stats_ref[...])
 
 
 def intra_prepare(frames, following, gains, wq, wk, wv):
     return kernel_call(
-        intra_prepare_kernel, "intra_prepare", 3, [HBM] * 6, [VMEM] * 2,
-        (bf16(HANDED_ROWS, 128), f32(4 * HEADS, K)),
-        [vbf(2, D, K)] + layer_scratch() + [dma(6)],
+        intra_prepare_kernel, "intra_prepare", 3, [HBM] * 6, VMEM, bf16(HANDED_ROWS, 128),
+        [pltpu.VMEM((4 * HEADS, K), F32), vbf(2, D, K)] + layer_scratch() + [dma(6)],
         PREPARE_LIMIT,
     )(frames, following, gains, wq, wk, wv)
 
 
 def intra_backward_kernel(
-    core_ref, m_ref, handed_any, stats_any, wo_any,
+    core_ref, m_ref, handed_any, wo_any,
     keep_ref, send_ref, grads_ref, gq_t, gk_ref, gv_ref,
     handed_ref, stats_ref, wo_ref, sems,
 ):
+    cuts = (KEYS, QUERIES, NORMED_T, HANDED_ROWS)
+    spans = [pl.ds(start, end - start) for start, end in zip(cuts, cuts[1:])]
     copies = begin(
-        sems, (wo_any.at[0], wo_ref), (stats_any, stats_ref), (handed_any, handed_ref)
+        sems,
+        (wo_any.at[0], wo_ref),
+        *[(handed_any.at[span], handed_ref.at[span]) for span in spans],
     )
     pick = select_rows(256, 256, owner_target)
     tiles = [nn(pick, m_ref[256 * t : 256 * t + 256, :]).astype(BF) for t in range(2)]
@@ -534,7 +555,8 @@
         context.append(nt(grads_ref[g], wo_ref[...]).astype(BF))
         context_t.append(context[g].T)
 
-    settle(copies[1:])
+    copies[1].wait()
+    stats_ref[...] = stats_of(handed_ref)
 
     def place(step):
         g, h = step // HEADS, step % HEADS
@@ -558,6 +580,8 @@
     sums = {}
 
     def collect(step, held):
+        if step == 0:
+            copies[2].wait()
         low, grad_scores = held
         g, at, b, i = place(step)
         block = slice(128 * b, 128 * b + 128)
@@ -573,6 +597,7 @@
             gk_ref[g, :, block] = sums["k"].astype(BF)
 
     staged(2 * HEADS, products, weigh, collect)
+    copies[3].wait()
     parts = []
     for g in range(2):
         normed_t = features_of(
@@ -595,11 +620,11 @@
 
 def intra_backward(core, grads, *rest):
     return kernel_call(
-        intra_backward_kernel, "intra_backward", 4, [SMEM, VMEM] + [HBM] * 3, [VMEM] * 6,
+        intra_backward_kernel, "intra_backward", 4, [SMEM, VMEM] + [HBM] * 2, [VMEM] * 6,
         (
             f32(2, D, D), bf16(2, D, D), bf16(2, K, D), bf16(2, D, K), bf16(2, K, D), bf16(2, K, D),
         ),
-        [vbf(HANDED_ROWS, 128), pltpu.VMEM((4 * HEADS, K), F32), vbf(D, D), dma(3)],
+        [vbf(HANDED_ROWS, 128), pltpu.VMEM((4 * HEADS, K), F32), vbf(D, D), dma(4)],
         BACKWARD_LIMIT,
     )(core, grads, *rest)
 
@@ -705,23 +730,22 @@
     core = lax.axis_index("core").astype(jnp.int32).reshape(1)
     following = shifted(frames, -1)
     front = intra_first(frames, gains, wq, wk, wv, wo)
-    packed = intra_second(following, frames, frames_grad[0], *front, gains, wq, wk, wv, wo)
+    packed = intra_second(
+        following, *front, frames, frames_grad[0], gains, wq, wk, wv, wo
+    )
     across = exchanged(packed.reshape(64, 24, 128), TM).reshape(64 * 24, 128)
     grad_middle, *operands = inter(across, gains, wq, wk, wv, wo)
     grad_local = exchanged(grad_middle.reshape(64, 8, D), TM).reshape(512, D)
     inter_half = core_sum(*inter_weights(core, *operands))
     grad_local, inter_half = lax.optimization_barrier((grad_local, inter_half))
-    prepared = intra_prepare(frames, following, gains, wq, wk, wv)
-    keep, send, *rest = intra_backward(core, grad_local, *prepared, wo)
+    handed = intra_prepare(frames, following, gains, wq, wk, wv)
+    keep, send, *rest = intra_backward(core, grad_local, handed, wo)
     half = jnp.concatenate([core_sum(keep, send), inter_half], axis=1)
     first, second, carry = intra_tail(*rest, frames, following, gains, wq, wk, wv)
-    pieces = exchanged(half, PLANE)
-    pieces, first, second, carry = lax.optimization_barrier((pieces, first, second, carry))
     carried = shifted(carry, 1)
-    piece = summed(pieces)
-    pieces = exchanged(copies(piece, 8), "z")
-    pieces, carried = lax.optimization_barrier((pieces, carried))
-    piece = summed(pieces)
+    sent = copies(summed(exchanged(half, PLANE)), 8)
+    sent, carried = lax.optimization_barrier((sent, carried))
+    piece = summed(exchanged(sent, "z"))
     whole = exchanged(copies(piece, 16), PLANE).reshape(16, 2, 32, D)
     other = swapped(whole)
     grad_frames, *weights = finish(

time: 127 us -> 124 us (0.976)
  blocking collectives: 13.1 us -> 25.3 us
  waiting for transfers between devices: 36.2 us -> 27.7 us
  starting transfers between devices: 45.3 us -> 41.3 us
  local copies, waits for them, and re-layouts: 3.58 us -> 0.81 us
    all_to_all x1 -> x2, blocking collectives: 13.1 us -> 25.3 us  [exchanged(): return lax.all_to_all(shard, axes, split_axis=0, concat_axis=0, tiled=True)]
    all_to_all x4 -> x3, waiting for transfers between devices: 29.1 us -> 22.9 us  [exchanged(): return lax.all_to_all(shard, axes, split_axis=0, concat_axis=0, tiled=True)]
    all_to_all x4 -> x3, starting transfers between devices: 29.7 us -> 26.3 us  [exchanged(): return lax.all_to_all(shard, axes, split_axis=0, concat_axis=0, tiled=True)]
    ppermute x2, waiting for transfers between devices: 4.44 us -> 2.11 us  [shifted(): return lax.ppermute(shard, TM, pairs)]
    unnamed x28 -> x30, local copies, waits for them, and re-layouts: 2.82 us -> 0.74 us
  transfers between devices with their start and end apart: 9 -> 8, of which waited for: 8 -> 6; matrix products, arithmetic and copies ran while one was open for 0% -> 0% of each run, Pallas kernels for 8% -> 8%
where the time goes in v4:
time: 124 us; the launch traced here: 123 us
  starting transfers between devices  41.3 us (33%)
  waiting for transfers between devices  27.7 us (22%)
  Pallas kernels  25.9 us (21%)
  blocking collectives  25.3 us (20%)
    all_to_all x3, starting transfers between devices, exchanged(): return lax.all_to_all(shard, axes, split_axis=0, concat_axis=0, tiled=True)  26.3 us
    all_to_all x2, blocking collectives, exchanged(): return lax.all_to_all(shard, axes, split_axis=0, concat_axis=0, tiled=True)  25.3 us
    all_to_all x3, waiting for transfers between devices, exchanged(): return lax.all_to_all(shard, axes, split_axis=0, concat_axis=0, tiled=True)  22.9 us
    ppermute x3, starting transfers between devices, swapped(): return lax.ppermute(shard, 'core', [(0, 1), (1, 0)])  11.2 us
    pallas_call x1, Pallas kernels, intra_prepare(): kernel_call(intra_prepare_kernel, 'intra_prepare', 3, [HBM] * 6, VMEM, bf...  5.04 us
    pallas_call x1, Pallas kernels, inter(): kernel_call(inter_kernel, 'inter', 5, [VMEM] * 6, [VMEM] * 7, (bf16(512,...  4.94 us
    pallas_call x1, Pallas kernels, intra_backward(): kernel_call(intra_backward_kernel, 'intra_backward', 4, [SMEM, VMEM] + [H...  4.72 us
    pallas_call x1, Pallas kernels, intra_second(): kernel_call(intra_second_kernel, 'intra_second', 3, [VMEM] * 5 + [HBM] *...  4.71 us
  transfers between devices with their start and end apart: 8, of which 6 were waited for; matrix products, arithmetic and copies ran while one was open for 0% of the time, Pallas kernels for 8%

profile of v4, /device:TPU:1, one launch (start us, length us, event | category | flops | bytes accessed | tf_op | source)
XLA Modules:
  0.0 122.9 jit_solution(10522190052178022007)
XLA Ops:
  0.6 0.0 copy-start.7
  0.6 0.0 copy-start.8
  0.7 1.4 %collective-permute-start = (bf16[256,256]{1,0:T(8,128)(2,1)}, bf16[256,256]{1,0:T(8,128)(2,1)S(1)}, u32[]{:S(2)}, u32[]{:S(2)}) collective-permute-start(bf16[256,256]{1,0:T(8,128)(2,1)} %bitcast.16), channel_id=1, source_target_pairs={{1,0},{2,1},{3,2},{4,3},{5,4},{6,5},{7,6},{8,7},{9,8},{10,9},{11,1... | collective-permute-start | bytes 393224 | tf_op jit(solution)/shard_map/ppermute | solution.py:705
  2.1 0.0 copy-start.12
  2.1 0.7 copy-done.12
  2.8 2.8 %intra_first.1 = (bf16[256,256]{1,0:T(8,128)(2,1)S(1)}, bf16[128,256]{1,0:T(8,128)(2,1)S(1)}, bf16[256,128]{1,0:T(8,128)(2,1)S(1)}, bf16[256,128]{1,0:T(8,128)(2,1)S(1)}) custom-call(bf16[256,256]{1,0:T(8,128)(2,1)} %bitcast.17, f32[2,256]{1,0:T(2,128)S(1)} %copy-done.12, bf16[2,256,256]{2,1,0:T(8,128)(2,1)} %wq_ref.3, bf16[2,256,256]{2,1,0:T(8,128)(2,1)} %wk_ref.3, ...), custom_call_target="tpu_custom_call" | custom-call | flops 1200000000 | bytes 1048576 | tf_op jit(solution)/shard_map/intra_first/pallas_call | solution.py:266
  5.6 2.1 %collective-permute-done.n_ref.n_any = bf16[256,256]{1,0:T(8,128)(2,1)S(1)} collective-permute-done((bf16[256,256]{1,0:T(8,128)(2,1)}, bf16[256,256]{1,0:T(8,128)(2,1)S(1)}, u32[]{:S(2)}, u32[]{:S(2)}) %collective-permute-start) | collective-permute-done | bytes 131104 | tf_op jit(solution)/shard_map/ppermute | solution.py:705
  7.7 0.0 copy-done.7
  7.7 0.0 copy-done.8
  7.7 0.0 copy-start.1
  7.8 0.0 copy-start.3
  7.8 0.0 copy-start.5
  7.8 0.0 copy-start.13
  7.8 4.7 %intra_second.1 = bf16[1536,128]{1,0:T(8,128)(2,1)} custom-call(bf16[256,256]{1,0:T(8,128)(2,1)S(1)} %collective-permute-done.n_ref.n_any, bf16[256,256]{1,0:T(8,128)(2,1)S(1)} %get-tuple-element.38.mid_in_ref, bf16[128,256]{1,0:T(8,128)(2,1)S(1)} %get-tuple-element.39.keys_ref, bf16[256,128]{1,0:T(8,128)(2,1)S(1)} %get-tuple-element.40.queries_ref, ...), custom_call_target="tpu_custom_call" | custom-call | flops 1200000000 | bytes 1048576 | tf_op jit(solution)/shard_map/intra_second/pallas_call | solution.py:275
  12.5 0.0 copy-done.10
  12.5 14.7 %all-to-all-start = ((bf16[64,24,128]{2,1,0:T(8,128)(2,1)}), bf16[64,24,128]{2,1,0:T(8,128)(2,1)S(1)}, u32[]{:S(2)}, u32[]{:S(2)}) async-start(bf16[64,24,128]{2,1,0:T(8,128)(2,1)} %bitcast.23), calls=%async_computation | async-start | bytes 786432 | tf_op jit(solution)/shard_map/all_to_all | solution.py:709
  27.2 13.4 %all-to-all-done = bf16[64,24,128]{2,1,0:T(8,128)(2,1)S(1)} async-done(((bf16[64,24,128]{2,1,0:T(8,128)(2,1)}), bf16[64,24,128]{2,1,0:T(8,128)(2,1)S(1)}, u32[]{:S(2)}, u32[]{:S(2)}) %all-to-all-start) | async-done | bytes 393248 | tf_op jit(solution)/shard_map/all_to_all | solution.py:709
  40.6 0.0 copy-done
  40.6 0.0 copy-done.1
  40.6 0.0 copy-done.3
  40.6 0.0 copy-done.5
  40.6 0.0 copy-done.13
  40.6 4.9 %inter.1 = (bf16[512,256]{1,0:T(8,128)(2,1)}, bf16[256,512]{1,0:T(8,128)(2,1)S(1)}, bf16[512,256]{1,0:T(8,128)(2,1)S(1)}, bf16[256,512]{1,0:T(8,128)(2,1)S(1)}, ...) custom-call(bf16[1536,128]{1,0:T(8,128)(2,1)S(1)} %bitcast.13, ...), custom_call_target="tpu_custom_call" | custom-call | flops 2000000000 | bytes 1048576 | tf_op jit(solution)/shard_map/inter/pallas_call | solution.py:380
  45.5 6.1 %all-to-all-start.1 = ((bf16[64,8,256]{2,1,0:T(8,128)(2,1)}), bf16[64,8,256]{2,1,0:T(8,128)(2,1)S(1)}, u32[]{:S(2)}, u32[]{:S(2)}) async-start(bf16[64,8,256]{2,1,0:T(8,128)(2,1)} %bitcast.5), calls=%async_computation.1 | async-start | bytes 524288 | tf_op jit(solution)/shard_map/all_to_all | solution.py:709
  51.6 0.5 inter_weights.1
  52.1 2.7 %collective-permute-start.1 = (bf16[2,256,256]{2,1,0:T(8,128)(2,1)S(1)}, bf16[2,256,256]{2,1,0:T(8,128)(2,1)S(1)}, u32[]{:S(2)}, u32[]{:S(2)}) collective-permute-start(bf16[2,256,256]{2,1,0:T(8,128)(2,1)S(1)} %get-tuple-element.50), channel_id=1, source_target_pairs={{0,64},{64,0},{1,65},{65,1},{2,66},{66,2},{3,67},{67,3},{4,68},{68... | collective-permute-start | bytes 786440 | tf_op jit(solution)/shard_map/ppermute | solution.py:713
  54.8 5.0 %intra_prepare.1.handed_any = bf16[5824,128]{1,0:T(8,128)(2,1)} custom-call(bf16[256,256]{1,0:T(8,128)(2,1)} %bitcast.18, bf16[256,256]{1,0:T(8,128)(2,1)} %copy-done.10, f32[2,256]{1,0:T(2,128)} %gain_ref.3, bf16[2,256,256]{2,1,0:T(8,128)(2,1)} %wq_ref.3, bf16[2,256,256]{2,1,0:T(8,128)(2,1)} %wk_ref.3, bf16[2,256,256]{2,1,0:T(8,128)(2,1)} %wv_ref.3), custom_call_target="tpu_custom_call" | custom-call | flops 1200000000 | bytes 1048576 | tf_op jit(solution)/shard_map/intra_prepare/pallas_call | solution.py:525
  59.8 0.0 collective-permute-done.1
  59.8 0.1 add_convert_fusion.1
  59.9 2.7 %all-to-all-done.1 = bf16[64,8,256]{2,1,0:T(8,128)(2,1)S(1)} async-done(((bf16[64,8,256]{2,1,0:T(8,128)(2,1)}), bf16[64,8,256]{2,1,0:T(8,128)(2,1)S(1)}, u32[]{:S(2)}, u32[]{:S(2)}) %all-to-all-start.1) | async-done | bytes 262176 | tf_op jit(solution)/shard_map/all_to_all | solution.py:709
  62.6 4.7 %intra_backward.1 = (f32[2,256,256]{2,1,0:T(8,128)S(1)}, bf16[2,256,256]{2,1,0:T(8,128)(2,1)S(1)}, bf16[2,256,256]{2,1,0:T(8,128)(2,1)S(1)}, bf16[2,256,256]{2,1...) custom-call(s32[1]{0:T(128)} %bitcast.core_ref, bf16[512,256]{1,0:T(8,128)(2,1)S(1)} %bitcast.14, ...), custom_call_target="tpu_custom_call" | custom-call | flops 1600000000 | bytes 1048576 | tf_op jit(solution)/shard_map/intra_backward/pallas_call | solution.py:622
  67.3 3.8 %collective-permute-start.2 = (bf16[2,256,256]{2,1,0:T(8,128)(2,1)S(1)}, bf16[2,256,256]{2,1,0:T(8,128)(2,1)S(1)}, u32[]{:S(2)}, u32[]{:S(2)}) collective-permute-start(bf16[2,256,256]{2,1,0:T(8,128)(2,1)S(1)} %get-tuple-element.53), channel_id=1, source_target_pairs={{0,64},{64,0},{1,65},{65,1},{2,66},{66,2},{3,67},{67,3},{4,68},{68... | collective-permute-start | bytes 786440 | tf_op jit(solution)/shard_map/ppermute | solution.py:713
  71.1 1.2 collective-permute-done.2
  72.3 0.0 copy-start.14
  72.3 0.1 add_convert_fusion
  72.4 0.8 pad_maximum_fusion
  73.2 5.6 %all-to-all-start.2 = ((bf16[16,64,256]{2,1,0:T(8,128)(2,1)}), bf16[16,64,256]{2,1,0:T(8,128)(2,1)S(1)}, u32[]{:S(2)}, u32[]{:S(2)}) async-start(bf16[16,64,256]{2,1,0:T(8,128)(2,1)} %pad_maximum_fusion), calls=%async_computation.2 | async-start | bytes 1048576 | tf_op jit(solution)/shard_map/all_to_all | solution.py:709
  78.8 0.0 copy-done.2
  78.9 1.5 %intra_tail.1 = (bf16[128,256]{1,0:T(8,128)(2,1)S(1)}, bf16[128,256]{1,0:T(8,128)(2,1)S(1)}, bf16[128,256]{1,0:T(8,128)(2,1)S(1)}) custom-call(bf16[2,256,256]{2,1,0:T(8,128)(2,1)S(1)} %get-tuple-element.55.grads_any, bf16[2,256,256]{2,1,0:T(8,128)(2,1)S(1)} %get-tuple-element.56.gq_t_any, bf16[2,256,256]{2,1,0:T(8,128)(2,1)S(1)} %get-tuple-element.57.gk_any, ...), custom_call_target="tpu_custom_call" | custom-call | flops 800000000 | bytes 1048576 | tf_op jit(solution)/shard_map/intra_tail/pallas_call | solution.py:659
  80.4 2.3 %collective-permute-start.3 = (bf16[128,256]{1,0:T(8,128)(2,1)S(1)}, bf16[128,256]{1,0:T(8,128)(2,1)S(1)}, u32[]{:S(2)}, u32[]{:S(2)}) collective-permute-start(bf16[128,256]{1,0:T(8,128)(2,1)S(1)} %get-tuple-element.59), channel_id=1, source_target_pairs={{0,1},{1,2},{2,3},{3,4},{4,5},{5,6},{6,7},{7,8},{8,9},{9,10},{10,1... | collective-permute-start | bytes 196616 | tf_op jit(solution)/shard_map/ppermute | solution.py:705
  82.8 6.8 %all-to-all-done.2 = bf16[16,64,256]{2,1,0:T(8,128)(2,1)S(1)} async-done(((bf16[16,64,256]{2,1,0:T(8,128)(2,1)}), bf16[16,64,256]{2,1,0:T(8,128)(2,1)S(1)}, u32[]{:S(2)}, u32[]{:S(2)}) %all-to-all-start.2) | async-done | bytes 524320 | tf_op jit(solution)/shard_map/all_to_all | solution.py:709
  89.5 0.1 reduce_sum.24
  89.6 0.0 collective-permute-done.3.carried_ref
  89.6 11.9 %all_to_all.25 = bf16[8,64,256]{2,1,0:T(8,128)(2,1)S(1)} all-to-all(bf16[8,64,256]{2,1,0:T(8,128)(2,1)S(1)} %broadcast_in_dim.6), channel_id=1, replica_groups=mesh['yh'=2,'core'=2,'yl'=2,'x'=4,'z'=8] {'z'}, dimensions={0} | all-to-all | bytes 524288 | tf_op jit(solution)/shard_map/all_to_all | solution.py:709
  101.6 13.4 %all_to_all.26 = bf16[16,64,256]{2,1,0:T(8,128)(2,1)S(1)} all-to-all(bf16[16,64,256]{2,1,0:T(8,128)(2,1)S(1)} %broadcast_in_dim.7), channel_id=1, replica_groups=mesh['yh'=2,'core'=2,'yl'=2,'x'=4,'z'=8] {'yh','yl','x'}, dimensions={0} | all-to-all | bytes 1048576 | tf_op jit(solution)/shard_map/all_to_all | solution.py:709
  115.0 4.7 %collective-permute-start.4 = (bf16[16,2,32,256]{3,2,1,0:T(8,128)(2,1)S(1)}, bf16[16,2,32,256]{3,2,1,0:T(8,128)(2,1)S(1)}, u32[]{:S(2)}, u32[]{:S(2)}) collective-permute-start(bf16[16,2,32,256]{3,2,1,0:T(8,128)(2,1)S(1)} %bitcast.11), channel_id=1, source_target_pairs={{0,64},{64,0},{1,65},{65,1},{2,66},{66,2},{3,67},{67,3},{4,68},{68... | collective-permute-start | bytes 1572872 | tf_op jit(solution)/shard_map/ppermute | solution.py:713
  119.8 1.5 %collective-permute-done.4.other_ref = bf16[16,2,32,256]{3,2,1,0:T(8,128)(2,1)S(1)} collective-permute-done((bf16[16,2,32,256]{3,2,1,0:T(8,128)(2,1)S(1)}, bf16[16,2,32,256]{3,2,1,0:T(8,128)(2,1)S(1)}, u32[]{:S(2)}, u32[]{:S(2)}) %collective-permute-start.4) | collective-permute-done | bytes 524320 | tf_op jit(solution)/shard_map/ppermute | solution.py:713
  121.3 1.6 %finish.1 = (bf16[256,256]{1,0:T(8,128)(2,1)}, f32[2,256,256]{2,1,0:T(8,128)}, f32[2,256,256]{2,1,0:T(8,128)}, f32[2,256,256]{2,1,0:T(8,128)}, f32[2,256,256]{2,1,0:T(8,128)}, /*index=5*/f32[2,256]{1,0:T(2,128)}) custom-call(s32[1]{0:T(128)} %bitcast.core_ref, bf16[16,2,32,256]{3,2,1,0:T(8,128)(2,1)S(1)} %bitcast.12, ...), custom_call_target="tpu_custom_call" | custom-call | flops 800000000 | bytes 1048576 | tf_op jit(solution)/shard_map/finish/pallas_call | solution.py:696
  (15 shorter events, 0.1 us)
Async XLA Ops:
  0.6 7.1 %copy-start.7 = (bf16[1,256,256]{2,1,0:T(8,128)(2,1)S(1)}, bf16[1,256,256]{2,1,0:T(8,128)(2,1)}, u32[]{:S(2)}) copy-start(bf16[1,256,256]{2,1,0:T(8,128)(2,1)} %param.8) | copy-start | bytes 393220
  0.6 7.1 %copy-start.8 = (bf16[1,256,256]{2,1,0:T(8,128)(2,1)S(1)}, bf16[1,256,256]{2,1,0:T(8,128)(2,1)}, u32[]{:S(2)}) copy-start(bf16[1,256,256]{2,1,0:T(8,128)(2,1)} %param.7) | copy-start | bytes 393220
  0.7 7.1 %collective-permute-start = (bf16[256,256]{1,0:T(8,128)(2,1)}, bf16[256,256]{1,0:T(8,128)(2,1)S(1)}, u32[]{:S(2)}, u32[]{:S(2)}) collective-permute-start(bf16[256,256]{1,0:T(8,128)(2,1)} %bitcast.16), channel_id=1, source_target_pairs={{1,0},{2,1},{3,2},{4,3},{5,4},{6,5},{7,6},{8,7},{9,8},{10,9},{11,1... | collective-permute-start | bytes 393224 | tf_op jit(solution)/shard_map/ppermute | solution.py:705
  2.1 0.7 copy-start.12
  7.7 4.8 %copy-start.10 = (bf16[256,256]{1,0:T(8,128)(2,1)}, bf16[256,256]{1,0:T(8,128)(2,1)S(1)}, u32[]{:S(2)}) copy-start(bf16[256,256]{1,0:T(8,128)(2,1)S(1)} %collective-permute-done.n_ref.n_any) | copy-start | bytes 393220
  7.7 32.8 %copy-start = (bf16[2,256,256]{2,1,0:T(8,128)(2,1)S(1)}, bf16[2,256,256]{2,1,0:T(8,128)(2,1)}, u32[]{:S(2)}) copy-start(bf16[2,256,256]{2,1,0:T(8,128)(2,1)} %wo_any.5) | copy-start | bytes 786436
  7.7 32.8 %copy-start.1 = (bf16[2,256,256]{2,1,0:T(8,128)(2,1)S(1)}, bf16[2,256,256]{2,1,0:T(8,128)(2,1)}, u32[]{:S(2)}) copy-start(bf16[2,256,256]{2,1,0:T(8,128)(2,1)} %wq_ref.3) | copy-start | bytes 786436
  7.8 32.8 %copy-start.3 = (bf16[2,256,256]{2,1,0:T(8,128)(2,1)S(1)}, bf16[2,256,256]{2,1,0:T(8,128)(2,1)}, u32[]{:S(2)}) copy-start(bf16[2,256,256]{2,1,0:T(8,128)(2,1)} %wk_ref.3) | copy-start | bytes 786436
  7.8 32.8 %copy-start.5 = (bf16[2,256,256]{2,1,0:T(8,128)(2,1)S(1)}, bf16[2,256,256]{2,1,0:T(8,128)(2,1)}, u32[]{:S(2)}) copy-start(bf16[2,256,256]{2,1,0:T(8,128)(2,1)} %wv_ref.3) | copy-start | bytes 786436
  7.8 32.8 %copy-start.13 = (f32[2,256]{1,0:T(2,128)S(1)}, f32[2,256]{1,0:T(2,128)}, u32[]{:S(2)}) copy-start(f32[2,256]{1,0:T(2,128)} %gain_ref.3) | copy-start | bytes 6148
  12.5 28.1 %all-to-all-start = ((bf16[64,24,128]{2,1,0:T(8,128)(2,1)}), bf16[64,24,128]{2,1,0:T(8,128)(2,1)S(1)}, u32[]{:S(2)}, u32[]{:S(2)}) async-start(bf16[64,24,128]{2,1,0:T(8,128)(2,1)} %bitcast.23), calls=%async_computation | async-start | bytes 786432 | tf_op jit(solution)/shard_map/all_to_all | solution.py:709
  45.5 17.1 %all-to-all-start.1 = ((bf16[64,8,256]{2,1,0:T(8,128)(2,1)}), bf16[64,8,256]{2,1,0:T(8,128)(2,1)S(1)}, u32[]{:S(2)}, u32[]{:S(2)}) async-start(bf16[64,8,256]{2,1,0:T(8,128)(2,1)} %bitcast.5), calls=%async_computation.1 | async-start | bytes 524288 | tf_op jit(solution)/shard_map/all_to_all | solution.py:709
  52.1 7.7 %collective-permute-start.1 = (bf16[2,256,256]{2,1,0:T(8,128)(2,1)S(1)}, bf16[2,256,256]{2,1,0:T(8,128)(2,1)S(1)}, u32[]{:S(2)}, u32[]{:S(2)}) collective-permute-start(bf16[2,256,256]{2,1,0:T(8,128)(2,1)S(1)} %get-tuple-element.50), channel_id=1, source_target_pairs={{0,64},{64,0},{1,65},{65,1},{2,66},{66,2},{3,67},{67,3},{4,68},{68... | collective-permute-start | bytes 786440 | tf_op jit(solution)/shard_map/ppermute | solution.py:713
  67.3 5.0 %collective-permute-start.2 = (bf16[2,256,256]{2,1,0:T(8,128)(2,1)S(1)}, bf16[2,256,256]{2,1,0:T(8,128)(2,1)S(1)}, u32[]{:S(2)}, u32[]{:S(2)}) collective-permute-start(bf16[2,256,256]{2,1,0:T(8,128)(2,1)S(1)} %get-tuple-element.53), channel_id=1, source_target_pairs={{0,64},{64,0},{1,65},{65,1},{2,66},{66,2},{3,67},{67,3},{4,68},{68... | collective-permute-start | bytes 786440 | tf_op jit(solution)/shard_map/ppermute | solution.py:713
  72.3 6.5 %copy-start.2 = (bf16[2,256,256]{2,1,0:T(8,128)(2,1)S(1)}, bf16[2,256,256]{2,1,0:T(8,128)(2,1)}, u32[]{:S(2)}) copy-start(bf16[2,256,256]{2,1,0:T(8,128)(2,1)} %wq_ref.3) | copy-start | bytes 786436
  72.3 6.5 %copy-start.4 = (bf16[2,256,256]{2,1,0:T(8,128)(2,1)S(1)}, bf16[2,256,256]{2,1,0:T(8,128)(2,1)}, u32[]{:S(2)}) copy-start(bf16[2,256,256]{2,1,0:T(8,128)(2,1)} %wk_ref.3) | copy-start | bytes 786436
  72.3 6.6 %copy-start.6 = (bf16[2,256,256]{2,1,0:T(8,128)(2,1)S(1)}, bf16[2,256,256]{2,1,0:T(8,128)(2,1)}, u32[]{:S(2)}) copy-start(bf16[2,256,256]{2,1,0:T(8,128)(2,1)} %wv_ref.3) | copy-start | bytes 786436
  72.3 6.6 %copy-start.9 = (bf16[1,256,256]{2,1,0:T(8,128)(2,1)S(1)}, bf16[1,256,256]{2,1,0:T(8,128)(2,1)}, u32[]{:S(2)}) copy-start(bf16[1,256,256]{2,1,0:T(8,128)(2,1)} %param.7) | copy-start | bytes 393220
  72.3 6.6 %copy-start.11 = (bf16[256,256]{1,0:T(8,128)(2,1)S(1)}, bf16[256,256]{1,0:T(8,128)(2,1)}, u32[]{:S(2)}) copy-start(bf16[256,256]{1,0:T(8,128)(2,1)} %copy-done.10) | copy-start | bytes 393220
  72.3 6.6 %copy-start.14 = (f32[2,256]{1,0:T(2,128)S(1)}, f32[2,256]{1,0:T(2,128)}, u32[]{:S(2)}) copy-start(f32[2,256]{1,0:T(2,128)} %gain_ref.3) | copy-start | bytes 6148
  73.2 16.3 %all-to-all-start.2 = ((bf16[16,64,256]{2,1,0:T(8,128)(2,1)}), bf16[16,64,256]{2,1,0:T(8,128)(2,1)S(1)}, u32[]{:S(2)}, u32[]{:S(2)}) async-start(bf16[16,64,256]{2,1,0:T(8,128)(2,1)} %pad_maximum_fusion), calls=%async_computation.2 | async-start | bytes 1048576 | tf_op jit(solution)/shard_map/all_to_all | solution.py:709
  80.4 9.2 %collective-permute-start.3 = (bf16[128,256]{1,0:T(8,128)(2,1)S(1)}, bf16[128,256]{1,0:T(8,128)(2,1)S(1)}, u32[]{:S(2)}, u32[]{:S(2)}) collective-permute-start(bf16[128,256]{1,0:T(8,128)(2,1)S(1)} %get-tuple-element.59), channel_id=1, source_target_pairs={{0,1},{1,2},{2,3},{3,4},{4,5},{5,6},{6,7},{7,8},{8,9},{9,10},{10,1... | collective-permute-start | bytes 196616 | tf_op jit(solution)/shard_map/ppermute | solution.py:705
  115.0 6.3 %collective-permute-start.4 = (bf16[16,2,32,256]{3,2,1,0:T(8,128)(2,1)S(1)}, bf16[16,2,32,256]{3,2,1,0:T(8,128)(2,1)S(1)}, u32[]{:S(2)}, u32[]{:S(2)}) collective-permute-start(bf16[16,2,32,256]{3,2,1,0:T(8,128)(2,1)S(1)} %bitcast.11), channel_id=1, source_target_pairs={{0,64},{64,0},{1,65},{65,1},{2,66},{66,2},{3,67},{67,3},{4,68},{68... | collective-permute-start | bytes 1572872 | tf_op jit(solution)/shard_map/ppermute | solution.py:713

commit v5 on v4

--- a/solution.py
+++ b/solution.py
@@ -24,10 +24,10 @@
 PREPARE_LIMIT = 56 * 1024 * 1024
 BACKWARD_LIMIT = 52850 * 1024
 
-AXES = ("yh", "core", "yl", "x", "z")
+AXES = ("yh", "core", "yl", "x", "za", "zb")
 DP = ("yh", "core")
-TM = ("yl", "x", "z")
-PLANE = ("yh", "yl", "x")
+TM = ("yl", "x", "za", "zb")
+PLANE = ("yh", "yl", "x", "zb")
 
 
 def dot(left, right, left_dim, right_dim):
@@ -94,23 +94,16 @@
 
 
 def packed_source(out):
-    device, row = out // 24, out % 24
-    part = row % 8
-    middle = (row // 8) * 128 + (part // 2) * 32 + device * 2 + part % 2
-    rest = row - 16
-    grads = 256 + (rest // 4) * 64 + ((rest % 4) // 2) * 32 + device * 2 + rest % 2
-    return jnp.where(row < 16, middle, grads)
-
-
-def unpacked_source(out):
-    column, place = out // 128, out % 128
-    segment = place % 32
-    middle = (segment // 2) * 24 + column * 8 + (segment % 2) * 4 + place // 32
-    rest = out - 256
-    column, place = rest // 64, rest % 64
-    segment = place % 32
-    grads = (segment // 2) * 24 + 16 + column * 4 + (segment % 2) * 2 + place // 32
-    return jnp.where(out < 256, middle, grads)
+    return ((out // 2) % 4) * 64 + (out // 8) * 2 + out % 2
+
+
+def middle_source(out):
+    return ((out % 64) // 2) * 8 + (out % 2) * 4 + out // 64
+
+
+def cotangent_source(out):
+    hop = out % 64
+    return (hop // 2) * 8 + (out // 128) * 4 + (hop % 2) * 2 + (out // 64) % 2
 
 
 def staged(count, *stages):
@@ -247,19 +240,17 @@
     rows = jnp.concatenate([f_ref[...].astype(F32), rows], axis=0)
     mids = (mid_in_ref[...], (rows + tn(ctx_ref[...], w_ref[3])).astype(BF))
     grads = grad_ref[...]
-    pick = select_rows(384, 384, packed_source)
-    for t in range(4):
-        middle = jnp.concatenate(
-            [mids[g][h * HOP + 32 * t : h * HOP + 32 * t + 32] for g in range(2) for h in range(2)],
-            axis=0,
-        )
-        cotangent = jnp.concatenate(
-            [grads[h * HOP + 32 * t : h * HOP + 32 * t + 32] for h in range(2)], axis=0
-        )
-        part = jnp.concatenate(
-            [middle[:, :128], middle[:, 128:], cotangent[:, :128], cotangent[:, 128:]], axis=0
-        )
-        packed_ref[384 * t : 384 * t + 384, :] = nn(pick, part).astype(BF)
+    pick = select_rows(256, 256, packed_source)
+    for t in range(2):
+        parts = []
+        for part in range(4):
+            high, low = part // 2, part % 2
+            at = slice(low * HOP + 64 * t, low * HOP + 64 * t + 64)
+            parts.append(
+                jnp.concatenate([mids[high][at], grads[at, 128 * high : 128 * high + 128]], axis=1)
+            )
+        rows = jnp.concatenate(parts, axis=0)
+        packed_ref[256 * t : 256 * t + 256, :] = nn(pick, rows).astype(BF)
 
 
 def intra_first(frames, gains, wq, wk, wv, wo):
@@ -274,7 +265,7 @@
 def intra_second(following, *rest):
     return kernel_call(
         intra_second_kernel, "intra_second", 3, [VMEM] * 5 + [HBM] * 7, VMEM,
-        bf16(64 * 24, 128),
+        bf16(512, 384),
         [
             vbf(HOP, D), vbf(K, D), pltpu.VMEM((2, D), F32), vbf(4, D, D), vbf(D, K), dma(7),
         ],
@@ -287,26 +278,20 @@
     out_ref, normed_t_ref, grads_ref, ctx_t, gq_t, gk_ref, gv_ref,
 ):
     gain = gain_ref[1:2, :]
-    pick = select_rows(384, 384, unpacked_source)
-    tiles = [nn(pick, packed_ref[384 * t : 384 * t + 384, :]) for t in range(4)]
+    pick = select_rows(256, 256, middle_source)
+    tiles = [nn(pick, packed_ref[256 * t : 256 * t + 256, :D]) for t in range(2)]
     rows = jnp.concatenate(
-        [
-            jnp.concatenate(
-                [tiles[t][c * 128 + 32 * p : c * 128 + 32 * p + 32] for c in range(2)], axis=1
-            )
-            for p in range(4)
-            for t in range(4)
-        ],
-        axis=0,
-    )
+        [tiles[t][64 * p : 64 * p + 64] for p in range(4) for t in range(2)], axis=0
+    )
+    pick = select_rows(256, 256, cotangent_source)
+    tiles = [nn(pick, packed_ref[256 * t : 256 * t + 256, D:]) for t in range(2)]
     hops = [
         jnp.concatenate(
             [
                 jnp.concatenate(
-                    [tiles[t][256 + c * 64 + 32 * r : 256 + c * 64 + 32 * r + 32] for c in range(2)],
-                    axis=1,
+                    [tiles[t][128 * c + 64 * r : 128 * c + 64 * r + 64] for c in range(2)], axis=1
                 )
-                for t in range(4)
+                for t in range(2)
             ],
             axis=0,
         )
@@ -713,16 +698,38 @@
     return lax.ppermute(shard, "core", [(0, 1), (1, 0)])
 
 
-def copies(piece, count):
-    return jnp.broadcast_to(piece[None], (count,) + piece.shape)
-
-
-def summed(pieces):
-    return jnp.sum(pieces.astype(F32), axis=0).astype(BF)
+def spread_kernel(pieces_ref, out_ref):
+    total = jnp.sum(pieces_ref[...].astype(F32), axis=0).astype(BF)
+    for i in range(out_ref.shape[0]):
+        out_ref[i] = total
+
+
+def spread(pieces, count):
+    return kernel_call(
+        spread_kernel, "spread", 1, [VMEM], VMEM, bf16(count, *pieces.shape[1:]), []
+    )(pieces)
+
+
+def core_sum_kernel(keep_ref, arrived_ref, out_ref):
+    out_ref[...] = (keep_ref[...] + arrived_ref[...].astype(F32)).astype(BF)
 
 
 def core_sum(keep, send):
-    return (keep + swapped(send).astype(F32)).astype(BF).reshape(16, 32, D)
+    return kernel_call(
+        core_sum_kernel, "core_sum", 1, [VMEM] * 2, VMEM, bf16(2, D, D), []
+    )(keep, swapped(send))
+
+
+def both_sums_kernel(keep_ref, arrived_ref, inter_ref, out_ref):
+    half = (keep_ref[...] + arrived_ref[...].astype(F32)).astype(BF)
+    out_ref[:, :16] = half.reshape(32, 16, D)
+    out_ref[:, 16:] = inter_ref[...].reshape(32, 16, D)
+
+
+def both_sums(keep, send, inter_half):
+    return kernel_call(
+        both_sums_kernel, "both_sums", 1, [VMEM] * 3, VMEM, bf16(32, 32, D), []
+    )(keep, swapped(send), inter_half)
 
 
 def shards(frames, frames_grad, wq, wk, wv, wo, gains):
@@ -733,20 +740,20 @@
     packed = intra_second(
         following, *front, frames, frames_grad[0], gains, wq, wk, wv, wo
     )
-    across = exchanged(packed.reshape(64, 24, 128), TM).reshape(64 * 24, 128)
+    across = exchanged(packed.reshape(64, 8, 384), TM).reshape(512, 384)
     grad_middle, *operands = inter(across, gains, wq, wk, wv, wo)
     grad_local = exchanged(grad_middle.reshape(64, 8, D), TM).reshape(512, D)
     inter_half = core_sum(*inter_weights(core, *operands))
     grad_local, inter_half = lax.optimization_barrier((grad_local, inter_half))
     handed = intra_prepare(frames, following, gains, wq, wk, wv)
     keep, send, *rest = intra_backward(core, grad_local, handed, wo)
-    half = jnp.concatenate([core_sum(keep, send), inter_half], axis=1)
+    half = both_sums(keep, send, inter_half)
     first, second, carry = intra_tail(*rest, frames, following, gains, wq, wk, wv)
     carried = shifted(carry, 1)
-    sent = copies(summed(exchanged(half, PLANE)), 8)
+    sent = spread(exchanged(half, PLANE), 4)
     sent, carried = lax.optimization_barrier((sent, carried))
-    piece = summed(exchanged(sent, "z"))
-    whole = exchanged(copies(piece, 16), PLANE).reshape(16, 2, 32, D)
+    sent = spread(exchanged(sent, "za"), 32)
+    whole = exchanged(sent, PLANE).reshape(32, 2, 16, D)
     other = swapped(whole)
     grad_frames, *weights = finish(
         core, whole, other, first, second, carried, gains, wq, wk, wv
@@ -755,7 +762,7 @@
 
 
 def solution(mesh):
-    split = Mesh(mesh.devices.reshape(2, 2, 2, 4, 8), AXES)
+    split = Mesh(mesh.devices.reshape(2, 2, 2, 4, 4, 2), AXES)
     placed = (P(DP, TM, None), P(DP, TM, None), P(), P(), P(), P(), P())
     return jax.shard_map(
         shards,

time: 124 us -> 121 us (0.976)
  blocking collectives: 25.3 us -> 51.1 us
  starting transfers between devices: 41.3 us -> 27.7 us
  waiting for transfers between devices: 27.7 us -> 14.2 us
    all_to_all x2 -> x3, blocking collectives: 25.3 us -> 51.1 us  [exchanged(): return lax.all_to_all(shard, axes, split_axis=0, concat_axis=0, tiled=True)]
    all_to_all x3 -> x2, starting transfers between devices: 26.3 us -> 12.1 us  [exchanged(): return lax.all_to_all(shard, axes, split_axis=0, concat_axis=0, tiled=True)]
    all_to_all x3 -> x2, waiting for transfers between devices: 22.9 us -> 9.37 us  [exchanged(): return lax.all_to_all(shard, axes, split_axis=0, concat_axis=0, tiled=True)]
  transfers between devices with their start and end apart: 8 -> 7, of which waited for: 6 -> 5; matrix products, arithmetic and copies ran while one was open for 0% -> 0% of each run, Pallas kernels for 8% -> 8%
where the time goes in v5:
time: 121 us; the launch traced here: 120 us
  blocking collectives  51.1 us (42%)
  starting transfers between devices  27.7 us (23%)
  Pallas kernels  25.7 us (21%)
  waiting for transfers between devices  14.2 us (12%)
    all_to_all x3, blocking collectives, exchanged(): return lax.all_to_all(shard, axes, split_axis=0, concat_axis=0, tiled=True)  51.1 us
    all_to_all x2, starting transfers between devices, exchanged(): return lax.all_to_all(shard, axes, split_axis=0, concat_axis=0, tiled=True)  12.1 us
    ppermute x3, starting transfers between devices, swapped(): return lax.ppermute(shard, 'core', [(0, 1), (1, 0)])  11.1 us
    all_to_all x2, waiting for transfers between devices, exchanged(): return lax.all_to_all(shard, axes, split_axis=0, concat_axis=0, tiled=True)  9.37 us
    pallas_call x1, Pallas kernels, intra_prepare(): kernel_call(intra_prepare_kernel, 'intra_prepare', 3, [HBM] * 6, VMEM, bf...  5.04 us
    pallas_call x1, Pallas kernels, intra_backward(): kernel_call(intra_backward_kernel, 'intra_backward', 4, [SMEM, VMEM] + [H...  4.72 us
    pallas_call x1, Pallas kernels, inter(): kernel_call(inter_kernel, 'inter', 5, [VMEM] * 6, [VMEM] * 7, (bf16(512,...  4.6 us
    ppermute x2, starting transfers between devices, shifted(): return lax.ppermute(shard, TM, pairs)  4.56 us
  transfers between devices with their start and end apart: 7, of which 5 were waited for; matrix products, arithmetic and copies ran while one was open for 0% of the time, Pallas kernels for 8%

profile of v5, /device:TPU:1, one launch (start us, length us, event | category | flops | bytes accessed | tf_op | source)
XLA Modules:
  0.0 120.4 jit_solution(17995996435422267335)
XLA Ops:
  0.6 0.0 copy-start.7
  0.6 0.0 copy-start.8
  0.7 1.4 %collective-permute-start = (bf16[256,256]{1,0:T(8,128)(2,1)}, bf16[256,256]{1,0:T(8,128)(2,1)S(1)}, u32[]{:S(2)}, u32[]{:S(2)}) collective-permute-start(bf16[256,256]{1,0:T(8,128)(2,1)} %bitcast.14), channel_id=1, source_target_pairs={{1,0},{2,1},{3,2},{4,3},{5,4},{6,5},{7,6},{8,7},{9,8},{10,9},{11,1... | collective-permute-start | bytes 393224 | tf_op jit(solution)/shard_map/ppermute | solution.py:690
  2.1 0.0 copy-start.12
  2.1 0.7 copy-done.12
  2.8 2.8 %intra_first.1 = (bf16[256,256]{1,0:T(8,128)(2,1)S(1)}, bf16[128,256]{1,0:T(8,128)(2,1)S(1)}, bf16[256,128]{1,0:T(8,128)(2,1)S(1)}, bf16[256,128]{1,0:T(8,128)(2,1)S(1)}) custom-call(bf16[256,256]{1,0:T(8,128)(2,1)} %bitcast.15, f32[2,256]{1,0:T(2,128)S(1)} %copy-done.12, bf16[2,256,256]{2,1,0:T(8,128)(2,1)} %wq_ref.3, bf16[2,256,256]{2,1,0:T(8,128)(2,1)} %wk_ref.3, ...), custom_call_target="tpu_custom_call" | custom-call | flops 1200000000 | bytes 1048576 | tf_op jit(solution)/shard_map/intra_first/pallas_call | solution.py:257
  5.6 2.1 %collective-permute-done.n_ref.n_any = bf16[256,256]{1,0:T(8,128)(2,1)S(1)} collective-permute-done((bf16[256,256]{1,0:T(8,128)(2,1)}, bf16[256,256]{1,0:T(8,128)(2,1)S(1)}, u32[]{:S(2)}, u32[]{:S(2)}) %collective-permute-start) | collective-permute-done | bytes 131104 | tf_op jit(solution)/shard_map/ppermute | solution.py:690
  7.7 0.0 copy-done.8
  7.7 0.0 copy-start.1
  7.8 0.0 copy-start.3
  7.8 0.0 copy-start.5
  7.8 3.8 %intra_second.1 = bf16[512,384]{1,0:T(8,128)(2,1)} custom-call(bf16[256,256]{1,0:T(8,128)(2,1)S(1)} %collective-permute-done.n_ref.n_any, bf16[256,256]{1,0:T(8,128)(2,1)S(1)} %get-tuple-element.38.mid_in_ref, bf16[128,256]{1,0:T(8,128)(2,1)S(1)} %get-tuple-element.39.keys_ref, bf16[256,128]{1,0:T(8,128)(2,1)S(1)} %get-tuple-element.40.queries_ref, ...), custom_call_target="tpu_custom_call" | custom-call | flops 1200000000 | bytes 1048576 | tf_op jit(solution)/shard_map/intra_second/pallas_call | solution.py:266
  11.6 28.0 %all_to_all.25 = bf16[64,8,384]{2,1,0:T(8,128)(2,1)S(1)} all-to-all(bf16[64,8,384]{2,1,0:T(8,128)(2,1)} %bitcast.19), channel_id=1, replica_groups=mesh['yh'=2,'core'=2,'yl'=2,'x'=4,'za'=4,'zb'=2] {'yl','x','za','zb'}, dimensions={0} | all-to-all | bytes 786432 | tf_op jit(solution)/shard_map/all_to_all | solution.py:694
  39.7 0.0 copy-done.5
  39.7 4.6 %inter.1 = (bf16[512,256]{1,0:T(8,128)(2,1)}, bf16[256,512]{1,0:T(8,128)(2,1)S(1)}, bf16[512,256]{1,0:T(8,128)(2,1)S(1)}, bf16[256,512]{1,0:T(8,128)(2,1)S(1)}, ...) custom-call(bf16[512,384]{1,0:T(8,128)(2,1)S(1)} %bitcast.11, ...), custom_call_target="tpu_custom_call" | custom-call | flops 2000000000 | bytes 1048576 | tf_op jit(solution)/shard_map/inter/pallas_call | solution.py:365
  44.3 6.1 %all-to-all-start.1 = ((bf16[64,8,256]{2,1,0:T(8,128)(2,1)}), bf16[64,8,256]{2,1,0:T(8,128)(2,1)S(1)}, u32[]{:S(2)}, u32[]{:S(2)}) async-start(bf16[64,8,256]{2,1,0:T(8,128)(2,1)} %bitcast.5), calls=%async_computation.1 | async-start | bytes 524288 | tf_op jit(solution)/shard_map/all_to_all | solution.py:694
  50.3 0.4 inter_weights.1
  50.8 2.7 %collective-permute-start.1 = (bf16[2,256,256]{2,1,0:T(8,128)(2,1)S(1)}, bf16[2,256,256]{2,1,0:T(8,128)(2,1)S(1)}, u32[]{:S(2)}, u32[]{:S(2)}) collective-permute-start(bf16[2,256,256]{2,1,0:T(8,128)(2,1)S(1)} %get-tuple-element.50), channel_id=1, source_target_pairs={{0,64},{64,0},{1,65},{65,1},{2,66},{66,2},{3,67},{67,3},{4,68},{68... | collective-permute-start | bytes 786440 | tf_op jit(solution)/shard_map/ppermute | solution.py:698
  53.5 5.0 %intra_prepare.1.handed_any = bf16[5824,128]{1,0:T(8,128)(2,1)} custom-call(bf16[256,256]{1,0:T(8,128)(2,1)} %bitcast.16, bf16[256,256]{1,0:T(8,128)(2,1)} %copy-done.10, f32[2,256]{1,0:T(2,128)} %gain_ref.3, bf16[2,256,256]{2,1,0:T(8,128)(2,1)} %wq_ref.3, bf16[2,256,256]{2,1,0:T(8,128)(2,1)} %wk_ref.3, bf16[2,256,256]{2,1,0:T(8,128)(2,1)} %wv_ref.3), custom_call_target="tpu_custom_call" | custom-call | flops 1200000000 | bytes 1048576 | tf_op jit(solution)/shard_map/intra_prepare/pallas_call | solution.py:510
  58.5 0.0 collective-permute-done.1.arrived_ref
  58.6 2.7 %all-to-all-done.1 = bf16[64,8,256]{2,1,0:T(8,128)(2,1)S(1)} async-done(((bf16[64,8,256]{2,1,0:T(8,128)(2,1)}), bf16[64,8,256]{2,1,0:T(8,128)(2,1)S(1)}, u32[]{:S(2)}, u32[]{:S(2)}) %all-to-all-start.1) | async-done | bytes 262176 | tf_op jit(solution)/shard_map/all_to_all | solution.py:694
  61.3 4.7 %intra_backward.1 = (f32[2,256,256]{2,1,0:T(8,128)S(1)}, bf16[2,256,256]{2,1,0:T(8,128)(2,1)S(1)}, bf16[2,256,256]{2,1,0:T(8,128)(2,1)S(1)}, bf16[2,256,256]{2,1...) custom-call(s32[1]{0:T(128)} %bitcast.core_ref, bf16[512,256]{1,0:T(8,128)(2,1)S(1)} %bitcast.12, ...), custom_call_target="tpu_custom_call" | custom-call | flops 1600000000 | bytes 1048576 | tf_op jit(solution)/shard_map/intra_backward/pallas_call | solution.py:607
  66.1 0.0 copy-start.2
  66.1 0.0 copy-start.4
  66.1 0.0 copy-start.6
  66.1 0.0 copy-start.9
  66.1 0.0 copy-start.11
  66.1 0.0 copy-start.13
  66.1 3.8 %collective-permute-start.2 = (bf16[2,256,256]{2,1,0:T(8,128)(2,1)S(1)}, bf16[2,256,256]{2,1,0:T(8,128)(2,1)S(1)}, u32[]{:S(2)}, u32[]{:S(2)}) collective-permute-start(bf16[2,256,256]{2,1,0:T(8,128)(2,1)S(1)} %get-tuple-element.53), channel_id=1, source_target_pairs={{0,64},{64,0},{1,65},{65,1},{2,66},{66,2},{3,67},{67,3},{4,68},{68... | collective-permute-start | bytes 786440 | tf_op jit(solution)/shard_map/ppermute | solution.py:698
  69.9 1.2 collective-permute-done.2.arrived_ref
  71.1 0.9 both_sums.1
  71.9 6.0 %all-to-all-start.2 = ((bf16[32,32,256]{2,1,0:T(8,128)(2,1)}), bf16[32,32,256]{2,1,0:T(8,128)(2,1)S(1)}, u32[]{:S(2)}, u32[]{:S(2)}) async-start(bf16[32,32,256]{2,1,0:T(8,128)(2,1)} %both_sums.1), calls=%async_computation.2 | async-start | bytes 1048576 | tf_op jit(solution)/shard_map/all_to_all | solution.py:694
  78.0 0.0 copy-done.2
  78.0 0.0 copy-done.4
  78.0 0.0 copy-done.6
  78.0 0.0 copy-done.9
  78.0 0.0 copy-done.11
  78.0 1.5 %intra_tail.1 = (bf16[128,256]{1,0:T(8,128)(2,1)S(1)}, bf16[128,256]{1,0:T(8,128)(2,1)S(1)}, bf16[128,256]{1,0:T(8,128)(2,1)S(1)}) custom-call(bf16[2,256,256]{2,1,0:T(8,128)(2,1)S(1)} %get-tuple-element.55.grads_any, bf16[2,256,256]{2,1,0:T(8,128)(2,1)S(1)} %get-tuple-element.56.gq_t_any, bf16[2,256,256]{2,1,0:T(8,128)(2,1)S(1)} %get-tuple-element.57.gk_any, ...), custom_call_target="tpu_custom_call" | custom-call | flops 800000000 | bytes 1048576 | tf_op jit(solution)/shard_map/intra_tail/pallas_call | solution.py:644
  79.6 3.1 %collective-permute-start.3 = (bf16[128,256]{1,0:T(8,128)(2,1)S(1)}, bf16[128,256]{1,0:T(8,128)(2,1)S(1)}, u32[]{:S(2)}, u32[]{:S(2)}) collective-permute-start(bf16[128,256]{1,0:T(8,128)(2,1)S(1)} %get-tuple-element.59), channel_id=1, source_target_pairs={{0,1},{1,2},{2,3},{3,4},{4,5},{5,6},{6,7},{7,8},{8,9},{9,10},{10,1... | collective-permute-start | bytes 196616 | tf_op jit(solution)/shard_map/ppermute | solution.py:690
  82.7 6.6 %all-to-all-done.2.pieces_ref = bf16[32,32,256]{2,1,0:T(8,128)(2,1)S(1)} async-done(((bf16[32,32,256]{2,1,0:T(8,128)(2,1)}), bf16[32,32,256]{2,1,0:T(8,128)(2,1)S(1)}, u32[]{:S(2)}, u32[]{:S(2)}) %all-to-all-start.2) | async-done | bytes 524320 | tf_op jit(solution)/shard_map/all_to_all | solution.py:694
  89.3 0.1 spread.2
  89.4 0.0 collective-permute-done.3.carried_ref
  89.4 9.3 %all_to_all.26.pieces_ref = bf16[4,32,256]{2,1,0:T(8,128)(2,1)S(1)} all-to-all(bf16[4,32,256]{2,1,0:T(8,128)(2,1)S(1)} %spread.2), channel_id=1, replica_groups=mesh['yh'=2,'core'=2,'yl'=2,'x'=4,'za'=4,'zb'=2] {'za'}, dimensions={0} | all-to-all | bytes 131072 | tf_op jit(solution)/shard_map/all_to_all | solution.py:694
  98.8 0.1 spread.3
  98.8 13.7 %all_to_all.27 = bf16[32,32,256]{2,1,0:T(8,128)(2,1)S(1)} all-to-all(bf16[32,32,256]{2,1,0:T(8,128)(2,1)S(1)} %spread.3), channel_id=1, replica_groups=mesh['yh'=2,'core'=2,'yl'=2,'x'=4,'za'=4,'zb'=2] {'yh','yl','x','zb'}, dimensions={0} | all-to-all | bytes 1048576 | tf_op jit(solution)/shard_map/all_to_all | solution.py:694
  112.5 4.6 %collective-permute-start.4 = (bf16[32,2,16,256]{3,2,1,0:T(8,128)(2,1)S(1)}, bf16[32,2,16,256]{3,2,1,0:T(8,128)(2,1)S(1)}, u32[]{:S(2)}, u32[]{:S(2)}) collective-permute-start(bf16[32,2,16,256]{3,2,1,0:T(8,128)(2,1)S(1)} %bitcast.9), channel_id=1, source_target_pairs={{0,64},{64,0},{1,65},{65,1},{2,66},{66,2},{3,67},{67,3},{4,68},{68... | collective-permute-start | bytes 1572872 | tf_op jit(solution)/shard_map/ppermute | solution.py:698
  117.2 1.5 %collective-permute-done.4.other_ref = bf16[32,2,16,256]{3,2,1,0:T(8,128)(2,1)S(1)} collective-permute-done((bf16[32,2,16,256]{3,2,1,0:T(8,128)(2,1)S(1)}, bf16[32,2,16,256]{3,2,1,0:T(8,128)(2,1)S(1)}, u32[]{:S(2)}, u32[]{:S(2)}) %collective-permute-start.4) | collective-permute-done | bytes 524320 | tf_op jit(solution)/shard_map/ppermute | solution.py:698
  118.7 1.7 %finish.1 = (bf16[256,256]{1,0:T(8,128)(2,1)}, f32[2,256,256]{2,1,0:T(8,128)}, f32[2,256,256]{2,1,0:T(8,128)}, f32[2,256,256]{2,1,0:T(8,128)}, f32[2,256,256]{2,1,0:T(8,128)}, /*index=5*/f32[2,256]{1,0:T(2,128)}) custom-call(s32[1]{0:T(128)} %bitcast.core_ref, bf16[32,2,16,256]{3,2,1,0:T(8,128)(2,1)S(1)} %bitcast.10, ...), custom_call_target="tpu_custom_call" | custom-call | flops 800000000 | bytes 1048576 | tf_op jit(solution)/shard_map/finish/pallas_call | solution.py:681
  (9 shorter events, 0.1 us)
Async XLA Ops:
  0.6 7.1 %copy-start.7 = (bf16[1,256,256]{2,1,0:T(8,128)(2,1)S(1)}, bf16[1,256,256]{2,1,0:T(8,128)(2,1)}, u32[]{:S(2)}) copy-start(bf16[1,256,256]{2,1,0:T(8,128)(2,1)} %param.8) | copy-start | bytes 393220
  0.6 7.1 %copy-start.8 = (bf16[1,256,256]{2,1,0:T(8,128)(2,1)S(1)}, bf16[1,256,256]{2,1,0:T(8,128)(2,1)}, u32[]{:S(2)}) copy-start(bf16[1,256,256]{2,1,0:T(8,128)(2,1)} %param.7) | copy-start | bytes 393220
  0.7 7.1 %collective-permute-start = (bf16[256,256]{1,0:T(8,128)(2,1)}, bf16[256,256]{1,0:T(8,128)(2,1)S(1)}, u32[]{:S(2)}, u32[]{:S(2)}) collective-permute-start(bf16[256,256]{1,0:T(8,128)(2,1)} %bitcast.14), channel_id=1, source_target_pairs={{1,0},{2,1},{3,2},{4,3},{5,4},{6,5},{7,6},{8,7},{9,8},{10,9},{11,1... | collective-permute-start | bytes 393224 | tf_op jit(solution)/shard_map/ppermute | solution.py:690
  2.1 0.7 copy-start.12
  7.7 3.9 %copy-start.10 = (bf16[256,256]{1,0:T(8,128)(2,1)}, bf16[256,256]{1,0:T(8,128)(2,1)S(1)}, u32[]{:S(2)}) copy-start(bf16[256,256]{1,0:T(8,128)(2,1)S(1)} %collective-permute-done.n_ref.n_any) | copy-start | bytes 393220
  7.7 31.9 %copy-start = (bf16[2,256,256]{2,1,0:T(8,128)(2,1)S(1)}, bf16[2,256,256]{2,1,0:T(8,128)(2,1)}, u32[]{:S(2)}) copy-start(bf16[2,256,256]{2,1,0:T(8,128)(2,1)} %wo_any.5) | copy-start | bytes 786436
  7.7 31.9 %copy-start.1 = (bf16[2,256,256]{2,1,0:T(8,128)(2,1)S(1)}, bf16[2,256,256]{2,1,0:T(8,128)(2,1)}, u32[]{:S(2)}) copy-start(bf16[2,256,256]{2,1,0:T(8,128)(2,1)} %wq_ref.3) | copy-start | bytes 786436
  7.8 31.9 %copy-start.3 = (bf16[2,256,256]{2,1,0:T(8,128)(2,1)S(1)}, bf16[2,256,256]{2,1,0:T(8,128)(2,1)}, u32[]{:S(2)}) copy-start(bf16[2,256,256]{2,1,0:T(8,128)(2,1)} %wk_ref.3) | copy-start | bytes 786436
  7.8 31.9 %copy-start.5 = (bf16[2,256,256]{2,1,0:T(8,128)(2,1)S(1)}, bf16[2,256,256]{2,1,0:T(8,128)(2,1)}, u32[]{:S(2)}) copy-start(bf16[2,256,256]{2,1,0:T(8,128)(2,1)} %wv_ref.3) | copy-start | bytes 786436
  44.3 17.1 %all-to-all-start.1 = ((bf16[64,8,256]{2,1,0:T(8,128)(2,1)}), bf16[64,8,256]{2,1,0:T(8,128)(2,1)S(1)}, u32[]{:S(2)}, u32[]{:S(2)}) async-start(bf16[64,8,256]{2,1,0:T(8,128)(2,1)} %bitcast.5), calls=%async_computation.1 | async-start | bytes 524288 | tf_op jit(solution)/shard_map/all_to_all | solution.py:694
  50.8 7.7 %collective-permute-start.1 = (bf16[2,256,256]{2,1,0:T(8,128)(2,1)S(1)}, bf16[2,256,256]{2,1,0:T(8,128)(2,1)S(1)}, u32[]{:S(2)}, u32[]{:S(2)}) collective-permute-start(bf16[2,256,256]{2,1,0:T(8,128)(2,1)S(1)} %get-tuple-element.50), channel_id=1, source_target_pairs={{0,64},{64,0},{1,65},{65,1},{2,66},{66,2},{3,67},{67,3},{4,68},{68... | collective-permute-start | bytes 786440 | tf_op jit(solution)/shard_map/ppermute | solution.py:698
  66.1 11.9 %copy-start.2 = (bf16[2,256,256]{2,1,0:T(8,128)(2,1)S(1)}, bf16[2,256,256]{2,1,0:T(8,128)(2,1)}, u32[]{:S(2)}) copy-start(bf16[2,256,256]{2,1,0:T(8,128)(2,1)} %wq_ref.3) | copy-start | bytes 786436
  66.1 11.9 %copy-start.4 = (bf16[2,256,256]{2,1,0:T(8,128)(2,1)S(1)}, bf16[2,256,256]{2,1,0:T(8,128)(2,1)}, u32[]{:S(2)}) copy-start(bf16[2,256,256]{2,1,0:T(8,128)(2,1)} %wk_ref.3) | copy-start | bytes 786436
  66.1 11.9 %copy-start.6 = (bf16[2,256,256]{2,1,0:T(8,128)(2,1)S(1)}, bf16[2,256,256]{2,1,0:T(8,128)(2,1)}, u32[]{:S(2)}) copy-start(bf16[2,256,256]{2,1,0:T(8,128)(2,1)} %wv_ref.3) | copy-start | bytes 786436
  66.1 11.9 %copy-start.9 = (bf16[1,256,256]{2,1,0:T(8,128)(2,1)S(1)}, bf16[1,256,256]{2,1,0:T(8,128)(2,1)}, u32[]{:S(2)}) copy-start(bf16[1,256,256]{2,1,0:T(8,128)(2,1)} %param.7) | copy-start | bytes 393220
  66.1 11.9 %copy-start.11 = (bf16[256,256]{1,0:T(8,128)(2,1)S(1)}, bf16[256,256]{1,0:T(8,128)(2,1)}, u32[]{:S(2)}) copy-start(bf16[256,256]{1,0:T(8,128)(2,1)} %copy-done.10) | copy-start | bytes 393220
  66.1 11.9 %copy-start.13 = (f32[2,256]{1,0:T(2,128)S(1)}, f32[2,256]{1,0:T(2,128)}, u32[]{:S(2)}) copy-start(f32[2,256]{1,0:T(2,128)} %gain_ref.3) | copy-start | bytes 6148
  66.1 4.9 %collective-permute-start.2 = (bf16[2,256,256]{2,1,0:T(8,128)(2,1)S(1)}, bf16[2,256,256]{2,1,0:T(8,128)(2,1)S(1)}, u32[]{:S(2)}, u32[]{:S(2)}) collective-permute-start(bf16[2,256,256]{2,1,0:T(8,128)(2,1)S(1)} %get-tuple-element.53), channel_id=1, source_target_pairs={{0,64},{64,0},{1,65},{65,1},{2,66},{66,2},{3,67},{67,3},{4,68},{68... | collective-permute-start | bytes 786440 | tf_op jit(solution)/shard_map/ppermute | solution.py:698
  71.9 17.4 %all-to-all-start.2 = ((bf16[32,32,256]{2,1,0:T(8,128)(2,1)}), bf16[32,32,256]{2,1,0:T(8,128)(2,1)S(1)}, u32[]{:S(2)}, u32[]{:S(2)}) async-start(bf16[32,32,256]{2,1,0:T(8,128)(2,1)} %both_sums.1), calls=%async_computation.2 | async-start | bytes 1048576 | tf_op jit(solution)/shard_map/all_to_all | solution.py:694
  79.6 9.9 %collective-permute-start.3 = (bf16[128,256]{1,0:T(8,128)(2,1)S(1)}, bf16[128,256]{1,0:T(8,128)(2,1)S(1)}, u32[]{:S(2)}, u32[]{:S(2)}) collective-permute-start(bf16[128,256]{1,0:T(8,128)(2,1)S(1)} %get-tuple-element.59), channel_id=1, source_target_pairs={{0,1},{1,2},{2,3},{3,4},{4,5},{5,6},{6,7},{7,8},{8,9},{9,10},{10,1... | collective-permute-start | bytes 196616 | tf_op jit(solution)/shard_map/ppermute | solution.py:690
  112.5 6.2 %collective-permute-start.4 = (bf16[32,2,16,256]{3,2,1,0:T(8,128)(2,1)S(1)}, bf16[32,2,16,256]{3,2,1,0:T(8,128)(2,1)S(1)}, u32[]{:S(2)}, u32[]{:S(2)}) collective-permute-start(bf16[32,2,16,256]{3,2,1,0:T(8,128)(2,1)S(1)} %bitcast.9), channel_id=1, source_target_pairs={{0,64},{64,0},{1,65},{65,1},{2,66},{66,2},{3,67},{67,3},{4,68},{68... | collective-permute-start | bytes 1572872 | tf_op jit(solution)/shard_map/ppermute | solution.py:698

commit v6 on v5

--- a/solution.py
+++ b/solution.py
@@ -21,7 +21,6 @@
 VMEM_LIMIT = 16 * 1024 * 1024
 FIRST_LIMIT = 54800 * 1024
 SECOND_LIMIT = 54300 * 1024
-PREPARE_LIMIT = 56 * 1024 * 1024
 BACKWARD_LIMIT = 52850 * 1024
 
 AXES = ("yh", "core", "yl", "x", "za", "zb")
@@ -317,19 +316,19 @@
     downs = row_masks()
 
     def place(step):
-        p, b = step // 2, step % 2
-        return slice(128 * p, 128 * p + 128), slice(128 * b, 128 * b + 128)
-
-    def columns(rows_t):
-        return jnp.concatenate([rows_t * down for down in downs], axis=1)
-
-    def stacked(rows):
-        return jnp.concatenate([rows * mask for mask in masks], axis=0)
+        p, b, pair = step // 4, (step // 2) % 2, step % 2
+        return slice(128 * p, 128 * p + 128), slice(128 * b, 128 * b + 128), pair
+
+    def columns(rows_t, pair):
+        return jnp.concatenate([rows_t * downs[2 * pair], rows_t * downs[2 * pair + 1]], axis=1)
+
+    def stacked(rows, pair):
+        return jnp.concatenate([rows * masks[2 * pair], rows * masks[2 * pair + 1]], axis=0)
 
     def products(step):
-        at, block = place(step)
-        scores = nn(keys[at, block], columns(queries_t[block, at]))
-        grad_probs = nn(values[at, block], columns(grad_context_t[block, at]))
+        at, block, pair = place(step)
+        scores = nn(keys[at, block], columns(queries_t[block, at], pair))
+        grad_probs = nn(values[at, block], columns(grad_context_t[block, at], pair))
         return scores, grad_probs
 
     def weigh(step, held):
@@ -338,18 +337,25 @@
         inner = jnp.sum(grad_probs * probs, axis=0, keepdims=True)
         return probs.astype(BF), (probs * (grad_probs - inner) * SCALE).astype(BF)
 
+    sums = {}
+
     def collect(step, held):
         low, grad_scores = held
-        at, block = place(step)
-        gv_ref[at, block] = nn(low, stacked(grad_context[at, block])).astype(BF)
-        gk_ref[at, block] = nn(grad_scores, stacked(queries[at, block])).astype(BF)
-        for i in range(4):
-            feats = slice(block.start + HEAD * i, block.start + HEAD * i + HEAD)
-            cols = slice(128 * i, 128 * i + 128)
-            ctx_t[feats, at] = nn(values_t[feats, at], low[:, cols]).astype(BF)
-            gq_t[feats, at] = nn(keys_t[feats, at], grad_scores[:, cols]).astype(BF)
-
-    staged(8, products, weigh, collect)
+        at, block, pair = place(step)
+        gv = nn(low, stacked(grad_context[at, block], pair))
+        gk = nn(grad_scores, stacked(queries[at, block], pair))
+        if pair == 0:
+            sums["v"], sums["k"] = gv, gk
+        else:
+            gv_ref[at, block] = (sums["v"] + gv).astype(BF)
+            gk_ref[at, block] = (sums["k"] + gk).astype(BF)
+        start = block.start + 64 * pair
+        for target, rows_t, right in ((ctx_t, values_t, low), (gq_t, keys_t, grad_scores)):
+            both = nn(rows_t[start : start + 64, at], right)
+            target[start : start + 32, at] = both[:32, :128].astype(BF)
+            target[start + 32 : start + 64, at] = both[32:, 128:].astype(BF)
+
+    staged(16, products, weigh, collect)
     gqt, gk, gv = gq_t[...], gk_ref[...], gv_ref[...]
     grad_normed = nt(gqt.T, wq) + nt(gk, wk) + nt(gv, wv)
     result = (grads.astype(F32) + norm_pullback(grad_normed, unit, inverse, gain)).astype(BF)
@@ -462,15 +468,14 @@
 
 
 def intra_prepare_kernel(
-    f_any, n_any, gain_any, wq_any, wk_any, wv_any, handed_ref,
-    stats_ref, ctx_ref, rows_ref, gain_ref, w_ref, sems,
+    f_ref, n_ref, gain_ref, wq_ref, wk_ref, wv_ref, handed_ref, stats_ref, ctx_ref
 ):
-    settle(begin_layer(sems, f_any, n_any, gain_any, wq_any, wk_any, wv_any, rows_ref, gain_ref, w_ref))
-    unit, _ = standardize(rows_ref[...].astype(F32))
+    rows = jnp.concatenate([f_ref[...], n_ref[:HOP]], axis=0)
+    unit, _ = standardize(rows.astype(F32))
     normed = (unit * gain_ref[0:1, :]).astype(BF)
-    queries = nn(normed, w_ref[0]).astype(BF)
-    keys = nn(normed, w_ref[1]).astype(BF)
-    values = nn(normed, w_ref[2]).astype(BF)
+    queries = nn(normed, wq_ref[0]).astype(BF)
+    keys = nn(normed, wk_ref[0]).astype(BF)
+    values = nn(normed, wv_ref[0]).astype(BF)
     queries_t = queries.T
     values_t = values.T
     put_blocks(handed_ref, NORMED_T, normed.T)
@@ -508,9 +513,8 @@
 
 def intra_prepare(frames, following, gains, wq, wk, wv):
     return kernel_call(
-        intra_prepare_kernel, "intra_prepare", 3, [HBM] * 6, VMEM, bf16(HANDED_ROWS, 128),
-        [pltpu.VMEM((4 * HEADS, K), F32), vbf(2, D, K)] + layer_scratch() + [dma(6)],
-        PREPARE_LIMIT,
+        intra_prepare_kernel, "intra_prepare", 3, [VMEM] * 6, VMEM, bf16(HANDED_ROWS, 128),
+        [pltpu.VMEM((4 * HEADS, K), F32), vbf(2, D, K)],
     )(frames, following, gains, wq, wk, wv)
 
 

time: 121 us -> 120 us (level)
  Pallas kernels: 25.7 us -> 23 us
    pallas_call x1, Pallas kernels: 5.04 us -> 2.72 us  [intra_prepare(): kernel_call(intra_prepare_kernel, 'intra_prepare', 3, [VMEM] * 6, VMEM, b...]
    all_to_all x2, waiting for transfers between devices: 9.37 us -> 10.6 us  [exchanged(): return lax.all_to_all(shard, axes, split_axis=0, concat_axis=0, tiled=True)]
  transfers between devices with their start and end apart: 7 -> 7, of which waited for: 5 -> 5; matrix products, arithmetic and copies ran while one was open for 0% -> 0% of each run, Pallas kernels for 8% -> 6%
where the time goes in v6:
time: 120 us
  blocking collectives  51 us (42%)
  starting transfers between devices  27.8 us (23%)
  Pallas kernels  23 us (19%)
  waiting for transfers between devices  15.4 us (13%)
  local copies, waits for them, and re-layouts  1.86 us (2%)
    all_to_all x3, blocking collectives, exchanged(): return lax.all_to_all(shard, axes, split_axis=0, concat_axis=0, tiled=True)  51 us
    all_to_all x2, starting transfers between devices, exchanged(): return lax.all_to_all(shard, axes, split_axis=0, concat_axis=0, tiled=True)  12.2 us
    ppermute x3, starting transfers between devices, swapped(): return lax.ppermute(shard, 'core', [(0, 1), (1, 0)])  11.1 us
    all_to_all x2, waiting for transfers between devices, exchanged(): return lax.all_to_all(shard, axes, split_axis=0, concat_axis=0, tiled=True)  10.6 us
    pallas_call x1, Pallas kernels, intra_backward(): kernel_call(intra_backward_kernel, 'intra_backward', 4, [SMEM, VMEM] + [H...  4.72 us
    ppermute x2, starting transfers between devices, shifted(): return lax.ppermute(shard, TM, pairs)  4.56 us
    pallas_call x1, Pallas kernels, inter(): kernel_call(inter_kernel, 'inter', 5, [VMEM] * 6, [VMEM] * 7, (bf16(512,...  4.21 us
    pallas_call x1, Pallas kernels, intra_second(): kernel_call(intra_second_kernel, 'intra_second', 3, [VMEM] * 5 + [HBM] *...  3.8 us
  transfers between devices with their start and end apart: 7, of which 5 were waited for; matrix products, arithmetic and copies ran while one was open for 0% of the time, Pallas kernels for 6%

profile of v6, /device:TPU:1, one launch (start us, length us, event | category | flops | bytes accessed | tf_op | source)
XLA Modules:
  0.0 119.9 jit_solution(9274857338411419032)
XLA Ops:
  0.6 0.0 copy-start.4
  0.6 0.0 copy-start.5
  0.7 1.4 %collective-permute-start = (bf16[256,256]{1,0:T(8,128)(2,1)}, bf16[256,256]{1,0:T(8,128)(2,1)S(1)}, u32[]{:S(2)}, u32[]{:S(2)}) collective-permute-start(bf16[256,256]{1,0:T(8,128)(2,1)} %bitcast.14), channel_id=1, source_target_pairs={{1,0},{2,1},{3,2},{4,3},{5,4},{6,5},{7,6},{8,7},{9,8},{10,9},{11,1... | collective-permute-start | bytes 393224 | tf_op jit(solution)/shard_map/ppermute | solution.py:694
  2.1 0.0 copy-start.6
  2.1 0.7 copy-done.6
  2.8 2.8 %intra_first.1 = (bf16[256,256]{1,0:T(8,128)(2,1)S(1)}, bf16[128,256]{1,0:T(8,128)(2,1)S(1)}, bf16[256,128]{1,0:T(8,128)(2,1)S(1)}, bf16[256,128]{1,0:T(8,128)(2,1)S(1)}) custom-call(bf16[256,256]{1,0:T(8,128)(2,1)} %bitcast.15, f32[2,256]{1,0:T(2,128)S(1)} %copy-done.6, bf16[2,256,256]{2,1,0:T(8,128)(2,1)} %wq_ref.5, bf16[2,256,256]{2,1,0:T(8,128)(2,1)} %wk_ref.5, ...), custom_call_target="tpu_custom_call" | custom-call | flops 1200000000 | bytes 1048576 | tf_op jit(solution)/shard_map/intra_first/pallas_call | solution.py:256
  5.6 2.1 %collective-permute-done.n_ref.n_any = bf16[256,256]{1,0:T(8,128)(2,1)S(1)} collective-permute-done((bf16[256,256]{1,0:T(8,128)(2,1)}, bf16[256,256]{1,0:T(8,128)(2,1)S(1)}, u32[]{:S(2)}, u32[]{:S(2)}) %collective-permute-start) | collective-permute-done | bytes 131104 | tf_op jit(solution)/shard_map/ppermute | solution.py:694
  7.7 0.0 copy-done.4
  7.7 0.0 copy-done.5
  7.7 0.0 copy-start
  7.7 0.0 copy-start.1
  7.7 0.0 copy-start.2
  7.7 0.0 copy-start.3
  7.8 3.8 %intra_second.1 = bf16[512,384]{1,0:T(8,128)(2,1)} custom-call(bf16[256,256]{1,0:T(8,128)(2,1)S(1)} %collective-permute-done.n_ref.n_any, bf16[256,256]{1,0:T(8,128)(2,1)S(1)} %get-tuple-element.38.mid_in_ref, bf16[128,256]{1,0:T(8,128)(2,1)S(1)} %get-tuple-element.39.keys_ref, bf16[256,128]{1,0:T(8,128)(2,1)S(1)} %get-tuple-element.40.queries_ref, ...), custom_call_target="tpu_custom_call" | custom-call | flops 1200000000 | bytes 1048576 | tf_op jit(solution)/shard_map/intra_second/pallas_call | solution.py:265
  11.6 28.0 %all_to_all.25 = bf16[64,8,384]{2,1,0:T(8,128)(2,1)S(1)} all-to-all(bf16[64,8,384]{2,1,0:T(8,128)(2,1)} %bitcast.19), channel_id=1, replica_groups=mesh['yh'=2,'core'=2,'yl'=2,'x'=4,'za'=4,'zb'=2] {'yl','x','za','zb'}, dimensions={0} | all-to-all | bytes 786432 | tf_op jit(solution)/shard_map/all_to_all | solution.py:698
  39.6 0.0 copy-done
  39.6 0.0 copy-done.1
  39.6 0.0 copy-done.2
  39.6 0.0 copy-done.3
  39.6 4.2 %inter.1 = (bf16[512,256]{1,0:T(8,128)(2,1)}, bf16[256,512]{1,0:T(8,128)(2,1)S(1)}, bf16[512,256]{1,0:T(8,128)(2,1)S(1)}, bf16[256,512]{1,0:T(8,128)(2,1)S(1)}, ...) custom-call(bf16[512,384]{1,0:T(8,128)(2,1)S(1)} %bitcast.11, ...), custom_call_target="tpu_custom_call" | custom-call | flops 2000000000 | bytes 1048576 | tf_op jit(solution)/shard_map/inter/pallas_call | solution.py:371
  43.8 0.0 copy-start.7
  43.8 6.2 %all-to-all-start.1 = ((bf16[64,8,256]{2,1,0:T(8,128)(2,1)}), bf16[64,8,256]{2,1,0:T(8,128)(2,1)S(1)}, u32[]{:S(2)}, u32[]{:S(2)}) async-start(bf16[64,8,256]{2,1,0:T(8,128)(2,1)} %bitcast.5), calls=%async_computation.1 | async-start | bytes 524288 | tf_op jit(solution)/shard_map/all_to_all | solution.py:698
  50.1 0.4 inter_weights.1
  50.5 2.7 %collective-permute-start.1 = (bf16[2,256,256]{2,1,0:T(8,128)(2,1)S(1)}, bf16[2,256,256]{2,1,0:T(8,128)(2,1)S(1)}, u32[]{:S(2)}, u32[]{:S(2)}) collective-permute-start(bf16[2,256,256]{2,1,0:T(8,128)(2,1)S(1)} %get-tuple-element.50), channel_id=1, source_target_pairs={{0,64},{64,0},{1,65},{65,1},{2,66},{66,2},{3,67},{67,3},{4,68},{68... | collective-permute-start | bytes 786440 | tf_op jit(solution)/shard_map/ppermute | solution.py:702
  53.2 0.0 copy-done.7
  53.2 2.7 %intra_prepare.1.handed_any = bf16[5824,128]{1,0:T(8,128)(2,1)S(1)} custom-call(bf16[256,256]{1,0:T(8,128)(2,1)S(1)} %bitcast.17, bf16[256,256]{1,0:T(8,128)(2,1)S(1)} %collective-permute-done.n_ref.n_any, f32[2,256]{1,0:T(2,128)S(1)} %copy-done.7, bf16[2,256,256]{2,1,0:T(8,128)(2,1)S(1)} %copy-done.1, bf16[2,256,256]{2,1,0:T(8,128)(2,1)S(1)} %copy-done.2, ...), custom_call_target="tpu_custom_call" | custom-call | flops 1200000000 | bytes 1048576 | tf_op jit(solution)/shard_map/intra_prepare/pallas_call | solution.py:515
  55.9 0.0 copy-start.8
  55.9 1.1 copy-done.8
  57.1 0.0 collective-permute-done.1.arrived_ref
  57.1 0.1 core_sum.1.inter_ref
  57.1 3.9 %all-to-all-done.1 = bf16[64,8,256]{2,1,0:T(8,128)(2,1)S(1)} async-done(((bf16[64,8,256]{2,1,0:T(8,128)(2,1)}), bf16[64,8,256]{2,1,0:T(8,128)(2,1)S(1)}, u32[]{:S(2)}, u32[]{:S(2)}) %all-to-all-start.1) | async-done | bytes 262176 | tf_op jit(solution)/shard_map/all_to_all | solution.py:698
  61.1 4.7 %intra_backward.1 = (f32[2,256,256]{2,1,0:T(8,128)S(1)}, bf16[2,256,256]{2,1,0:T(8,128)(2,1)S(1)}, bf16[2,256,256]{2,1,0:T(8,128)(2,1)S(1)}, bf16[2,256,256]{2,1...) custom-call(s32[1]{0:T(128)} %bitcast.core_ref, bf16[512,256]{1,0:T(8,128)(2,1)S(1)} %bitcast.12, ...), custom_call_target="tpu_custom_call" | custom-call | flops 1600000000 | bytes 1048576 | tf_op jit(solution)/shard_map/intra_backward/pallas_call | solution.py:611
  65.8 3.8 %collective-permute-start.2 = (bf16[2,256,256]{2,1,0:T(8,128)(2,1)S(1)}, bf16[2,256,256]{2,1,0:T(8,128)(2,1)S(1)}, u32[]{:S(2)}, u32[]{:S(2)}) collective-permute-start(bf16[2,256,256]{2,1,0:T(8,128)(2,1)S(1)} %get-tuple-element.53), channel_id=1, source_target_pairs={{0,64},{64,0},{1,65},{65,1},{2,66},{66,2},{3,67},{67,3},{4,68},{68... | collective-permute-start | bytes 786440 | tf_op jit(solution)/shard_map/ppermute | solution.py:702
  69.6 1.2 collective-permute-done.2.arrived_ref
  70.7 0.9 both_sums.1
  71.6 6.0 %all-to-all-start.2 = ((bf16[32,32,256]{2,1,0:T(8,128)(2,1)}), bf16[32,32,256]{2,1,0:T(8,128)(2,1)S(1)}, u32[]{:S(2)}, u32[]{:S(2)}) async-start(bf16[32,32,256]{2,1,0:T(8,128)(2,1)} %both_sums.1), calls=%async_computation.2 | async-start | bytes 1048576 | tf_op jit(solution)/shard_map/all_to_all | solution.py:698
  77.6 1.5 %intra_tail.1 = (bf16[128,256]{1,0:T(8,128)(2,1)S(1)}, bf16[128,256]{1,0:T(8,128)(2,1)S(1)}, bf16[128,256]{1,0:T(8,128)(2,1)S(1)}) custom-call(bf16[2,256,256]{2,1,0:T(8,128)(2,1)S(1)} %get-tuple-element.55.grads_any, bf16[2,256,256]{2,1,0:T(8,128)(2,1)S(1)} %get-tuple-element.56.gq_t_any, bf16[2,256,256]{2,1,0:T(8,128)(2,1)S(1)} %get-tuple-element.57.gk_any, ...), custom_call_target="tpu_custom_call" | custom-call | flops 800000000 | bytes 1048576 | tf_op jit(solution)/shard_map/intra_tail/pallas_call | solution.py:648
  79.1 3.1 %collective-permute-start.3 = (bf16[128,256]{1,0:T(8,128)(2,1)S(1)}, bf16[128,256]{1,0:T(8,128)(2,1)S(1)}, u32[]{:S(2)}, u32[]{:S(2)}) collective-permute-start(bf16[128,256]{1,0:T(8,128)(2,1)S(1)} %get-tuple-element.59), channel_id=1, source_target_pairs={{0,1},{1,2},{2,3},{3,4},{4,5},{5,6},{6,7},{7,8},{8,9},{9,10},{10,1... | collective-permute-start | bytes 196616 | tf_op jit(solution)/shard_map/ppermute | solution.py:694
  82.3 6.7 %all-to-all-done.2.pieces_ref = bf16[32,32,256]{2,1,0:T(8,128)(2,1)S(1)} async-done(((bf16[32,32,256]{2,1,0:T(8,128)(2,1)}), bf16[32,32,256]{2,1,0:T(8,128)(2,1)S(1)}, u32[]{:S(2)}, u32[]{:S(2)}) %all-to-all-start.2) | async-done | bytes 524320 | tf_op jit(solution)/shard_map/all_to_all | solution.py:698
  89.0 0.1 spread.2
  89.1 0.0 collective-permute-done.3.carried_ref
  89.1 9.3 %all_to_all.26.pieces_ref = bf16[4,32,256]{2,1,0:T(8,128)(2,1)S(1)} all-to-all(bf16[4,32,256]{2,1,0:T(8,128)(2,1)S(1)} %spread.2), channel_id=1, replica_groups=mesh['yh'=2,'core'=2,'yl'=2,'x'=4,'za'=4,'zb'=2] {'za'}, dimensions={0} | all-to-all | bytes 131072 | tf_op jit(solution)/shard_map/all_to_all | solution.py:698
  98.4 0.1 spread.3
  98.5 13.6 %all_to_all.27 = bf16[32,32,256]{2,1,0:T(8,128)(2,1)S(1)} all-to-all(bf16[32,32,256]{2,1,0:T(8,128)(2,1)S(1)} %spread.3), channel_id=1, replica_groups=mesh['yh'=2,'core'=2,'yl'=2,'x'=4,'za'=4,'zb'=2] {'yh','yl','x','zb'}, dimensions={0} | all-to-all | bytes 1048576 | tf_op jit(solution)/shard_map/all_to_all | solution.py:698
  112.1 4.6 %collective-permute-start.4 = (bf16[32,2,16,256]{3,2,1,0:T(8,128)(2,1)S(1)}, bf16[32,2,16,256]{3,2,1,0:T(8,128)(2,1)S(1)}, u32[]{:S(2)}, u32[]{:S(2)}) collective-permute-start(bf16[32,2,16,256]{3,2,1,0:T(8,128)(2,1)S(1)} %bitcast.9), channel_id=1, source_target_pairs={{0,64},{64,0},{1,65},{65,1},{2,66},{66,2},{3,67},{67,3},{4,68},{68... | collective-permute-start | bytes 1572872 | tf_op jit(solution)/shard_map/ppermute | solution.py:702
  116.7 1.5 %collective-permute-done.4.other_ref = bf16[32,2,16,256]{3,2,1,0:T(8,128)(2,1)S(1)} collective-permute-done((bf16[32,2,16,256]{3,2,1,0:T(8,128)(2,1)S(1)}, bf16[32,2,16,256]{3,2,1,0:T(8,128)(2,1)S(1)}, u32[]{:S(2)}, u32[]{:S(2)}) %collective-permute-start.4) | collective-permute-done | bytes 524320 | tf_op jit(solution)/shard_map/ppermute | solution.py:702
  118.3 1.7 %finish.1 = (bf16[256,256]{1,0:T(8,128)(2,1)}, f32[2,256,256]{2,1,0:T(8,128)}, f32[2,256,256]{2,1,0:T(8,128)}, f32[2,256,256]{2,1,0:T(8,128)}, f32[2,256,256]{2,1,0:T(8,128)}, /*index=5*/f32[2,256]{1,0:T(2,128)}) custom-call(s32[1]{0:T(128)} %bitcast.core_ref, bf16[32,2,16,256]{3,2,1,0:T(8,128)(2,1)S(1)} %bitcast.10, ...), custom_call_target="tpu_custom_call" | custom-call | flops 800000000 | bytes 1048576 | tf_op jit(solution)/shard_map/finish/pallas_call | solution.py:685
Async XLA Ops:
  0.6 7.1 %copy-start.4 = (bf16[1,256,256]{2,1,0:T(8,128)(2,1)S(1)}, bf16[1,256,256]{2,1,0:T(8,128)(2,1)}, u32[]{:S(2)}) copy-start(bf16[1,256,256]{2,1,0:T(8,128)(2,1)} %param.8) | copy-start | bytes 393220
  0.6 7.1 %copy-start.5 = (bf16[1,256,256]{2,1,0:T(8,128)(2,1)S(1)}, bf16[1,256,256]{2,1,0:T(8,128)(2,1)}, u32[]{:S(2)}) copy-start(bf16[1,256,256]{2,1,0:T(8,128)(2,1)} %param.7) | copy-start | bytes 393220
  0.7 7.1 %collective-permute-start = (bf16[256,256]{1,0:T(8,128)(2,1)}, bf16[256,256]{1,0:T(8,128)(2,1)S(1)}, u32[]{:S(2)}, u32[]{:S(2)}) collective-permute-start(bf16[256,256]{1,0:T(8,128)(2,1)} %bitcast.14), channel_id=1, source_target_pairs={{1,0},{2,1},{3,2},{4,3},{5,4},{6,5},{7,6},{8,7},{9,8},{10,9},{11,1... | collective-permute-start | bytes 393224 | tf_op jit(solution)/shard_map/ppermute | solution.py:694
  2.1 0.7 copy-start.6
  7.7 31.9 %copy-start = (bf16[2,256,256]{2,1,0:T(8,128)(2,1)S(1)}, bf16[2,256,256]{2,1,0:T(8,128)(2,1)}, u32[]{:S(2)}) copy-start(bf16[2,256,256]{2,1,0:T(8,128)(2,1)} %wo_any.5) | copy-start | bytes 786436
  7.7 31.9 %copy-start.1 = (bf16[2,256,256]{2,1,0:T(8,128)(2,1)S(1)}, bf16[2,256,256]{2,1,0:T(8,128)(2,1)}, u32[]{:S(2)}) copy-start(bf16[2,256,256]{2,1,0:T(8,128)(2,1)} %wq_ref.5) | copy-start | bytes 786436
  7.7 31.9 %copy-start.2 = (bf16[2,256,256]{2,1,0:T(8,128)(2,1)S(1)}, bf16[2,256,256]{2,1,0:T(8,128)(2,1)}, u32[]{:S(2)}) copy-start(bf16[2,256,256]{2,1,0:T(8,128)(2,1)} %wk_ref.5) | copy-start | bytes 786436
  7.7 31.9 %copy-start.3 = (bf16[2,256,256]{2,1,0:T(8,128)(2,1)S(1)}, bf16[2,256,256]{2,1,0:T(8,128)(2,1)}, u32[]{:S(2)}) copy-start(bf16[2,256,256]{2,1,0:T(8,128)(2,1)} %wv_ref.5) | copy-start | bytes 786436
  43.8 9.3 %copy-start.7 = (f32[2,256]{1,0:T(2,128)S(1)}, f32[2,256]{1,0:T(2,128)}, u32[]{:S(2)}) copy-start(f32[2,256]{1,0:T(2,128)} %gain_ref.5) | copy-start | bytes 6148
  43.8 17.2 %all-to-all-start.1 = ((bf16[64,8,256]{2,1,0:T(8,128)(2,1)}), bf16[64,8,256]{2,1,0:T(8,128)(2,1)S(1)}, u32[]{:S(2)}, u32[]{:S(2)}) async-start(bf16[64,8,256]{2,1,0:T(8,128)(2,1)} %bitcast.5), calls=%async_computation.1 | async-start | bytes 524288 | tf_op jit(solution)/shard_map/all_to_all | solution.py:698
  50.5 6.5 %collective-permute-start.1 = (bf16[2,256,256]{2,1,0:T(8,128)(2,1)S(1)}, bf16[2,256,256]{2,1,0:T(8,128)(2,1)S(1)}, u32[]{:S(2)}, u32[]{:S(2)}) collective-permute-start(bf16[2,256,256]{2,1,0:T(8,128)(2,1)S(1)} %get-tuple-element.50), channel_id=1, source_target_pairs={{0,64},{64,0},{1,65},{65,1},{2,66},{66,2},{3,67},{67,3},{4,68},{68... | collective-permute-start | bytes 786440 | tf_op jit(solution)/shard_map/ppermute | solution.py:702
  55.9 1.1 copy-start.8
  65.8 4.9 %collective-permute-start.2 = (bf16[2,256,256]{2,1,0:T(8,128)(2,1)S(1)}, bf16[2,256,256]{2,1,0:T(8,128)(2,1)S(1)}, u32[]{:S(2)}, u32[]{:S(2)}) collective-permute-start(bf16[2,256,256]{2,1,0:T(8,128)(2,1)S(1)} %get-tuple-element.53), channel_id=1, source_target_pairs={{0,64},{64,0},{1,65},{65,1},{2,66},{66,2},{3,67},{67,3},{4,68},{68... | collective-permute-start | bytes 786440 | tf_op jit(solution)/shard_map/ppermute | solution.py:702
  71.6 17.4 %all-to-all-start.2 = ((bf16[32,32,256]{2,1,0:T(8,128)(2,1)}), bf16[32,32,256]{2,1,0:T(8,128)(2,1)S(1)}, u32[]{:S(2)}, u32[]{:S(2)}) async-start(bf16[32,32,256]{2,1,0:T(8,128)(2,1)} %both_sums.1), calls=%async_computation.2 | async-start | bytes 1048576 | tf_op jit(solution)/shard_map/all_to_all | solution.py:698
  79.1 9.9 %collective-permute-start.3 = (bf16[128,256]{1,0:T(8,128)(2,1)S(1)}, bf16[128,256]{1,0:T(8,128)(2,1)S(1)}, u32[]{:S(2)}, u32[]{:S(2)}) collective-permute-start(bf16[128,256]{1,0:T(8,128)(2,1)S(1)} %get-tuple-element.59), channel_id=1, source_target_pairs={{0,1},{1,2},{2,3},{3,4},{4,5},{5,6},{6,7},{7,8},{8,9},{9,10},{10,1... | collective-permute-start | bytes 196616 | tf_op jit(solution)/shard_map/ppermute | solution.py:694
  112.1 6.2 %collective-permute-start.4 = (bf16[32,2,16,256]{3,2,1,0:T(8,128)(2,1)S(1)}, bf16[32,2,16,256]{3,2,1,0:T(8,128)(2,1)S(1)}, u32[]{:S(2)}, u32[]{:S(2)}) collective-permute-start(bf16[32,2,16,256]{3,2,1,0:T(8,128)(2,1)S(1)} %bitcast.9), channel_id=1, source_target_pairs={{0,64},{64,0},{1,65},{65,1},{2,66},{66,2},{3,67},{67,3},{4,68},{68... | collective-permute-start | bytes 1572872 | tf_op jit(solution)/shard_map/ppermute | solution.py:702

commit v7 on v6

--- a/solution.py
+++ b/solution.py
@@ -19,9 +19,6 @@
 BF = jnp.bfloat16
 F32 = jnp.float32
 VMEM_LIMIT = 16 * 1024 * 1024
-FIRST_LIMIT = 54800 * 1024
-SECOND_LIMIT = 54300 * 1024
-BACKWARD_LIMIT = 52850 * 1024
 
 AXES = ("yh", "core", "yl", "x", "za", "zb")
 DP = ("yh", "core")
@@ -179,10 +176,14 @@
     return pltpu.VMEM(shape, BF)
 
 
+def pinned(*arrays):
+    return [pltpu.with_memory_space_constraint(array, pltpu.HBM) for array in arrays]
+
+
 def intra_first_kernel(
     f_any, gain_any, wq_any, wk_any, wv_any, wo_any,
-    mid_ref, keys_ref, queries_ref, values_ref,
-    w_ref, gain_ref, f_ref, ctx_ref, sems,
+    mid_ref, keys_ref, queries_ref, values_ref, w_ref, gain_ref,
+    f_ref, ctx_ref, sems,
 ):
     copies = begin(
         sems,
@@ -211,23 +212,12 @@
 
 
 def intra_second_kernel(
-    n_ref, mid_in_ref, keys_ref, queries_ref, values_ref,
-    f_any, grad_any, gain_any, wq_any, wk_any, wv_any, wo_any, packed_ref,
-    f_ref, grad_ref, gain_ref, w_ref, ctx_ref, sems,
+    n_ref, mid_in_ref, keys_ref, queries_ref, values_ref, w_ref, gain_ref, f_any, grad_any, packed_ref,
+    f_ref, grad_ref, ctx_ref, sems,
 ):
-    copies = begin(
-        sems,
-        (gain_any, gain_ref),
-        (wk_any.at[0], w_ref.at[1]),
-        (wq_any.at[0], w_ref.at[0]),
-        (wv_any.at[0], w_ref.at[2]),
-        (wo_any.at[0], w_ref.at[3]),
-        (f_any.at[pl.ds(HOP, HOP)], f_ref),
-        (grad_any, grad_ref),
-    )
+    copies = begin(sems, (f_any.at[pl.ds(HOP, HOP)], f_ref), (grad_any, grad_ref))
     rows = n_ref[:HOP].astype(F32)
     unit, _ = standardize(rows)
-    settle(copies[:4])
     normed = (unit * gain_ref[0:1, :]).astype(BF)
     keys = jnp.concatenate([keys_ref[...], nn(normed, w_ref[1]).astype(BF)], axis=0)
     queries_t = jnp.concatenate(
@@ -235,7 +225,7 @@
     )
     values_t = jnp.concatenate([values_ref[...], nt(w_ref[2].T, normed).astype(BF)], axis=1)
     attend(keys, queries_t, values_t, ctx_ref)
-    settle(copies[4:])
+    settle(copies)
     rows = jnp.concatenate([f_ref[...].astype(F32), rows], axis=0)
     mids = (mid_in_ref[...], (rows + tn(ctx_ref[...], w_ref[3])).astype(BF))
     grads = grad_ref[...]
@@ -252,24 +242,19 @@
         packed_ref[256 * t : 256 * t + 256, :] = nn(pick, rows).astype(BF)
 
 
-def intra_first(frames, gains, wq, wk, wv, wo):
-    return kernel_call(
-        intra_first_kernel, "intra_first", 3, [HBM] * 6, [VMEM] * 4,
-        (bf16(K, D), bf16(HOP, D), bf16(D, HOP), bf16(D, HOP)),
-        [vbf(4, D, D), pltpu.VMEM((2, D), F32), vbf(K, D), vbf(D, K), dma(6)],
-        FIRST_LIMIT,
-    )(frames, gains, wq, wk, wv, wo)
-
-
-def intra_second(following, *rest):
-    return kernel_call(
-        intra_second_kernel, "intra_second", 3, [VMEM] * 5 + [HBM] * 7, VMEM,
-        bf16(512, 384),
-        [
-            vbf(HOP, D), vbf(K, D), pltpu.VMEM((2, D), F32), vbf(4, D, D), vbf(D, K), dma(7),
-        ],
-        SECOND_LIMIT,
-    )(following, *rest)
+def intra_first(*operands):
+    return kernel_call(
+        intra_first_kernel, "intra_first", 3, [HBM] * 6, [VMEM] * 6,
+        (bf16(K, D), bf16(HOP, D), bf16(D, HOP), bf16(D, HOP), bf16(4, D, D), f32(2, D)),
+        [vbf(K, D), vbf(D, K), dma(6)],
+    )(*pinned(*operands))
+
+
+def intra_second(following, frames, grads, *front):
+    return kernel_call(
+        intra_second_kernel, "intra_second", 3, [VMEM] * 7 + [HBM] * 2, VMEM, bf16(512, 384),
+        [vbf(HOP, D), vbf(K, D), vbf(D, K), dma(2)],
+    )(following, *front, *pinned(frames, grads))
 
 
 def inter_kernel(
@@ -614,8 +599,7 @@
             f32(2, D, D), bf16(2, D, D), bf16(2, K, D), bf16(2, D, K), bf16(2, K, D), bf16(2, K, D),
         ),
         [vbf(HANDED_ROWS, 128), pltpu.VMEM((4 * HEADS, K), F32), vbf(D, D), dma(4)],
-        BACKWARD_LIMIT,
-    )(core, grads, *rest)
+    )(core, grads, *pinned(*rest))
 
 
 def intra_tail_kernel(
@@ -741,9 +725,7 @@
     core = lax.axis_index("core").astype(jnp.int32).reshape(1)
     following = shifted(frames, -1)
     front = intra_first(frames, gains, wq, wk, wv, wo)
-    packed = intra_second(
-        following, *front, frames, frames_grad[0], gains, wq, wk, wv, wo
-    )
+    packed = intra_second(following, frames, frames_grad[0], *front)
     across = exchanged(packed.reshape(64, 8, 384), TM).reshape(512, 384)
     grad_middle, *operands = inter(across, gains, wq, wk, wv, wo)
     grad_local = exchanged(grad_middle.reshape(64, 8, D), TM).reshape(512, D)

time: 120 us -> 118 us (0.983)
  Pallas kernels: 23 us -> 21.2 us
    pallas_call x2, Pallas kernels: 6.64 us -> 4.89 us  [the longest x1 2.85 us: intra_first(): kernel_call(intra_first_kernel, 'intra_first', 3, [HBM] * 6, [VMEM] * 6,...]
  transfers between devices with their start and end apart: 7 -> 7, of which waited for: 5 -> 5; matrix products, arithmetic and copies ran while one was open for 0% -> 0% of each run, Pallas kernels for 6% -> 7%
where the time goes in v7:
time: 118 us
  blocking collectives  50.8 us (43%)
  starting transfers between devices  27.7 us (23%)
  Pallas kernels  21.2 us (18%)
  waiting for transfers between devices  16.2 us (14%)
  local copies, waits for them, and re-layouts  1.18 us (1%)
    all_to_all x3, blocking collectives, exchanged(): return lax.all_to_all(shard, axes, split_axis=0, concat_axis=0, tiled=True)  50.8 us
    all_to_all x2, starting transfers between devices, exchanged(): return lax.all_to_all(shard, axes, split_axis=0, concat_axis=0, tiled=True)  12.2 us
    ppermute x3, starting transfers between devices, swapped(): return lax.ppermute(shard, 'core', [(0, 1), (1, 0)])  11 us
    all_to_all x2, waiting for transfers between devices, exchanged(): return lax.all_to_all(shard, axes, split_axis=0, concat_axis=0, tiled=True)  10.7 us
    pallas_call x1, Pallas kernels, intra_backward(): kernel_call(intra_backward_kernel, 'intra_backward', 4, [SMEM, VMEM] + [H...  4.74 us
    ppermute x2, starting transfers between devices, shifted(): return lax.ppermute(shard, TM, pairs)  4.43 us
    pallas_call x1, Pallas kernels, inter(): kernel_call(inter_kernel, 'inter', 5, [VMEM] * 6, [VMEM] * 7, (bf16(512,...  4.2 us
    pallas_call x1, Pallas kernels, intra_first(): kernel_call(intra_first_kernel, 'intra_first', 3, [HBM] * 6, [VMEM] * 6,...  2.85 us
  transfers between devices with their start and end apart: 7, of which 5 were waited for; matrix products, arithmetic and copies ran while one was open for 0% of the time, Pallas kernels for 7%

profile of v7, /device:TPU:1, one launch (start us, length us, event | category | flops | bytes accessed | tf_op | source)
XLA Modules:
  0.0 117.8 jit_solution(11654995379368998799)
XLA Ops:
  0.6 1.3 %collective-permute-start = (bf16[256,256]{1,0:T(8,128)(2,1)}, bf16[256,256]{1,0:T(8,128)(2,1)S(1)}, u32[]{:S(2)}, u32[]{:S(2)}) collective-permute-start(bf16[256,256]{1,0:T(8,128)(2,1)} %bitcast.14), channel_id=1, source_target_pairs={{1,0},{2,1},{3,2},{4,3},{5,4},{6,5},{7,6},{8,7},{9,8},{10,9},{11,1... | collective-permute-start | bytes 393224 | tf_op jit(solution)/shard_map/ppermute | solution.py:678
  1.9 2.8 %intra_first.1 = (bf16[256,256]{1,0:T(8,128)(2,1)S(1)}, bf16[128,256]{1,0:T(8,128)(2,1)S(1)}, bf16[256,128]{1,0:T(8,128)(2,1)S(1)}, bf16[256,128]{1,0:T(8,128)(2...) custom-call(bf16[256,256]{1,0:T(8,128)(2,1)} %bitcast.15, f32[2,256]{1,0:T(2,128)} %gain_ref.5, ...), custom_call_target="tpu_custom_call" | custom-call | flops 1200000000 | bytes 1048576 | tf_op jit(solution)/shard_map/intra_first/pallas_call | solution.py:246
  4.8 2.8 %collective-permute-done.n_ref.n_any = bf16[256,256]{1,0:T(8,128)(2,1)S(1)} collective-permute-done((bf16[256,256]{1,0:T(8,128)(2,1)}, bf16[256,256]{1,0:T(8,128)(2,1)S(1)}, u32[]{:S(2)}, u32[]{:S(2)}) %collective-permute-start) | collective-permute-done | bytes 131104 | tf_op jit(solution)/shard_map/ppermute | solution.py:678
  7.6 0.0 copy-start
  7.6 0.0 copy-start.1
  7.6 0.0 copy-start.2
  7.6 0.0 copy-start.3
  7.6 0.0 copy-start.5
  7.6 2.0 %intra_second.1 = bf16[512,384]{1,0:T(8,128)(2,1)S(1)} custom-call(bf16[256,256]{1,0:T(8,128)(2,1)S(1)} %collective-permute-done.n_ref.n_any, bf16[256,256]{1,0:T(8,128)(2,1)S(1)} %get-tuple-element.40.mid_in_ref, bf16[128,256]{1,0:T(8,128)(2,1)S(1)} %get-tuple-element.41.keys_ref, bf16[256,128]{1,0:T(8,128)(2,1)S(1)} %get-tuple-element.42.queries_ref, ...), custom_call_target="tpu_custom_call" | custom-call | flops 1200000000 | bytes 1048576 | tf_op jit(solution)/shard_map/intra_second/pallas_call | solution.py:254
  9.6 27.8 %all_to_all.25 = bf16[64,8,384]{2,1,0:T(8,128)(2,1)S(1)} all-to-all(bf16[64,8,384]{2,1,0:T(8,128)(2,1)S(1)} %bitcast.12), channel_id=1, replica_groups=mesh['yh'=2,'core'=2,'yl'=2,'x'=4,'za'=4,'zb'=2] {'yl','x','za','zb'}, dimensions={0} | all-to-all | bytes 786432 | tf_op jit(solution)/shard_map/all_to_all | solution.py:682
  37.5 0.0 copy-done
  37.5 0.0 copy-done.1
  37.5 0.0 copy-done.2
  37.5 0.0 copy-done.3
  37.5 0.0 copy-done.5
  37.5 4.2 %inter.1 = (bf16[512,256]{1,0:T(8,128)(2,1)}, bf16[256,512]{1,0:T(8,128)(2,1)S(1)}, bf16[512,256]{1,0:T(8,128)(2,1)S(1)}, bf16[256,512]{1,0:T(8,128)(2,1)S(1)}, ...) custom-call(bf16[512,384]{1,0:T(8,128)(2,1)S(1)} %bitcast.11, ...), custom_call_target="tpu_custom_call" | custom-call | flops 2000000000 | bytes 1048576 | tf_op jit(solution)/shard_map/inter/pallas_call | solution.py:356
  41.7 0.0 copy-start.4
  41.7 6.2 %all-to-all-start.1 = ((bf16[64,8,256]{2,1,0:T(8,128)(2,1)}), bf16[64,8,256]{2,1,0:T(8,128)(2,1)S(1)}, u32[]{:S(2)}, u32[]{:S(2)}) async-start(bf16[64,8,256]{2,1,0:T(8,128)(2,1)} %bitcast.5), calls=%async_computation.1 | async-start | bytes 524288 | tf_op jit(solution)/shard_map/all_to_all | solution.py:682
  48.0 0.4 inter_weights.1
  48.4 2.6 %collective-permute-start.1 = (bf16[2,256,256]{2,1,0:T(8,128)(2,1)S(1)}, bf16[2,256,256]{2,1,0:T(8,128)(2,1)S(1)}, u32[]{:S(2)}, u32[]{:S(2)}) collective-permute-start(bf16[2,256,256]{2,1,0:T(8,128)(2,1)S(1)} %get-tuple-element.54), channel_id=1, source_target_pairs={{0,64},{64,0},{1,65},{65,1},{2,66},{66,2},{3,67},{67,3},{4,68},{68... | collective-permute-start | bytes 786440 | tf_op jit(solution)/shard_map/ppermute | solution.py:686
  51.1 0.0 copy-done.4
  51.1 2.7 %intra_prepare.1.handed_any = bf16[5824,128]{1,0:T(8,128)(2,1)S(1)} custom-call(bf16[256,256]{1,0:T(8,128)(2,1)S(1)} %bitcast.17, bf16[256,256]{1,0:T(8,128)(2,1)S(1)} %collective-permute-done.n_ref.n_any, f32[2,256]{1,0:T(2,128)S(1)} %copy-done.5, bf16[2,256,256]{2,1,0:T(8,128)(2,1)S(1)} %copy-done.1, bf16[2,256,256]{2,1,0:T(8,128)(2,1)S(1)} %copy-done.2, ...), custom_call_target="tpu_custom_call" | custom-call | flops 1200000000 | bytes 1048576 | tf_op jit(solution)/shard_map/intra_prepare/pallas_call | solution.py:500
  53.8 0.0 copy-start.6
  53.8 1.2 copy-done.6
  54.9 0.0 collective-permute-done.1.arrived_ref
  55.0 4.0 %all-to-all-done.1 = bf16[64,8,256]{2,1,0:T(8,128)(2,1)S(1)} async-done(((bf16[64,8,256]{2,1,0:T(8,128)(2,1)}), bf16[64,8,256]{2,1,0:T(8,128)(2,1)S(1)}, u32[]{:S(2)}, u32[]{:S(2)}) %all-to-all-start.1) | async-done | bytes 262176 | tf_op jit(solution)/shard_map/all_to_all | solution.py:682
  59.0 4.7 %intra_backward.1 = (f32[2,256,256]{2,1,0:T(8,128)S(1)}, bf16[2,256,256]{2,1,0:T(8,128)(2,1)S(1)}, bf16[2,256,256]{2,1,0:T(8,128)(2,1)S(1)}, bf16[2,256,256]{2,1...) custom-call(s32[1]{0:T(128)} %bitcast.core_ref, bf16[512,256]{1,0:T(8,128)(2,1)S(1)} %bitcast.13, ...), custom_call_target="tpu_custom_call" | custom-call | flops 1600000000 | bytes 1048576 | tf_op jit(solution)/shard_map/intra_backward/pallas_call | solution.py:596
  63.7 3.8 %collective-permute-start.2 = (bf16[2,256,256]{2,1,0:T(8,128)(2,1)S(1)}, bf16[2,256,256]{2,1,0:T(8,128)(2,1)S(1)}, u32[]{:S(2)}, u32[]{:S(2)}) collective-permute-start(bf16[2,256,256]{2,1,0:T(8,128)(2,1)S(1)} %get-tuple-element.57), channel_id=1, source_target_pairs={{0,64},{64,0},{1,65},{65,1},{2,66},{66,2},{3,67},{67,3},{4,68},{68... | collective-permute-start | bytes 786440 | tf_op jit(solution)/shard_map/ppermute | solution.py:686
  67.5 1.2 collective-permute-done.2.arrived_ref
  68.6 0.9 both_sums.1
  69.5 6.0 %all-to-all-start.2 = ((bf16[32,32,256]{2,1,0:T(8,128)(2,1)}), bf16[32,32,256]{2,1,0:T(8,128)(2,1)S(1)}, u32[]{:S(2)}, u32[]{:S(2)}) async-start(bf16[32,32,256]{2,1,0:T(8,128)(2,1)} %both_sums.1), calls=%async_computation.2 | async-start | bytes 1048576 | tf_op jit(solution)/shard_map/all_to_all | solution.py:682
  75.5 1.5 %intra_tail.1 = (bf16[128,256]{1,0:T(8,128)(2,1)S(1)}, bf16[128,256]{1,0:T(8,128)(2,1)S(1)}, bf16[128,256]{1,0:T(8,128)(2,1)S(1)}) custom-call(bf16[2,256,256]{2,1,0:T(8,128)(2,1)S(1)} %get-tuple-element.59.grads_any, bf16[2,256,256]{2,1,0:T(8,128)(2,1)S(1)} %get-tuple-element.60.gq_t_any, bf16[2,256,256]{2,1,0:T(8,128)(2,1)S(1)} %get-tuple-element.61.gk_any, ...), custom_call_target="tpu_custom_call" | custom-call | flops 800000000 | bytes 1048576 | tf_op jit(solution)/shard_map/intra_tail/pallas_call | solution.py:632
  77.0 3.1 %collective-permute-start.3 = (bf16[128,256]{1,0:T(8,128)(2,1)S(1)}, bf16[128,256]{1,0:T(8,128)(2,1)S(1)}, u32[]{:S(2)}, u32[]{:S(2)}) collective-permute-start(bf16[128,256]{1,0:T(8,128)(2,1)S(1)} %get-tuple-element.63), channel_id=1, source_target_pairs={{0,1},{1,2},{2,3},{3,4},{4,5},{5,6},{6,7},{7,8},{8,9},{9,10},{10,1... | collective-permute-start | bytes 196616 | tf_op jit(solution)/shard_map/ppermute | solution.py:678
  80.2 6.7 %all-to-all-done.2.pieces_ref = bf16[32,32,256]{2,1,0:T(8,128)(2,1)S(1)} async-done(((bf16[32,32,256]{2,1,0:T(8,128)(2,1)}), bf16[32,32,256]{2,1,0:T(8,128)(2,1)S(1)}, u32[]{:S(2)}, u32[]{:S(2)}) %all-to-all-start.2) | async-done | bytes 524320 | tf_op jit(solution)/shard_map/all_to_all | solution.py:682
  86.9 0.1 spread.2
  86.9 0.0 collective-permute-done.3.carried_ref
  86.9 9.3 %all_to_all.26.pieces_ref = bf16[4,32,256]{2,1,0:T(8,128)(2,1)S(1)} all-to-all(bf16[4,32,256]{2,1,0:T(8,128)(2,1)S(1)} %spread.2), channel_id=1, replica_groups=mesh['yh'=2,'core'=2,'yl'=2,'x'=4,'za'=4,'zb'=2] {'za'}, dimensions={0} | all-to-all | bytes 131072 | tf_op jit(solution)/shard_map/all_to_all | solution.py:682
  96.3 0.1 spread.3
  96.4 13.6 %all_to_all.27 = bf16[32,32,256]{2,1,0:T(8,128)(2,1)S(1)} all-to-all(bf16[32,32,256]{2,1,0:T(8,128)(2,1)S(1)} %spread.3), channel_id=1, replica_groups=mesh['yh'=2,'core'=2,'yl'=2,'x'=4,'za'=4,'zb'=2] {'yh','yl','x','zb'}, dimensions={0} | all-to-all | bytes 1048576 | tf_op jit(solution)/shard_map/all_to_all | solution.py:682
  110.0 4.6 %collective-permute-start.4 = (bf16[32,2,16,256]{3,2,1,0:T(8,128)(2,1)S(1)}, bf16[32,2,16,256]{3,2,1,0:T(8,128)(2,1)S(1)}, u32[]{:S(2)}, u32[]{:S(2)}) collective-permute-start(bf16[32,2,16,256]{3,2,1,0:T(8,128)(2,1)S(1)} %bitcast.9), channel_id=1, source_target_pairs={{0,64},{64,0},{1,65},{65,1},{2,66},{66,2},{3,67},{67,3},{4,68},{68... | collective-permute-start | bytes 1572872 | tf_op jit(solution)/shard_map/ppermute | solution.py:686
  114.6 1.5 %collective-permute-done.4.other_ref = bf16[32,2,16,256]{3,2,1,0:T(8,128)(2,1)S(1)} collective-permute-done((bf16[32,2,16,256]{3,2,1,0:T(8,128)(2,1)S(1)}, bf16[32,2,16,256]{3,2,1,0:T(8,128)(2,1)S(1)}, u32[]{:S(2)}, u32[]{:S(2)}) %collective-permute-start.4) | collective-permute-done | bytes 524320 | tf_op jit(solution)/shard_map/ppermute | solution.py:686
  116.1 1.7 %finish.1 = (bf16[256,256]{1,0:T(8,128)(2,1)}, f32[2,256,256]{2,1,0:T(8,128)}, f32[2,256,256]{2,1,0:T(8,128)}, f32[2,256,256]{2,1,0:T(8,128)}, f32[2,256,256]{2,1,0:T(8,128)}, /*index=5*/f32[2,256]{1,0:T(2,128)}) custom-call(s32[1]{0:T(128)} %bitcast.core_ref, bf16[32,2,16,256]{3,2,1,0:T(8,128)(2,1)S(1)} %bitcast.10, ...), custom_call_target="tpu_custom_call" | custom-call | flops 800000000 | bytes 1048576 | tf_op jit(solution)/shard_map/finish/pallas_call | solution.py:669
  (1 shorter events, 0.0 us)
Async XLA Ops:
  0.6 6.9 %collective-permute-start = (bf16[256,256]{1,0:T(8,128)(2,1)}, bf16[256,256]{1,0:T(8,128)(2,1)S(1)}, u32[]{:S(2)}, u32[]{:S(2)}) collective-permute-start(bf16[256,256]{1,0:T(8,128)(2,1)} %bitcast.14), channel_id=1, source_target_pairs={{1,0},{2,1},{3,2},{4,3},{5,4},{6,5},{7,6},{8,7},{9,8},{10,9},{11,1... | collective-permute-start | bytes 393224 | tf_op jit(solution)/shard_map/ppermute | solution.py:678
  7.6 29.9 %copy-start = (bf16[2,256,256]{2,1,0:T(8,128)(2,1)S(1)}, bf16[2,256,256]{2,1,0:T(8,128)(2,1)}, u32[]{:S(2)}) copy-start(bf16[2,256,256]{2,1,0:T(8,128)(2,1)} %wo_any.3) | copy-start | bytes 786436
  7.6 29.9 %copy-start.1 = (bf16[2,256,256]{2,1,0:T(8,128)(2,1)S(1)}, bf16[2,256,256]{2,1,0:T(8,128)(2,1)}, u32[]{:S(2)}) copy-start(bf16[2,256,256]{2,1,0:T(8,128)(2,1)} %wq_ref.5) | copy-start | bytes 786436
  7.6 29.9 %copy-start.2 = (bf16[2,256,256]{2,1,0:T(8,128)(2,1)S(1)}, bf16[2,256,256]{2,1,0:T(8,128)(2,1)}, u32[]{:S(2)}) copy-start(bf16[2,256,256]{2,1,0:T(8,128)(2,1)} %wk_ref.5) | copy-start | bytes 786436
  7.6 29.9 %copy-start.3 = (bf16[2,256,256]{2,1,0:T(8,128)(2,1)S(1)}, bf16[2,256,256]{2,1,0:T(8,128)(2,1)}, u32[]{:S(2)}) copy-start(bf16[2,256,256]{2,1,0:T(8,128)(2,1)} %wv_ref.5) | copy-start | bytes 786436
  7.6 29.9 %copy-start.5 = (f32[2,256]{1,0:T(2,128)S(1)}, f32[2,256]{1,0:T(2,128)}, u32[]{:S(2)}) copy-start(f32[2,256]{1,0:T(2,128)} %gain_ref.5) | copy-start | bytes 6148
  41.7 9.3 %copy-start.4 = (bf16[1,256,256]{2,1,0:T(8,128)(2,1)S(1)}, bf16[1,256,256]{2,1,0:T(8,128)(2,1)}, u32[]{:S(2)}) copy-start(bf16[1,256,256]{2,1,0:T(8,128)(2,1)} %param.7) | copy-start | bytes 393220
  41.7 17.2 %all-to-all-start.1 = ((bf16[64,8,256]{2,1,0:T(8,128)(2,1)}), bf16[64,8,256]{2,1,0:T(8,128)(2,1)S(1)}, u32[]{:S(2)}, u32[]{:S(2)}) async-start(bf16[64,8,256]{2,1,0:T(8,128)(2,1)} %bitcast.5), calls=%async_computation.1 | async-start | bytes 524288 | tf_op jit(solution)/shard_map/all_to_all | solution.py:682
  48.4 6.5 %collective-permute-start.1 = (bf16[2,256,256]{2,1,0:T(8,128)(2,1)S(1)}, bf16[2,256,256]{2,1,0:T(8,128)(2,1)S(1)}, u32[]{:S(2)}, u32[]{:S(2)}) collective-permute-start(bf16[2,256,256]{2,1,0:T(8,128)(2,1)S(1)} %get-tuple-element.54), channel_id=1, source_target_pairs={{0,64},{64,0},{1,65},{65,1},{2,66},{66,2},{3,67},{67,3},{4,68},{68... | collective-permute-start | bytes 786440 | tf_op jit(solution)/shard_map/ppermute | solution.py:686
  53.8 1.2 copy-start.6
  63.7 4.9 %collective-permute-start.2 = (bf16[2,256,256]{2,1,0:T(8,128)(2,1)S(1)}, bf16[2,256,256]{2,1,0:T(8,128)(2,1)S(1)}, u32[]{:S(2)}, u32[]{:S(2)}) collective-permute-start(bf16[2,256,256]{2,1,0:T(8,128)(2,1)S(1)} %get-tuple-element.57), channel_id=1, source_target_pairs={{0,64},{64,0},{1,65},{65,1},{2,66},{66,2},{3,67},{67,3},{4,68},{68... | collective-permute-start | bytes 786440 | tf_op jit(solution)/shard_map/ppermute | solution.py:686
  69.5 17.4 %all-to-all-start.2 = ((bf16[32,32,256]{2,1,0:T(8,128)(2,1)}), bf16[32,32,256]{2,1,0:T(8,128)(2,1)S(1)}, u32[]{:S(2)}, u32[]{:S(2)}) async-start(bf16[32,32,256]{2,1,0:T(8,128)(2,1)} %both_sums.1), calls=%async_computation.2 | async-start | bytes 1048576 | tf_op jit(solution)/shard_map/all_to_all | solution.py:682
  77.0 9.9 %collective-permute-start.3 = (bf16[128,256]{1,0:T(8,128)(2,1)S(1)}, bf16[128,256]{1,0:T(8,128)(2,1)S(1)}, u32[]{:S(2)}, u32[]{:S(2)}) collective-permute-start(bf16[128,256]{1,0:T(8,128)(2,1)S(1)} %get-tuple-element.63), channel_id=1, source_target_pairs={{0,1},{1,2},{2,3},{3,4},{4,5},{5,6},{6,7},{7,8},{8,9},{9,10},{10,1... | collective-permute-start | bytes 196616 | tf_op jit(solution)/shard_map/ppermute | solution.py:678
  110.0 6.2 %collective-permute-start.4 = (bf16[32,2,16,256]{3,2,1,0:T(8,128)(2,1)S(1)}, bf16[32,2,16,256]{3,2,1,0:T(8,128)(2,1)S(1)}, u32[]{:S(2)}, u32[]{:S(2)}) collective-permute-start(bf16[32,2,16,256]{3,2,1,0:T(8,128)(2,1)S(1)} %bitcast.9), channel_id=1, source_target_pairs={{0,64},{64,0},{1,65},{65,1},{2,66},{66,2},{3,67},{67,3},{4,68},{68... | collective-permute-start | bytes 1572872 | tf_op jit(solution)/shard_map/ppermute | solution.py:686

commit v8 on v7

--- a/solution.py
+++ b/solution.py
@@ -111,12 +111,11 @@
                 held[i][step] = stage(step, *([held[i - 1].pop(step)] if i else []))
 
 
-def attend(keys, queries_t, values_t, ctx_ref):
-    masks = head_masks()
+def attend(keys, queries_t, values_t, ctx_ref, ahead):
 
     def scores_of(h):
-        block = slice((h // 4) * 128, (h // 4) * 128 + 128)
-        return nn(keys[:, block] * masks[h % 4], queries_t[block, :])
+        feats = slice(h * HEAD, h * HEAD + HEAD)
+        return nn(keys[:, feats], queries_t[feats, :])
 
     def weigh(h, scores):
         return softmax_keys(scores).astype(BF)
@@ -125,7 +124,8 @@
         feats = slice(h * HEAD, h * HEAD + HEAD)
         ctx_ref[feats, :] = nn(values_t[feats, :], low).astype(BF)
 
-    staged(HEADS, scores_of, weigh, collect)
+    waiting = [lambda h, scores: scores] * ahead
+    staged(HEADS, scores_of, *waiting, weigh, collect)
 
 
 VMEM = pl.BlockSpec(memory_space=pltpu.VMEM)
@@ -203,7 +203,7 @@
     keys = nn(normed, w_ref[1]).astype(BF)
     queries_t = nt(w_ref[0].T, normed).astype(BF)
     values_t = nt(w_ref[2].T, normed).astype(BF)
-    attend(keys, queries_t, values_t, ctx_ref)
+    attend(keys, queries_t, values_t, ctx_ref, 1)
     copies[5].wait()
     mid_ref[...] = (rows + tn(ctx_ref[...], w_ref[3])).astype(BF)
     keys_ref[...] = keys[HOP:]
@@ -224,7 +224,7 @@
         [queries_ref[...], nt(w_ref[0].T, normed).astype(BF)], axis=1
     )
     values_t = jnp.concatenate([values_ref[...], nt(w_ref[2].T, normed).astype(BF)], axis=1)
-    attend(keys, queries_t, values_t, ctx_ref)
+    attend(keys, queries_t, values_t, ctx_ref, 0)
     settle(copies)
     rows = jnp.concatenate([f_ref[...].astype(F32), rows], axis=0)
     mids = (mid_in_ref[...], (rows + tn(ctx_ref[...], w_ref[3])).astype(BF))
@@ -318,7 +318,10 @@
 
     def weigh(step, held):
         scores, grad_probs = held
-        probs = softmax_keys(scores)
+        return softmax_keys(scores), grad_probs
+
+    def weigh_rest(step, held):
+        probs, grad_probs = held
         inner = jnp.sum(grad_probs * probs, axis=0, keepdims=True)
         return probs.astype(BF), (probs * (grad_probs - inner) * SCALE).astype(BF)
 
@@ -340,7 +343,7 @@
             target[start : start + 32, at] = both[:32, :128].astype(BF)
             target[start + 32 : start + 64, at] = both[32:, 128:].astype(BF)
 
-    staged(16, products, weigh, collect)
+    staged(16, products, weigh, weigh_rest, collect)
     gqt, gk, gv = gq_t[...], gk_ref[...], gv_ref[...]
     grad_normed = nt(gqt.T, wq) + nt(gk, wk) + nt(gv, wv)
     result = (grads.astype(F32) + norm_pullback(grad_normed, unit, inverse, gain)).astype(BF)
@@ -504,17 +507,13 @@
 
 
 def intra_backward_kernel(
-    core_ref, m_ref, handed_any, wo_any,
+    core_ref, m_ref, wo_ref, handed_any,
     keep_ref, send_ref, grads_ref, gq_t, gk_ref, gv_ref,
-    handed_ref, stats_ref, wo_ref, sems,
+    handed_ref, stats_ref, sems,
 ):
     cuts = (KEYS, QUERIES, NORMED_T, HANDED_ROWS)
     spans = [pl.ds(start, end - start) for start, end in zip(cuts, cuts[1:])]
-    copies = begin(
-        sems,
-        (wo_any.at[0], wo_ref),
-        *[(handed_any.at[span], handed_ref.at[span]) for span in spans],
-    )
+    copies = begin(sems, *[(handed_any.at[span], handed_ref.at[span]) for span in spans])
     pick = select_rows(256, 256, owner_target)
     tiles = [nn(pick, m_ref[256 * t : 256 * t + 256, :]).astype(BF) for t in range(2)]
     masks = head_masks()
@@ -524,12 +523,10 @@
             [tiles[t][128 * g + 64 * h : 128 * g + 64 * h + 64] for h in range(2) for t in range(2)],
             axis=0,
         )
-        if g == 0:
-            copies[0].wait()
-        context.append(nt(grads_ref[g], wo_ref[...]).astype(BF))
+        context.append(nt(grads_ref[g], wo_ref[0]).astype(BF))
         context_t.append(context[g].T)
 
-    copies[1].wait()
+    copies[0].wait()
     stats_ref[...] = stats_of(handed_ref)
 
     def place(step):
@@ -555,7 +552,7 @@
 
     def collect(step, held):
         if step == 0:
-            copies[2].wait()
+            copies[1].wait()
         low, grad_scores = held
         g, at, b, i = place(step)
         block = slice(128 * b, 128 * b + 128)
@@ -571,7 +568,7 @@
             gk_ref[g, :, block] = sums["k"].astype(BF)
 
     staged(2 * HEADS, products, weigh, collect)
-    copies[3].wait()
+    copies[2].wait()
     parts = []
     for g in range(2):
         normed_t = features_of(
@@ -592,14 +589,14 @@
     split_by_core(core_ref, totals, keep_ref, send_ref)
 
 
-def intra_backward(core, grads, *rest):
-    return kernel_call(
-        intra_backward_kernel, "intra_backward", 4, [SMEM, VMEM] + [HBM] * 2, [VMEM] * 6,
+def intra_backward(core, grads, handed, wo):
+    return kernel_call(
+        intra_backward_kernel, "intra_backward", 4, [SMEM] + [VMEM] * 2 + [HBM], [VMEM] * 6,
         (
             f32(2, D, D), bf16(2, D, D), bf16(2, K, D), bf16(2, D, K), bf16(2, K, D), bf16(2, K, D),
         ),
-        [vbf(HANDED_ROWS, 128), pltpu.VMEM((4 * HEADS, K), F32), vbf(D, D), dma(4)],
-    )(core, grads, *pinned(*rest))
+        [vbf(HANDED_ROWS, 128), pltpu.VMEM((4 * HEADS, K), F32), dma(3)],
+    )(core, grads, wo, *pinned(handed))
 
 
 def intra_tail_kernel(

time: 118 us -> 118 us (level)
  transfers between devices with their start and end apart: 7 -> 7, of which waited for: 5 -> 5; matrix products, arithmetic and copies ran while one was open for 0% -> 0% of each run, Pallas kernels for 7% -> 6%
where the time goes in v8:
time: 118 us
  blocking collectives  50.8 us (43%)
  starting transfers between devices  27.7 us (23%)
  Pallas kernels  20.8 us (18%)
  waiting for transfers between devices  16.3 us (14%)
  local copies, waits for them, and re-layouts  1.18 us (1%)
    all_to_all x3, blocking collectives, exchanged(): return lax.all_to_all(shard, axes, split_axis=0, concat_axis=0, tiled=True)  50.8 us
    all_to_all x2, starting transfers between devices, exchanged(): return lax.all_to_all(shard, axes, split_axis=0, concat_axis=0, tiled=True)  12.2 us
    ppermute x3, starting transfers between devices, swapped(): return lax.ppermute(shard, 'core', [(0, 1), (1, 0)])  11.1 us
    all_to_all x2, waiting for transfers between devices, exchanged(): return lax.all_to_all(shard, axes, split_axis=0, concat_axis=0, tiled=True)  10.6 us
    pallas_call x1, Pallas kernels, intra_backward(): kernel_call(intra_backward_kernel, 'intra_backward', 4, [SMEM] + [VMEM] *...  4.57 us
    ppermute x2, starting transfers between devices, shifted(): return lax.ppermute(shard, TM, pairs)  4.43 us
    pallas_call x1, Pallas kernels, inter(): kernel_call(inter_kernel, 'inter', 5, [VMEM] * 6, [VMEM] * 7, (bf16(512,...  4.14 us
    ppermute x2, waiting for transfers between devices, shifted(): return lax.ppermute(shard, TM, pairs)  2.94 us
  transfers between devices with their start and end apart: 7, of which 5 were waited for; matrix products, arithmetic and copies ran while one was open for 0% of the time, Pallas kernels for 6%

profile of v8, /device:TPU:1, one launch (start us, length us, event | category | flops | bytes accessed | tf_op | source)
XLA Modules:
  0.0 117.6 jit_solution(11934149121600831568)
XLA Ops:
  0.6 1.3 %collective-permute-start = (bf16[256,256]{1,0:T(8,128)(2,1)}, bf16[256,256]{1,0:T(8,128)(2,1)S(1)}, u32[]{:S(2)}, u32[]{:S(2)}) collective-permute-start(bf16[256,256]{1,0:T(8,128)(2,1)} %bitcast.14), channel_id=1, source_target_pairs={{1,0},{2,1},{3,2},{4,3},{5,4},{6,5},{7,6},{8,7},{9,8},{10,9},{11,1... | collective-permute-start | bytes 393224 | tf_op jit(solution)/shard_map/ppermute | solution.py:675
  1.9 2.7 %intra_first.1 = (bf16[256,256]{1,0:T(8,128)(2,1)S(1)}, bf16[128,256]{1,0:T(8,128)(2,1)S(1)}, bf16[256,128]{1,0:T(8,128)(2,1)S(1)}, bf16[256,128]{1,0:T(8,128)(2...) custom-call(bf16[256,256]{1,0:T(8,128)(2,1)} %bitcast.15, f32[2,256]{1,0:T(2,128)} %gain_ref.5, ...), custom_call_target="tpu_custom_call" | custom-call | flops 1200000000 | bytes 1048576 | tf_op jit(solution)/shard_map/intra_first/pallas_call | solution.py:246
  4.6 2.9 %collective-permute-done.n_ref.n_any = bf16[256,256]{1,0:T(8,128)(2,1)S(1)} collective-permute-done((bf16[256,256]{1,0:T(8,128)(2,1)}, bf16[256,256]{1,0:T(8,128)(2,1)S(1)}, u32[]{:S(2)}, u32[]{:S(2)}) %collective-permute-start) | collective-permute-done | bytes 131104 | tf_op jit(solution)/shard_map/ppermute | solution.py:675
  7.6 0.0 copy-start
  7.6 0.0 copy-start.1
  7.6 0.0 copy-start.2
  7.6 0.0 copy-start.3
  7.6 0.0 copy-start.5
  7.6 2.0 %intra_second.1 = bf16[512,384]{1,0:T(8,128)(2,1)S(1)} custom-call(bf16[256,256]{1,0:T(8,128)(2,1)S(1)} %collective-permute-done.n_ref.n_any, bf16[256,256]{1,0:T(8,128)(2,1)S(1)} %get-tuple-element.40.mid_in_ref, bf16[128,256]{1,0:T(8,128)(2,1)S(1)} %get-tuple-element.41.keys_ref, bf16[256,128]{1,0:T(8,128)(2,1)S(1)} %get-tuple-element.42.queries_ref, ...), custom_call_target="tpu_custom_call" | custom-call | flops 1200000000 | bytes 1048576 | tf_op jit(solution)/shard_map/intra_second/pallas_call | solution.py:254
  9.6 27.8 %all_to_all.25 = bf16[64,8,384]{2,1,0:T(8,128)(2,1)S(1)} all-to-all(bf16[64,8,384]{2,1,0:T(8,128)(2,1)S(1)} %bitcast.12), channel_id=1, replica_groups=mesh['yh'=2,'core'=2,'yl'=2,'x'=4,'za'=4,'zb'=2] {'yl','x','za','zb'}, dimensions={0} | all-to-all | bytes 786432 | tf_op jit(solution)/shard_map/all_to_all | solution.py:679
  37.4 0.0 copy-done
  37.4 0.0 copy-done.1
  37.4 0.0 copy-done.2
  37.4 0.0 copy-done.3
  37.4 0.0 copy-done.5
  37.5 4.1 %inter.1 = (bf16[512,256]{1,0:T(8,128)(2,1)}, bf16[256,512]{1,0:T(8,128)(2,1)S(1)}, bf16[512,256]{1,0:T(8,128)(2,1)S(1)}, bf16[256,512]{1,0:T(8,128)(2,1)S(1)}, ...) custom-call(bf16[512,384]{1,0:T(8,128)(2,1)S(1)} %bitcast.11, ...), custom_call_target="tpu_custom_call" | custom-call | flops 2000000000 | bytes 1048576 | tf_op jit(solution)/shard_map/inter/pallas_call | solution.py:359
  41.6 0.0 copy-start.4
  41.6 6.2 %all-to-all-start.1 = ((bf16[64,8,256]{2,1,0:T(8,128)(2,1)}), bf16[64,8,256]{2,1,0:T(8,128)(2,1)S(1)}, u32[]{:S(2)}, u32[]{:S(2)}) async-start(bf16[64,8,256]{2,1,0:T(8,128)(2,1)} %bitcast.5), calls=%async_computation.1 | async-start | bytes 524288 | tf_op jit(solution)/shard_map/all_to_all | solution.py:679
  47.8 0.4 inter_weights.1
  48.3 2.7 %collective-permute-start.1 = (bf16[2,256,256]{2,1,0:T(8,128)(2,1)S(1)}, bf16[2,256,256]{2,1,0:T(8,128)(2,1)S(1)}, u32[]{:S(2)}, u32[]{:S(2)}) collective-permute-start(bf16[2,256,256]{2,1,0:T(8,128)(2,1)S(1)} %get-tuple-element.54), channel_id=1, source_target_pairs={{0,64},{64,0},{1,65},{65,1},{2,66},{66,2},{3,67},{67,3},{4,68},{68... | collective-permute-start | bytes 786440 | tf_op jit(solution)/shard_map/ppermute | solution.py:683
  50.9 0.0 copy-done.4
  50.9 2.7 %intra_prepare.1.handed_any = bf16[5824,128]{1,0:T(8,128)(2,1)S(1)} custom-call(bf16[256,256]{1,0:T(8,128)(2,1)S(1)} %bitcast.17, bf16[256,256]{1,0:T(8,128)(2,1)S(1)} %collective-permute-done.n_ref.n_any, f32[2,256]{1,0:T(2,128)S(1)} %copy-done.5, bf16[2,256,256]{2,1,0:T(8,128)(2,1)S(1)} %copy-done.1, bf16[2,256,256]{2,1,0:T(8,128)(2,1)S(1)} %copy-done.2, ...), custom_call_target="tpu_custom_call" | custom-call | flops 1200000000 | bytes 1048576 | tf_op jit(solution)/shard_map/intra_prepare/pallas_call | solution.py:503
  53.7 0.0 copy-start.6
  53.7 1.2 copy-done.6
  54.8 0.0 collective-permute-done.1.arrived_ref
  54.8 0.1 core_sum.1.inter_ref
  54.9 3.9 %all-to-all-done.1 = bf16[64,8,256]{2,1,0:T(8,128)(2,1)S(1)} async-done(((bf16[64,8,256]{2,1,0:T(8,128)(2,1)}), bf16[64,8,256]{2,1,0:T(8,128)(2,1)S(1)}, u32[]{:S(2)}, u32[]{:S(2)}) %all-to-all-start.1) | async-done | bytes 262176 | tf_op jit(solution)/shard_map/all_to_all | solution.py:679
  58.8 4.6 %intra_backward.1 = (f32[2,256,256]{2,1,0:T(8,128)S(1)}, bf16[2,256,256]{2,1,0:T(8,128)(2,1)S(1)}, bf16[2,256,256]{2,1,0:T(8,128)(2,1)S(1)}, bf16[2,256,256]{2,1...) custom-call(s32[1]{0:T(128)} %bitcast.core_ref, bf16[512,256]{1,0:T(8,128)(2,1)S(1)} %bitcast.13, ...), custom_call_target="tpu_custom_call" | custom-call | flops 1600000000 | bytes 1048576 | tf_op jit(solution)/shard_map/intra_backward/pallas_call | solution.py:593
  63.4 3.8 %collective-permute-start.2 = (bf16[2,256,256]{2,1,0:T(8,128)(2,1)S(1)}, bf16[2,256,256]{2,1,0:T(8,128)(2,1)S(1)}, u32[]{:S(2)}, u32[]{:S(2)}) collective-permute-start(bf16[2,256,256]{2,1,0:T(8,128)(2,1)S(1)} %get-tuple-element.57), channel_id=1, source_target_pairs={{0,64},{64,0},{1,65},{65,1},{2,66},{66,2},{3,67},{67,3},{4,68},{68... | collective-permute-start | bytes 786440 | tf_op jit(solution)/shard_map/ppermute | solution.py:683
  67.2 1.2 collective-permute-done.2.arrived_ref
  68.3 0.9 both_sums.1
  69.2 6.0 %all-to-all-start.2 = ((bf16[32,32,256]{2,1,0:T(8,128)(2,1)}), bf16[32,32,256]{2,1,0:T(8,128)(2,1)S(1)}, u32[]{:S(2)}, u32[]{:S(2)}) async-start(bf16[32,32,256]{2,1,0:T(8,128)(2,1)} %both_sums.1), calls=%async_computation.2 | async-start | bytes 1048576 | tf_op jit(solution)/shard_map/all_to_all | solution.py:679
  75.2 1.5 %intra_tail.1 = (bf16[128,256]{1,0:T(8,128)(2,1)S(1)}, bf16[128,256]{1,0:T(8,128)(2,1)S(1)}, bf16[128,256]{1,0:T(8,128)(2,1)S(1)}) custom-call(bf16[2,256,256]{2,1,0:T(8,128)(2,1)S(1)} %get-tuple-element.59.grads_any, bf16[2,256,256]{2,1,0:T(8,128)(2,1)S(1)} %get-tuple-element.60.gq_t_any, bf16[2,256,256]{2,1,0:T(8,128)(2,1)S(1)} %get-tuple-element.61.gk_any, ...), custom_call_target="tpu_custom_call" | custom-call | flops 800000000 | bytes 1048576 | tf_op jit(solution)/shard_map/intra_tail/pallas_call | solution.py:629
  76.7 3.1 %collective-permute-start.3 = (bf16[128,256]{1,0:T(8,128)(2,1)S(1)}, bf16[128,256]{1,0:T(8,128)(2,1)S(1)}, u32[]{:S(2)}, u32[]{:S(2)}) collective-permute-start(bf16[128,256]{1,0:T(8,128)(2,1)S(1)} %get-tuple-element.63), channel_id=1, source_target_pairs={{0,1},{1,2},{2,3},{3,4},{4,5},{5,6},{6,7},{7,8},{8,9},{9,10},{10,1... | collective-permute-start | bytes 196616 | tf_op jit(solution)/shard_map/ppermute | solution.py:675
  79.9 6.7 %all-to-all-done.2.pieces_ref = bf16[32,32,256]{2,1,0:T(8,128)(2,1)S(1)} async-done(((bf16[32,32,256]{2,1,0:T(8,128)(2,1)}), bf16[32,32,256]{2,1,0:T(8,128)(2,1)S(1)}, u32[]{:S(2)}, u32[]{:S(2)}) %all-to-all-start.2) | async-done | bytes 524320 | tf_op jit(solution)/shard_map/all_to_all | solution.py:679
  86.6 0.1 spread.2
  86.7 0.0 collective-permute-done.3.carried_ref
  86.7 9.3 %all_to_all.26.pieces_ref = bf16[4,32,256]{2,1,0:T(8,128)(2,1)S(1)} all-to-all(bf16[4,32,256]{2,1,0:T(8,128)(2,1)S(1)} %spread.2), channel_id=1, replica_groups=mesh['yh'=2,'core'=2,'yl'=2,'x'=4,'za'=4,'zb'=2] {'za'}, dimensions={0} | all-to-all | bytes 131072 | tf_op jit(solution)/shard_map/all_to_all | solution.py:679
  96.0 0.1 spread.3
  96.1 13.6 %all_to_all.27 = bf16[32,32,256]{2,1,0:T(8,128)(2,1)S(1)} all-to-all(bf16[32,32,256]{2,1,0:T(8,128)(2,1)S(1)} %spread.3), channel_id=1, replica_groups=mesh['yh'=2,'core'=2,'yl'=2,'x'=4,'za'=4,'zb'=2] {'yh','yl','x','zb'}, dimensions={0} | all-to-all | bytes 1048576 | tf_op jit(solution)/shard_map/all_to_all | solution.py:679
  109.7 4.6 %collective-permute-start.4 = (bf16[32,2,16,256]{3,2,1,0:T(8,128)(2,1)S(1)}, bf16[32,2,16,256]{3,2,1,0:T(8,128)(2,1)S(1)}, u32[]{:S(2)}, u32[]{:S(2)}) collective-permute-start(bf16[32,2,16,256]{3,2,1,0:T(8,128)(2,1)S(1)} %bitcast.9), channel_id=1, source_target_pairs={{0,64},{64,0},{1,65},{65,1},{2,66},{66,2},{3,67},{67,3},{4,68},{68... | collective-permute-start | bytes 1572872 | tf_op jit(solution)/shard_map/ppermute | solution.py:683
  114.3 1.5 %collective-permute-done.4.other_ref = bf16[32,2,16,256]{3,2,1,0:T(8,128)(2,1)S(1)} collective-permute-done((bf16[32,2,16,256]{3,2,1,0:T(8,128)(2,1)S(1)}, bf16[32,2,16,256]{3,2,1,0:T(8,128)(2,1)S(1)}, u32[]{:S(2)}, u32[]{:S(2)}) %collective-permute-start.4) | collective-permute-done | bytes 524320 | tf_op jit(solution)/shard_map/ppermute | solution.py:683
  115.9 1.7 %finish.1 = (bf16[256,256]{1,0:T(8,128)(2,1)}, f32[2,256,256]{2,1,0:T(8,128)}, f32[2,256,256]{2,1,0:T(8,128)}, f32[2,256,256]{2,1,0:T(8,128)}, f32[2,256,256]{2,1,0:T(8,128)}, /*index=5*/f32[2,256]{1,0:T(2,128)}) custom-call(s32[1]{0:T(128)} %bitcast.core_ref, bf16[32,2,16,256]{3,2,1,0:T(8,128)(2,1)S(1)} %bitcast.10, ...), custom_call_target="tpu_custom_call" | custom-call | flops 800000000 | bytes 1048576 | tf_op jit(solution)/shard_map/finish/pallas_call | solution.py:666
Async XLA Ops:
  0.6 6.9 %collective-permute-start = (bf16[256,256]{1,0:T(8,128)(2,1)}, bf16[256,256]{1,0:T(8,128)(2,1)S(1)}, u32[]{:S(2)}, u32[]{:S(2)}) collective-permute-start(bf16[256,256]{1,0:T(8,128)(2,1)} %bitcast.14), channel_id=1, source_target_pairs={{1,0},{2,1},{3,2},{4,3},{5,4},{6,5},{7,6},{8,7},{9,8},{10,9},{11,1... | collective-permute-start | bytes 393224 | tf_op jit(solution)/shard_map/ppermute | solution.py:675
  7.6 29.9 %copy-start = (bf16[2,256,256]{2,1,0:T(8,128)(2,1)S(1)}, bf16[2,256,256]{2,1,0:T(8,128)(2,1)}, u32[]{:S(2)}) copy-start(bf16[2,256,256]{2,1,0:T(8,128)(2,1)} %wo_ref.3) | copy-start | bytes 786436
  7.6 29.9 %copy-start.1 = (bf16[2,256,256]{2,1,0:T(8,128)(2,1)S(1)}, bf16[2,256,256]{2,1,0:T(8,128)(2,1)}, u32[]{:S(2)}) copy-start(bf16[2,256,256]{2,1,0:T(8,128)(2,1)} %wq_ref.5) | copy-start | bytes 786436
  7.6 29.9 %copy-start.2 = (bf16[2,256,256]{2,1,0:T(8,128)(2,1)S(1)}, bf16[2,256,256]{2,1,0:T(8,128)(2,1)}, u32[]{:S(2)}) copy-start(bf16[2,256,256]{2,1,0:T(8,128)(2,1)} %wk_ref.5) | copy-start | bytes 786436
  7.6 29.9 %copy-start.3 = (bf16[2,256,256]{2,1,0:T(8,128)(2,1)S(1)}, bf16[2,256,256]{2,1,0:T(8,128)(2,1)}, u32[]{:S(2)}) copy-start(bf16[2,256,256]{2,1,0:T(8,128)(2,1)} %wv_ref.5) | copy-start | bytes 786436
  7.6 29.9 %copy-start.5 = (f32[2,256]{1,0:T(2,128)S(1)}, f32[2,256]{1,0:T(2,128)}, u32[]{:S(2)}) copy-start(f32[2,256]{1,0:T(2,128)} %gain_ref.5) | copy-start | bytes 6148
  41.6 9.3 %copy-start.4 = (bf16[1,256,256]{2,1,0:T(8,128)(2,1)S(1)}, bf16[1,256,256]{2,1,0:T(8,128)(2,1)}, u32[]{:S(2)}) copy-start(bf16[1,256,256]{2,1,0:T(8,128)(2,1)} %param.7) | copy-start | bytes 393220
  41.6 17.2 %all-to-all-start.1 = ((bf16[64,8,256]{2,1,0:T(8,128)(2,1)}), bf16[64,8,256]{2,1,0:T(8,128)(2,1)S(1)}, u32[]{:S(2)}, u32[]{:S(2)}) async-start(bf16[64,8,256]{2,1,0:T(8,128)(2,1)} %bitcast.5), calls=%async_computation.1 | async-start | bytes 524288 | tf_op jit(solution)/shard_map/all_to_all | solution.py:679
  48.3 6.6 %collective-permute-start.1 = (bf16[2,256,256]{2,1,0:T(8,128)(2,1)S(1)}, bf16[2,256,256]{2,1,0:T(8,128)(2,1)S(1)}, u32[]{:S(2)}, u32[]{:S(2)}) collective-permute-start(bf16[2,256,256]{2,1,0:T(8,128)(2,1)S(1)} %get-tuple-element.54), channel_id=1, source_target_pairs={{0,64},{64,0},{1,65},{65,1},{2,66},{66,2},{3,67},{67,3},{4,68},{68... | collective-permute-start | bytes 786440 | tf_op jit(solution)/shard_map/ppermute | solution.py:683
  53.7 1.2 copy-start.6
  63.4 4.9 %collective-permute-start.2 = (bf16[2,256,256]{2,1,0:T(8,128)(2,1)S(1)}, bf16[2,256,256]{2,1,0:T(8,128)(2,1)S(1)}, u32[]{:S(2)}, u32[]{:S(2)}) collective-permute-start(bf16[2,256,256]{2,1,0:T(8,128)(2,1)S(1)} %get-tuple-element.57), channel_id=1, source_target_pairs={{0,64},{64,0},{1,65},{65,1},{2,66},{66,2},{3,67},{67,3},{4,68},{68... | collective-permute-start | bytes 786440 | tf_op jit(solution)/shard_map/ppermute | solution.py:683
  69.2 17.4 %all-to-all-start.2 = ((bf16[32,32,256]{2,1,0:T(8,128)(2,1)}), bf16[32,32,256]{2,1,0:T(8,128)(2,1)S(1)}, u32[]{:S(2)}, u32[]{:S(2)}) async-start(bf16[32,32,256]{2,1,0:T(8,128)(2,1)} %both_sums.1), calls=%async_computation.2 | async-start | bytes 1048576 | tf_op jit(solution)/shard_map/all_to_all | solution.py:679
  76.7 9.9 %collective-permute-start.3 = (bf16[128,256]{1,0:T(8,128)(2,1)S(1)}, bf16[128,256]{1,0:T(8,128)(2,1)S(1)}, u32[]{:S(2)}, u32[]{:S(2)}) collective-permute-start(bf16[128,256]{1,0:T(8,128)(2,1)S(1)} %get-tuple-element.63), channel_id=1, source_target_pairs={{0,1},{1,2},{2,3},{3,4},{4,5},{5,6},{6,7},{7,8},{8,9},{9,10},{10,1... | collective-permute-start | bytes 196616 | tf_op jit(solution)/shard_map/ppermute | solution.py:675
  109.7 6.2 %collective-permute-start.4 = (bf16[32,2,16,256]{3,2,1,0:T(8,128)(2,1)S(1)}, bf16[32,2,16,256]{3,2,1,0:T(8,128)(2,1)S(1)}, u32[]{:S(2)}, u32[]{:S(2)}) collective-permute-start(bf16[32,2,16,256]{3,2,1,0:T(8,128)(2,1)S(1)} %bitcast.9), channel_id=1, source_target_pairs={{0,64},{64,0},{1,65},{65,1},{2,66},{66,2},{3,67},{67,3},{4,68},{68... | collective-permute-start | bytes 1572872 | tf_op jit(solution)/shard_map/ppermute | solution.py:683

commit v9 on v8

--- a/solution.py
+++ b/solution.py
@@ -732,6 +732,7 @@
     keep, send, *rest = intra_backward(core, grad_local, handed, wo)
     half = both_sums(keep, send, inter_half)
     first, second, carry = intra_tail(*rest, frames, following, gains, wq, wk, wv)
+    half, carry = lax.optimization_barrier((half, carry))
     carried = shifted(carry, 1)
     sent = spread(exchanged(half, PLANE), 4)
     sent, carried = lax.optimization_barrier((sent, carried))

time: 118 us -> 118 us (level)
    all_to_all x2, waiting for transfers between devices: 10.6 us -> 12.5 us  [exchanged(): return lax.all_to_all(shard, axes, split_axis=0, concat_axis=0, tiled=True)]
  transfers between devices with their start and end apart: 7 -> 7, of which waited for: 5 -> 4; matrix products, arithmetic and copies ran while one was open for 0% -> 0% of each run, Pallas kernels for 6% -> 6%
where the time goes in v9:
time: 118 us; the launch traced here: 117 us
  blocking collectives  50.7 us (43%)
  starting transfers between devices  27 us (23%)
  Pallas kernels  20.8 us (18%)
  waiting for transfers between devices  17 us (14%)
  local copies, waits for them, and re-layouts  1.18 us (1%)
    all_to_all x3, blocking collectives, exchanged(): return lax.all_to_all(shard, axes, split_axis=0, concat_axis=0, tiled=True)  50.7 us
    all_to_all x2, waiting for transfers between devices, exchanged(): return lax.all_to_all(shard, axes, split_axis=0, concat_axis=0, tiled=True)  12.5 us
    all_to_all x2, starting transfers between devices, exchanged(): return lax.all_to_all(shard, axes, split_axis=0, concat_axis=0, tiled=True)  12.2 us
    ppermute x3, starting transfers between devices, swapped(): return lax.ppermute(shard, 'core', [(0, 1), (1, 0)])  10.3 us
    pallas_call x1, Pallas kernels, intra_backward(): kernel_call(intra_backward_kernel, 'intra_backward', 4, [SMEM] + [VMEM] *...  4.57 us
    ppermute x2, starting transfers between devices, shifted(): return lax.ppermute(shard, TM, pairs)  4.43 us
    pallas_call x1, Pallas kernels, inter(): kernel_call(inter_kernel, 'inter', 5, [VMEM] * 6, [VMEM] * 7, (bf16(512,...  4.14 us
    ppermute x2, waiting for transfers between devices, shifted(): return lax.ppermute(shard, TM, pairs)  2.94 us
  transfers between devices with their start and end apart: 7, of which 4 were waited for; matrix products, arithmetic and copies ran while one was open for 0% of the time, Pallas kernels for 6%

profile of v9, /device:TPU:1, one launch (start us, length us, event | category | flops | bytes accessed | tf_op | source)
XLA Modules:
  0.0 117.4 jit_solution(16027360970276669461)
XLA Ops:
  0.6 1.3 %collective-permute-start = (bf16[256,256]{1,0:T(8,128)(2,1)}, bf16[256,256]{1,0:T(8,128)(2,1)S(1)}, u32[]{:S(2)}, u32[]{:S(2)}) collective-permute-start(bf16[256,256]{1,0:T(8,128)(2,1)} %bitcast.14), channel_id=1, source_target_pairs={{1,0},{2,1},{3,2},{4,3},{5,4},{6,5},{7,6},{8,7},{9,8},{10,9},{11,1... | collective-permute-start | bytes 393224 | tf_op jit(solution)/shard_map/ppermute | solution.py:675
  1.9 2.7 %intra_first.1 = (bf16[256,256]{1,0:T(8,128)(2,1)S(1)}, bf16[128,256]{1,0:T(8,128)(2,1)S(1)}, bf16[256,128]{1,0:T(8,128)(2,1)S(1)}, bf16[256,128]{1,0:T(8,128)(2...) custom-call(bf16[256,256]{1,0:T(8,128)(2,1)} %bitcast.15, f32[2,256]{1,0:T(2,128)} %gain_ref.5, ...), custom_call_target="tpu_custom_call" | custom-call | flops 1200000000 | bytes 1048576 | tf_op jit(solution)/shard_map/intra_first/pallas_call | solution.py:246
  4.6 2.9 %collective-permute-done.n_ref.n_any = bf16[256,256]{1,0:T(8,128)(2,1)S(1)} collective-permute-done((bf16[256,256]{1,0:T(8,128)(2,1)}, bf16[256,256]{1,0:T(8,128)(2,1)S(1)}, u32[]{:S(2)}, u32[]{:S(2)}) %collective-permute-start) | collective-permute-done | bytes 131104 | tf_op jit(solution)/shard_map/ppermute | solution.py:675
  7.6 0.0 copy-start
  7.6 0.0 copy-start.1
  7.6 0.0 copy-start.2
  7.6 0.0 copy-start.3
  7.6 0.0 copy-start.5
  7.6 2.0 %intra_second.1 = bf16[512,384]{1,0:T(8,128)(2,1)S(1)} custom-call(bf16[256,256]{1,0:T(8,128)(2,1)S(1)} %collective-permute-done.n_ref.n_any, bf16[256,256]{1,0:T(8,128)(2,1)S(1)} %get-tuple-element.42.mid_in_ref, bf16[128,256]{1,0:T(8,128)(2,1)S(1)} %get-tuple-element.43.keys_ref, bf16[256,128]{1,0:T(8,128)(2,1)S(1)} %get-tuple-element.44.queries_ref, ...), custom_call_target="tpu_custom_call" | custom-call | flops 1200000000 | bytes 1048576 | tf_op jit(solution)/shard_map/intra_second/pallas_call | solution.py:254
  9.6 27.8 %all_to_all.25 = bf16[64,8,384]{2,1,0:T(8,128)(2,1)S(1)} all-to-all(bf16[64,8,384]{2,1,0:T(8,128)(2,1)S(1)} %bitcast.12), channel_id=1, replica_groups=mesh['yh'=2,'core'=2,'yl'=2,'x'=4,'za'=4,'zb'=2] {'yl','x','za','zb'}, dimensions={0} | all-to-all | bytes 786432 | tf_op jit(solution)/shard_map/all_to_all | solution.py:679
  37.4 0.0 copy-done
  37.4 0.0 copy-done.1
  37.4 0.0 copy-done.2
  37.4 0.0 copy-done.3
  37.4 0.0 copy-done.5
  37.5 4.1 %inter.1 = (bf16[512,256]{1,0:T(8,128)(2,1)}, bf16[256,512]{1,0:T(8,128)(2,1)S(1)}, bf16[512,256]{1,0:T(8,128)(2,1)S(1)}, bf16[256,512]{1,0:T(8,128)(2,1)S(1)}, ...) custom-call(bf16[512,384]{1,0:T(8,128)(2,1)S(1)} %bitcast.11, ...), custom_call_target="tpu_custom_call" | custom-call | flops 2000000000 | bytes 1048576 | tf_op jit(solution)/shard_map/inter/pallas_call | solution.py:359
  41.6 0.0 copy-start.4
  41.6 6.2 %all-to-all-start.1 = ((bf16[64,8,256]{2,1,0:T(8,128)(2,1)}), bf16[64,8,256]{2,1,0:T(8,128)(2,1)S(1)}, u32[]{:S(2)}, u32[]{:S(2)}) async-start(bf16[64,8,256]{2,1,0:T(8,128)(2,1)} %bitcast.5), calls=%async_computation.1 | async-start | bytes 524288 | tf_op jit(solution)/shard_map/all_to_all | solution.py:679
  47.8 0.4 inter_weights.1
  48.3 2.7 %collective-permute-start.1 = (bf16[2,256,256]{2,1,0:T(8,128)(2,1)S(1)}, bf16[2,256,256]{2,1,0:T(8,128)(2,1)S(1)}, u32[]{:S(2)}, u32[]{:S(2)}) collective-permute-start(bf16[2,256,256]{2,1,0:T(8,128)(2,1)S(1)} %get-tuple-element.56), channel_id=1, source_target_pairs={{0,64},{64,0},{1,65},{65,1},{2,66},{66,2},{3,67},{67,3},{4,68},{68... | collective-permute-start | bytes 786440 | tf_op jit(solution)/shard_map/ppermute | solution.py:683
  50.9 0.0 copy-done.4
  50.9 2.7 %intra_prepare.1.handed_any = bf16[5824,128]{1,0:T(8,128)(2,1)S(1)} custom-call(bf16[256,256]{1,0:T(8,128)(2,1)S(1)} %bitcast.17, bf16[256,256]{1,0:T(8,128)(2,1)S(1)} %collective-permute-done.n_ref.n_any, f32[2,256]{1,0:T(2,128)S(1)} %copy-done.5, bf16[2,256,256]{2,1,0:T(8,128)(2,1)S(1)} %copy-done.1, bf16[2,256,256]{2,1,0:T(8,128)(2,1)S(1)} %copy-done.2, ...), custom_call_target="tpu_custom_call" | custom-call | flops 1200000000 | bytes 1048576 | tf_op jit(solution)/shard_map/intra_prepare/pallas_call | solution.py:503
  53.7 0.0 copy-start.6
  53.7 1.2 copy-done.6
  54.8 0.0 collective-permute-done.1.arrived_ref
  54.8 0.1 core_sum.1.inter_ref
  54.9 3.9 %all-to-all-done.1 = bf16[64,8,256]{2,1,0:T(8,128)(2,1)S(1)} async-done(((bf16[64,8,256]{2,1,0:T(8,128)(2,1)}), bf16[64,8,256]{2,1,0:T(8,128)(2,1)S(1)}, u32[]{:S(2)}, u32[]{:S(2)}) %all-to-all-start.1) | async-done | bytes 262176 | tf_op jit(solution)/shard_map/all_to_all | solution.py:679
  58.8 4.6 %intra_backward.1 = (f32[2,256,256]{2,1,0:T(8,128)S(1)}, bf16[2,256,256]{2,1,0:T(8,128)(2,1)S(1)}, bf16[2,256,256]{2,1,0:T(8,128)(2,1)S(1)}, bf16[2,256,256]{2,1...) custom-call(s32[1]{0:T(128)} %bitcast.core_ref, bf16[512,256]{1,0:T(8,128)(2,1)S(1)} %bitcast.13, ...), custom_call_target="tpu_custom_call" | custom-call | flops 1600000000 | bytes 1048576 | tf_op jit(solution)/shard_map/intra_backward/pallas_call | solution.py:593
  63.4 3.8 %collective-permute-start.2 = (bf16[2,256,256]{2,1,0:T(8,128)(2,1)S(1)}, bf16[2,256,256]{2,1,0:T(8,128)(2,1)S(1)}, u32[]{:S(2)}, u32[]{:S(2)}) collective-permute-start(bf16[2,256,256]{2,1,0:T(8,128)(2,1)S(1)} %get-tuple-element.59), channel_id=1, source_target_pairs={{0,64},{64,0},{1,65},{65,1},{2,66},{66,2},{3,67},{67,3},{4,68},{68... | collective-permute-start | bytes 786440 | tf_op jit(solution)/shard_map/ppermute | solution.py:683
  67.2 1.5 %intra_tail.1 = (bf16[128,256]{1,0:T(8,128)(2,1)S(1)}, bf16[128,256]{1,0:T(8,128)(2,1)S(1)}, bf16[128,256]{1,0:T(8,128)(2,1)S(1)}) custom-call(bf16[2,256,256]{2,1,0:T(8,128)(2,1)S(1)} %get-tuple-element.61.grads_any, bf16[2,256,256]{2,1,0:T(8,128)(2,1)S(1)} %get-tuple-element.62.gq_t_any, bf16[2,256,256]{2,1,0:T(8,128)(2,1)S(1)} %get-tuple-element.63.gk_any, ...), custom_call_target="tpu_custom_call" | custom-call | flops 800000000 | bytes 1048576 | tf_op jit(solution)/shard_map/intra_tail/pallas_call | solution.py:629
  68.7 0.0 collective-permute-done.2.arrived_ref
  68.7 0.9 both_sums.1
  69.5 6.0 %all-to-all-start.2 = ((bf16[32,32,256]{2,1,0:T(8,128)(2,1)}), bf16[32,32,256]{2,1,0:T(8,128)(2,1)S(1)}, u32[]{:S(2)}, u32[]{:S(2)}) async-start(bf16[32,32,256]{2,1,0:T(8,128)(2,1)} %both_sums.1), calls=%async_computation.2 | async-start | bytes 1048576 | tf_op jit(solution)/shard_map/all_to_all | solution.py:679
  75.6 3.1 %collective-permute-start.3 = (bf16[128,256]{1,0:T(8,128)(2,1)S(1)}, bf16[128,256]{1,0:T(8,128)(2,1)S(1)}, u32[]{:S(2)}, u32[]{:S(2)}) collective-permute-start(bf16[128,256]{1,0:T(8,128)(2,1)S(1)} %get-tuple-element.67), channel_id=1, source_target_pairs={{0,1},{1,2},{2,3},{3,4},{4,5},{5,6},{6,7},{7,8},{8,9},{9,10},{10,1... | collective-permute-start | bytes 196616 | tf_op jit(solution)/shard_map/ppermute | solution.py:675
  78.7 8.6 %all-to-all-done.2.pieces_ref = bf16[32,32,256]{2,1,0:T(8,128)(2,1)S(1)} async-done(((bf16[32,32,256]{2,1,0:T(8,128)(2,1)}), bf16[32,32,256]{2,1,0:T(8,128)(2,1)S(1)}, u32[]{:S(2)}, u32[]{:S(2)}) %all-to-all-start.2) | async-done | bytes 524320 | tf_op jit(solution)/shard_map/all_to_all | solution.py:679
  87.3 0.1 spread.2
  87.4 0.0 collective-permute-done.3.carried_ref
  87.4 9.3 %all_to_all.26.pieces_ref = bf16[4,32,256]{2,1,0:T(8,128)(2,1)S(1)} all-to-all(bf16[4,32,256]{2,1,0:T(8,128)(2,1)S(1)} %spread.2), channel_id=1, replica_groups=mesh['yh'=2,'core'=2,'yl'=2,'x'=4,'za'=4,'zb'=2] {'za'}, dimensions={0} | all-to-all | bytes 131072 | tf_op jit(solution)/shard_map/all_to_all | solution.py:679
  96.6 0.1 spread.3
  96.7 13.6 %all_to_all.27 = bf16[32,32,256]{2,1,0:T(8,128)(2,1)S(1)} all-to-all(bf16[32,32,256]{2,1,0:T(8,128)(2,1)S(1)} %spread.3), channel_id=1, replica_groups=mesh['yh'=2,'core'=2,'yl'=2,'x'=4,'za'=4,'zb'=2] {'yh','yl','x','zb'}, dimensions={0} | all-to-all | bytes 1048576 | tf_op jit(solution)/shard_map/all_to_all | solution.py:679
  110.3 3.9 %collective-permute-start.4 = (bf16[32,2,16,256]{3,2,1,0:T(8,128)(2,1)S(1)}, bf16[32,2,16,256]{3,2,1,0:T(8,128)(2,1)S(1)}, u32[]{:S(2)}, u32[]{:S(2)}) collective-permute-start(bf16[32,2,16,256]{3,2,1,0:T(8,128)(2,1)S(1)} %bitcast.9), channel_id=1, source_target_pairs={{0,64},{64,0},{1,65},{65,1},{2,66},{66,2},{3,67},{67,3},{4,68},{68... | collective-permute-start | bytes 1572872 | tf_op jit(solution)/shard_map/ppermute | solution.py:683
  114.2 1.5 %collective-permute-done.4.other_ref = bf16[32,2,16,256]{3,2,1,0:T(8,128)(2,1)S(1)} collective-permute-done((bf16[32,2,16,256]{3,2,1,0:T(8,128)(2,1)S(1)}, bf16[32,2,16,256]{3,2,1,0:T(8,128)(2,1)S(1)}, u32[]{:S(2)}, u32[]{:S(2)}) %collective-permute-start.4) | collective-permute-done | bytes 524320 | tf_op jit(solution)/shard_map/ppermute | solution.py:683
  115.7 1.7 %finish.1 = (bf16[256,256]{1,0:T(8,128)(2,1)}, f32[2,256,256]{2,1,0:T(8,128)}, f32[2,256,256]{2,1,0:T(8,128)}, f32[2,256,256]{2,1,0:T(8,128)}, f32[2,256,256]{2,1,0:T(8,128)}, /*index=5*/f32[2,256]{1,0:T(2,128)}) custom-call(s32[1]{0:T(128)} %bitcast.core_ref, bf16[32,2,16,256]{3,2,1,0:T(8,128)(2,1)S(1)} %bitcast.10, ...), custom_call_target="tpu_custom_call" | custom-call | flops 800000000 | bytes 1048576 | tf_op jit(solution)/shard_map/finish/pallas_call | solution.py:666
Async XLA Ops:
  0.6 6.9 %collective-permute-start = (bf16[256,256]{1,0:T(8,128)(2,1)}, bf16[256,256]{1,0:T(8,128)(2,1)S(1)}, u32[]{:S(2)}, u32[]{:S(2)}) collective-permute-start(bf16[256,256]{1,0:T(8,128)(2,1)} %bitcast.14), channel_id=1, source_target_pairs={{1,0},{2,1},{3,2},{4,3},{5,4},{6,5},{7,6},{8,7},{9,8},{10,9},{11,1... | collective-permute-start | bytes 393224 | tf_op jit(solution)/shard_map/ppermute | solution.py:675
  7.6 29.9 %copy-start = (bf16[2,256,256]{2,1,0:T(8,128)(2,1)S(1)}, bf16[2,256,256]{2,1,0:T(8,128)(2,1)}, u32[]{:S(2)}) copy-start(bf16[2,256,256]{2,1,0:T(8,128)(2,1)} %wo_ref.3) | copy-start | bytes 786436
  7.6 29.9 %copy-start.1 = (bf16[2,256,256]{2,1,0:T(8,128)(2,1)S(1)}, bf16[2,256,256]{2,1,0:T(8,128)(2,1)}, u32[]{:S(2)}) copy-start(bf16[2,256,256]{2,1,0:T(8,128)(2,1)} %wq_ref.5) | copy-start | bytes 786436
  7.6 29.9 %copy-start.2 = (bf16[2,256,256]{2,1,0:T(8,128)(2,1)S(1)}, bf16[2,256,256]{2,1,0:T(8,128)(2,1)}, u32[]{:S(2)}) copy-start(bf16[2,256,256]{2,1,0:T(8,128)(2,1)} %wk_ref.5) | copy-start | bytes 786436
  7.6 29.9 %copy-start.3 = (bf16[2,256,256]{2,1,0:T(8,128)(2,1)S(1)}, bf16[2,256,256]{2,1,0:T(8,128)(2,1)}, u32[]{:S(2)}) copy-start(bf16[2,256,256]{2,1,0:T(8,128)(2,1)} %wv_ref.5) | copy-start | bytes 786436
  7.6 29.9 %copy-start.5 = (f32[2,256]{1,0:T(2,128)S(1)}, f32[2,256]{1,0:T(2,128)}, u32[]{:S(2)}) copy-start(f32[2,256]{1,0:T(2,128)} %gain_ref.5) | copy-start | bytes 6148
  41.6 9.3 %copy-start.4 = (bf16[1,256,256]{2,1,0:T(8,128)(2,1)S(1)}, bf16[1,256,256]{2,1,0:T(8,128)(2,1)}, u32[]{:S(2)}) copy-start(bf16[1,256,256]{2,1,0:T(8,128)(2,1)} %param.7) | copy-start | bytes 393220
  41.6 17.2 %all-to-all-start.1 = ((bf16[64,8,256]{2,1,0:T(8,128)(2,1)}), bf16[64,8,256]{2,1,0:T(8,128)(2,1)S(1)}, u32[]{:S(2)}, u32[]{:S(2)}) async-start(bf16[64,8,256]{2,1,0:T(8,128)(2,1)} %bitcast.5), calls=%async_computation.1 | async-start | bytes 524288 | tf_op jit(solution)/shard_map/all_to_all | solution.py:679
  48.3 6.6 %collective-permute-start.1 = (bf16[2,256,256]{2,1,0:T(8,128)(2,1)S(1)}, bf16[2,256,256]{2,1,0:T(8,128)(2,1)S(1)}, u32[]{:S(2)}, u32[]{:S(2)}) collective-permute-start(bf16[2,256,256]{2,1,0:T(8,128)(2,1)S(1)} %get-tuple-element.56), channel_id=1, source_target_pairs={{0,64},{64,0},{1,65},{65,1},{2,66},{66,2},{3,67},{67,3},{4,68},{68... | collective-permute-start | bytes 786440 | tf_op jit(solution)/shard_map/ppermute | solution.py:683
  53.7 1.2 copy-start.6
  63.4 5.3 %collective-permute-start.2 = (bf16[2,256,256]{2,1,0:T(8,128)(2,1)S(1)}, bf16[2,256,256]{2,1,0:T(8,128)(2,1)S(1)}, u32[]{:S(2)}, u32[]{:S(2)}) collective-permute-start(bf16[2,256,256]{2,1,0:T(8,128)(2,1)S(1)} %get-tuple-element.59), channel_id=1, source_target_pairs={{0,64},{64,0},{1,65},{65,1},{2,66},{66,2},{3,67},{67,3},{4,68},{68... | collective-permute-start | bytes 786440 | tf_op jit(solution)/shard_map/ppermute | solution.py:683
  69.5 17.7 %all-to-all-start.2 = ((bf16[32,32,256]{2,1,0:T(8,128)(2,1)}), bf16[32,32,256]{2,1,0:T(8,128)(2,1)S(1)}, u32[]{:S(2)}, u32[]{:S(2)}) async-start(bf16[32,32,256]{2,1,0:T(8,128)(2,1)} %both_sums.1), calls=%async_computation.2 | async-start | bytes 1048576 | tf_op jit(solution)/shard_map/all_to_all | solution.py:679
  75.6 11.8 %collective-permute-start.3 = (bf16[128,256]{1,0:T(8,128)(2,1)S(1)}, bf16[128,256]{1,0:T(8,128)(2,1)S(1)}, u32[]{:S(2)}, u32[]{:S(2)}) collective-permute-start(bf16[128,256]{1,0:T(8,128)(2,1)S(1)} %get-tuple-element.67), channel_id=1, source_target_pairs={{0,1},{1,2},{2,3},{3,4},{4,5},{5,6},{6,7},{7,8},{8,9},{9,10},{10,1... | collective-permute-start | bytes 196616 | tf_op jit(solution)/shard_map/ppermute | solution.py:675
  110.3 5.4 %collective-permute-start.4 = (bf16[32,2,16,256]{3,2,1,0:T(8,128)(2,1)S(1)}, bf16[32,2,16,256]{3,2,1,0:T(8,128)(2,1)S(1)}, u32[]{:S(2)}, u32[]{:S(2)}) collective-permute-start(bf16[32,2,16,256]{3,2,1,0:T(8,128)(2,1)S(1)} %bitcast.9), channel_id=1, source_target_pairs={{0,64},{64,0},{1,65},{65,1},{2,66},{66,2},{3,67},{67,3},{4,68},{68... | collective-permute-start | bytes 1572872 | tf_op jit(solution)/shard_map/ppermute | solution.py:683
